TPU v7x, 512 devices: a whole 4x4x16 slice. The times are simulated.
512 devices in a mesh: grp: 4 (over y), ctx: 32 (over x_lo, z), tp: 4 (over x_hi, core).
Axes of the slice: x: 4 (x_hi: 2, x_lo: 2; x = x_hi * 2 + x_lo), y: 4, z: 16, core: 2. Of those that a mesh axis runs over, the one named last changes fastest.
Arguments:
- state: float32 [4, 512, 5120], P(None, 'ctx', ('grp', 'tp')), may hold values from -6 to 6
- clean_tokens: bfloat16 [512, 5120], P('ctx', ('grp', 'tp')), may hold values from -6 to 6
- w_query: bfloat16 [5120, 4096], P('ctx', ('grp', 'tp')), may hold values from -0.078125 to 0.078125
- w_key: bfloat16 [5120, 4096], P('ctx', ('grp', 'tp')), may hold values from -0.078125 to 0.078125
- w_value: bfloat16 [5120, 4096], P('ctx', ('grp', 'tp')), may hold values from -0.078125 to 0.078125
- w_out: bfloat16 [4096, 5120], P(('grp', 'tp'), 'ctx'), may hold values from -0.09375 to 0.09375
- cache_keys: bfloat16 [16384, 4096], P('ctx', ('grp', 'tp')), may hold values from -200 to 200
- cache_values: bfloat16 [16384, 4096], P('ctx', ('grp', 'tp')), may hold values from -6 to 6
- norm_gain: float32 [5120], P(('grp', 'tp')), may hold values from 0.25 to 1.75
- mod_gain: float32 [5120], P(('grp', 'tp')), may hold values from -3 to 3
- out_gain: float32 [5120], P(('grp', 'tp')), may hold values from 0.1 to 1.9
- levels: float32 [50], replicated, may hold values from 0.05 to 1
- noise_index: int32 [4], replicated, may hold values from 0 to 47
- placement: int32 [64], P('ctx'), may hold values from 0 to 63, each once
- group_mask: int32 [4, 64], replicated, may hold values 0 or 1
Outputs:
- new_state: float32 [4, 512, 5120], P(None, 'ctx', ('grp', 'tp'))
- new_keys: bfloat16 [512, 4096], P('ctx', ('grp', 'tp'))
- new_values: bfloat16 [512, 4096], P('ctx', ('grp', 'tp'))
All inputs are finite; a program needn't handle non-finite values.
Results may differ from a plain program's by a relative error of at most 0.0062.
The roundings to bfloat16 on the way count: a program that leaves them out, or rounds other values in their place, can miss the bound.
Values may be sent and summed in bfloat16 or wider, within the bound.
No kernel may reach another device: no remote copies, remote signals or barrier semaphores. Data moves between devices by JAX's collectives and lax.ppermute only.
A program may use at most 64 MiB of HBM per device.

v0:
```python
import math

import jax
import jax.numpy as jnp
from jax import lax
from jax.sharding import Mesh
from jax.sharding import PartitionSpec as P

D = 5120
HD = 128
SLOT = 256
CTX = ("ctx_0", "ctx_1")


epsilon = 1e-06


def sent_to_all(array, axis):
    devices = lax.axis_size(axis)
    return lax.all_to_all(
        jnp.broadcast_to(array[None], (devices, *array.shape)), axis, 0, 0, tiled=True
    )


def taken_together(array, axis):
    return sent_to_all(array, axis).sum(axis=0)


def joined_along(tiles, dim):
    tiles = jnp.moveaxis(tiles, 0, dim)
    lengths = tiles.shape
    return tiles.reshape(*lengths[:dim], lengths[dim] * lengths[dim + 1], *lengths[dim + 2 :])


def gathered_copies(array, axis, dim):
    tiles = sent_to_all(array, axis)
    return joined_along(tiles, dim)


def turned_gather(arrays, axis, dims):
    turned = [jnp.moveaxis(a, dim, 0) for a, dim in zip(arrays, dims)]
    both = jnp.concatenate([t.reshape(len(t), -1) for t in turned], axis=1)
    whole, at, gathered = (lax.all_gather(both, axis, axis=0, tiled=True), 0, [])
    for t, dim in zip(turned, dims):
        share = whole[:, at : at + t[0].size].reshape(-1, *t.shape[1:])
        gathered.append(jnp.moveaxis(share, 0, dim))
        at += t[0].size
    return tuple(gathered)


def stacked_from(array, axes, sequence):
    tiles = array[None]
    for k in sequence:
        tiles = lax.all_gather(tiles, axes[k], axis=0, tiled=True)
    block = [lax.axis_size(axes[k]) for k in reversed(sequence)]
    tiles = tiles.reshape(*block, *array.shape)
    turned = sorted(range(len(sequence)), key=lambda place: sequence[len(sequence) - 1 - place])
    return tiles.transpose(*turned, *range(len(sequence), tiles.ndim)).reshape(-1, *array.shape)


def gather_axes(array, axes, sequence, dim):
    return joined_along(stacked_from(array, axes, sequence), dim)


def over_copies(array, axis):
    everything = sent_to_all(array, axis)
    return jnp.max(everything, axis=0)


def reduced_to_own(tiles, axes, sequence):
    inside = tiles.shape[1:]
    tiles = tiles.reshape(*(lax.axis_size(a) for a in axes), *inside)
    tiles = jnp.moveaxis(tiles, sequence, range(len(axes))).reshape(-1, *inside)
    for k in sequence:
        tiles = lax.psum_scatter(tiles, axes[k], scatter_dimension=0, tiled=True)
    return tiles[0]


def split_up(array, dim, devices):
    before, after = (array.shape[:dim], array.shape[dim + 1 :])
    return jnp.moveaxis(array.reshape(*before, devices, -1, *after), dim, 0)


def scatter_axes(array, axes, sequence, dim):
    devices = lax.axis_size(axes)
    return reduced_to_own(split_up(array, dim, devices), axes, sequence)


def sent_and_summed(array, axis, dim):
    devices = lax.axis_size(axis)
    tiles = lax.all_to_all(split_up(array, dim, devices), axis, 0, 0, tiled=True)
    return jnp.sum(tiles, axis=0)


def level_lookup(levels, indices):
    table = jnp.arange(levels.shape[0], dtype=jnp.int32)
    picked = (indices[:, None] == table[None, :]).astype(jnp.float32)
    return jnp.sum(picked * levels[None, :], axis=1)


def normalize_rows(rows, sigma_rows, norm_gain, mod_gain):
    squares = taken_together(jnp.sum(rows * rows, axis=1), ("grp", "tp"))
    inverse = lax.rsqrt(squares / D + epsilon)
    scaled = (
        rows
        * inverse[:, None]
        * norm_gain[None, :]
        * (1.0 + sigma_rows[:, None] * mod_gain[None, :])
    )
    return gathered_copies(scaled.astype(jnp.bfloat16), ("grp", "tp"), 1)


def local(
    state,
    clean_tokens,
    w_query,
    w_key,
    w_value,
    w_out,
    cache_keys,
    cache_values,
    norm_gain,
    mod_gain,
    out_gain,
    levels,
    noise_index,
    placement,
    group_mask,
):
    flight, ch_dev, local_width = state.shape
    ctx_count = lax.axis_size(CTX)
    group = ch_dev * ctx_count
    cache_dev = cache_keys.shape[0]
    slots_dev = cache_dev // SLOT
    heads_dev = cache_keys.shape[1] // HD
    rows_count = flight * ch_dev
    scale = 1.0 / math.sqrt(HD)
    wq_full, wk_full, wv_full, wo_full = turned_gather(
        (w_query, w_key, w_value, w_out), CTX, (0, 0, 0, 1)
    )
    group_table = jnp.arange(group_mask.shape[1], dtype=jnp.int32)
    slot_onehot = (placement[:, None] == group_table[None, :]).astype(jnp.int32)
    slot_seen = jnp.sum(slot_onehot[None, :, :] * group_mask[:, None, :], axis=2) > 0
    cache_seen = slot_seen[:, None, None, :, None]
    own_group = jnp.arange(flight, dtype=jnp.int32)
    flight_seen = (own_group[None, :] <= own_group[:, None])[:, None, None, :, None]
    cache_k = cache_keys.reshape(slots_dev, SLOT, heads_dev, HD)
    cache_v = cache_values.reshape(slots_dev, SLOT, heads_dev, HD)
    finished_keys = None
    finished_values = None
    current = level_lookup(levels, noise_index + 0)
    following = level_lookup(levels, noise_index + 0 + 1)
    rows = state.reshape(rows_count, local_width)
    sigma_rows = jnp.repeat(current, ch_dev)
    rows = jnp.concatenate([rows, clean_tokens.astype(jnp.float32)], axis=0)
    sigma_rows = jnp.concatenate([sigma_rows, jnp.zeros((ch_dev,), jnp.float32)])
    features = normalize_rows(rows, sigma_rows, norm_gain, mod_gain)
    keys_new = jnp.dot(features, wk_full, preferred_element_type=jnp.float32).astype(jnp.bfloat16)
    values_new = jnp.dot(features, wv_full, preferred_element_type=jnp.float32).astype(jnp.bfloat16)
    finished_keys = keys_new[rows_count:]
    finished_values = values_new[rows_count:]
    keys_new = keys_new[:rows_count]
    values_new = values_new[:rows_count]
    noisy = features[:rows_count]
    local_q = jnp.dot(noisy, wq_full, preferred_element_type=jnp.float32).astype(jnp.bfloat16)
    queries = gather_axes(local_q.reshape(flight, ch_dev, -1), CTX, (0, 1), 1)
    query_heads = queries.reshape(flight, group, heads_dev, HD)
    finished_k = finished_keys.reshape(ch_dev, heads_dev, HD)
    finished_v = finished_values.reshape(ch_dev, heads_dev, HD)
    flight_k = keys_new.reshape(flight, ch_dev, heads_dev, HD)
    flight_v = values_new.reshape(flight, ch_dev, heads_dev, HD)
    cache_scores = (
        jnp.einsum("fqhd,sthd->fqhst", query_heads, cache_k, preferred_element_type=jnp.float32)
        * scale
    )
    finished_scores = (
        jnp.einsum("fqhd,thd->fqht", query_heads, finished_k, preferred_element_type=jnp.float32)
        * scale
    )
    flight_scores = (
        jnp.einsum("fqhd,gthd->fqhgt", query_heads, flight_k, preferred_element_type=jnp.float32)
        * scale
    )
    peak = jnp.max(finished_scores, axis=3)
    peak = jnp.maximum(peak, jnp.max(jnp.where(cache_seen, cache_scores, -jnp.inf), axis=(3, 4)))
    peak = jnp.maximum(peak, jnp.max(jnp.where(flight_seen, flight_scores, -jnp.inf), axis=(3, 4)))
    peak = over_copies(peak, CTX)
    cache_p = jnp.where(cache_seen, jnp.exp(cache_scores - peak[..., None, None]), 0.0).astype(
        jnp.bfloat16
    )
    finished_p = jnp.exp(finished_scores - peak[..., None]).astype(jnp.bfloat16)
    flight_p = jnp.where(flight_seen, jnp.exp(flight_scores - peak[..., None, None]), 0.0).astype(
        jnp.bfloat16
    )
    numer = jnp.einsum("fqhst,sthd->fqhd", cache_p, cache_v, preferred_element_type=jnp.float32)
    numer = numer + jnp.einsum(
        "fqht,thd->fqhd", finished_p, finished_v, preferred_element_type=jnp.float32
    )
    numer = numer + jnp.einsum(
        "fqhgt,gthd->fqhd", flight_p, flight_v, preferred_element_type=jnp.float32
    )
    denom = jnp.sum(cache_p, axis=(3, 4), dtype=jnp.float32)
    denom = denom + jnp.sum(finished_p, axis=3, dtype=jnp.float32)
    denom = denom + jnp.sum(flight_p, axis=(3, 4), dtype=jnp.float32)
    numer, denom = (
        scatter_axes(numer.reshape(flight, group, heads_dev * HD), CTX, (1, 0), 1),
        scatter_axes(denom, CTX, (1, 0), 1),
    )
    attention = numer.reshape(flight, ch_dev, heads_dev, HD) / denom[..., None]
    attention = attention.astype(jnp.bfloat16).reshape(rows_count, heads_dev * HD)
    partial_y = jnp.dot(attention, wo_full, preferred_element_type=jnp.float32)
    y_rows = sent_and_summed(partial_y, ("grp", "tp"), 1)
    y_squares = taken_together(jnp.sum(y_rows * y_rows, axis=1), ("grp", "tp"))
    velocity = y_rows * lax.rsqrt(y_squares / D + epsilon)[:, None] * out_gain[None, :]
    state = state + (following - current)[:, None, None] * velocity.reshape(
        flight, ch_dev, local_width
    )
    return (state, finished_keys, finished_values)


def solution(mesh):
    finer = Mesh(
        mesh.devices.reshape(mesh.shape["grp"], 2, 16, mesh.shape["tp"]),
        ("grp", "ctx_0", "ctx_1", "tp"),
    )
    in_specs = (
        P(None, CTX, ("grp", "tp")),
        P(CTX, ("grp", "tp")),
        P(CTX, ("grp", "tp")),
        P(CTX, ("grp", "tp")),
        P(CTX, ("grp", "tp")),
        P(("grp", "tp"), CTX),
        P(CTX, ("grp", "tp")),
        P(CTX, ("grp", "tp")),
        P(("grp", "tp")),
        P(("grp", "tp")),
        P(("grp", "tp")),
        P(),
        P(),
        P(CTX),
        P(),
    )
    out_specs = (P(None, CTX, ("grp", "tp")), P(CTX, ("grp", "tp")), P(CTX, ("grp", "tp")))
    return jax.shard_map(local, mesh=finer, in_specs=in_specs, out_specs=out_specs, check_vma=False)
```

profile of v0, /device:TPU:1, one launch (start us, length us, event | category | flops | bytes accessed | tf_op | source)
XLA Modules:
  0.0 471.8 jit_solution(4263949515945108787)
XLA Ops:
  7.2 1.8 pad_maximum_fusion
  11.4 10.1 %all-to-all-start = ((f32[16,1,80]{2,1,0:T(1,128)}), f32[16,1,80]{2,1,0:T(1,128)S(1)}, u32[]{:S(2)}, u32[]{:S(2)}) async-start(f32[16,1,80]{2,1,0:T(1,128)} %broadcast_in_dim.49), calls=%async_computation | async-start | bytes 16384 | tf_op jit(solution)/shard_map/all_to_all | solution.py:20
  23.2 5.2 %all-to-all-done = f32[16,1,80]{2,1,0:T(1,128)S(1)} async-done(((f32[16,1,80]{2,1,0:T(1,128)}), f32[16,1,80]{2,1,0:T(1,128)S(1)}, u32[]{:S(2)}, u32[]{:S(2)}) %all-to-all-start) | async-done | bytes 5152 | tf_op jit(solution)/shard_map/all_to_all | solution.py:20
  29.6 89.2 %all_to_all.27 = bf16[16,80,320]{2,1,0:T(8,128)(2,1)S(1)} all-to-all(bf16[16,80,320]{2,1,0:T(8,128)(2,1)S(1)} %broadcast_in_dim.51), channel_id=1, replica_groups=mesh['grp'=4,'ctx_0'=2,'ctx_1'=16,'tp'=4] {'grp','tp'}, dimensions={0} | all-to-all | bytes 1638400 | tf_op jit(solution)/shard_map/all_to_all | solution.py:20
  120.0 32.2 %all-gather.3.cloned.1.call-done = bf16[5120,1024]{1,0:T(8,128)(2,1)} async-done(((bf16[160,1024]{1,0:T(8,128)(2,1)}), bf16[5120,1024]{1,0:T(8,128)(2,1)}) %all-gather.3.cloned.1.call-update) | async-done | bytes 10485776 | tf_op jit(solution)/shard_map/all_gather | solution.py:43
  152.2 2.3 fusion.18
  154.5 3.6 all_gather.10
  159.6 2.3 fusion.12
  162.0 67.4 %all-gather.5.cloned.1.call-done = bf16[32,4,16,256]{3,2,1,0:T(8,128)(2,1)} async-done(((bf16[2,4,16,256]{3,2,1,0:T(8,128)(2,1)}), bf16[32,4,16,256]{3,2,1,0:T(8,128)(2,1)}) %all-gather.5.cloned.1.call-update) | async-done | bytes 1048592 | tf_op jit(solution)/shard_map/all_gather | solution.py:54
  232.0 4.6 fusion
  237.5 8.0 %all-to-all-start.2 = ((f32[32,4,512,2]{2,1,3,0:T(4,128)}), f32[32,4,512,2]{2,1,3,0:T(4,128)S(1)}, u32[]{:S(2)}, u32[]{:S(2)}) async-start(f32[32,4,512,2]{2,1,3,0:T(4,128)} %broadcast_in_dim.55), calls=%async_computation.2 | async-start | bytes 1048576 | tf_op jit(solution)/shard_map/all_to_all | solution.py:20
  246.8 2.3 fusion.15
  249.2 17.5 %all-to-all-done.2 = f32[32,4,512,2]{2,1,3,0:T(4,128)S(1)} async-done(((f32[32,4,512,2]{2,1,3,0:T(4,128)}), f32[32,4,512,2]{2,1,3,0:T(4,128)S(1)}, u32[]{:S(2)}, u32[]{:S(2)}) %all-to-all-start.2) | async-done | bytes 524320 | tf_op jit(solution)/shard_map/all_to_all | solution.py:20
  267.1 5.9 %fusion.27 = f32[2,4,512,128,1]{3,2,4,1,0:T(8,128)S(1)} fusion(bf16[2,256,2,128,1]{3,2,1,0,4:T(2,128)(2,1)S(1)} %bitcast.107, f32[2,4,512,2,256]{2,4,3,1,0:T(8,128)} %get-tuple-element.12, f32[4,512,2]{1,0,2:T(4,128)S(1)} %reduce_max.39, pred[4,2]{1,0:T(4,128)(4,1)S(1)} %copy.119), kind=kOutput, calls=%fused_computation.33 | convolution fusion | flops 545259520 | bytes 10764296 | tf_op jit(solution)/shard_map/fqhst,sthd->fqhd/dot_general | solution.py:195
  274.1 1.6 copy.138
  275.7 2.7 reshape_reshape.7
  278.5 3.1 copy.140
  285.0 5.2 %convert_reduce_fusion = f32[4,512,2]{1,0,2:T(4,128)S(1)} fusion(f32[4,512,2]{1,0,2:T(4,128)S(1)} %reduce_max.39, f32[2,4,512,2,256]{2,4,3,1,0:T(8,128)} %get-tuple-element.12, pred[4,2]{1,0:T(4,128)(4,1)S(1)} %copy.119), kind=kLoop, calls=%fused_computation.6 | loop fusion | flops 12578816 | bytes 8421384 | tf_op jit(solution)/shard_map/reduce_sum | solution.py:202
  290.2 58.9 %reduce-scatter.3.cloned.1.call-done = f32[2,4,16,256]{3,2,1,0:T(8,128)} async-done(((f32[32,4,16,256]{3,2,1,0:T(8,128)}), f32[2,4,16,256]{3,2,1,0:T(8,128)}) %reduce-scatter.3.cloned.1.call-update) | async-done | bytes 131088 | tf_op jit(solution)/shard_map/reduce_scatter | solution.py:75
  349.4 42.0 %all-reduce.1 = f32[32,4,16,2]{2,1,3,0:T(4,128)S(1)} all-reduce(f32[32,4,16,2]{2,1,3,0:T(4,128)S(1)} %copy.144), channel_id=4, replica_groups=mesh['grp'=4,'ctx_0'=2,'ctx_1'=16,'tp'=4] {'ctx_1'}, use_global_device_ids=true, to_apply=%region_14.15.clone | all-reduce | flops 4096 | bytes 32768
  391.4 4.0 all-reduce.2
  398.2 54.0 %all_to_all.28 = f32[16,64,320]{2,1,0:T(8,128)S(1)} all-to-all(f32[16,64,320]{2,1,0:T(8,128)S(1)} %convolution_bitcast_fusion), channel_id=1, replica_groups=mesh['grp'=4,'ctx_0'=2,'ctx_1'=16,'tp'=4] {'grp','tp'}, dimensions={0} | all-to-all | bytes 2621440 | tf_op jit(solution)/shard_map/all_to_all | solution.py:91
  453.0 4.4 all-to-all-start.4
  457.5 7.0 %all-to-all-done.4 = f32[16,1,64]{2,1,0:T(1,128)S(1)} async-done(((f32[16,1,64]{2,1,0:T(1,128)}), f32[16,1,64]{2,1,0:T(1,128)S(1)}, u32[]{:S(2)}, u32[]{:S(2)}) %all-to-all-start.4) | async-done | bytes 4128 | tf_op jit(solution)/shard_map/all_to_all | solution.py:20
  (91 shorter events, 21.6 us)
Async XLA Ops:
  7.2 145.0 %all-gather.3.cloned.1.call-start = ((), (), s32[]{:S(2)}) async-start(), calls=%async_computation.7 | async-start | bytes 10813440 | tf_op jit(solution)/shard_map/all_gather | solution.py:43
  11.4 17.1 %all-to-all-start = ((f32[16,1,80]{2,1,0:T(1,128)}), f32[16,1,80]{2,1,0:T(1,128)S(1)}, u32[]{:S(2)}, u32[]{:S(2)}) async-start(f32[16,1,80]{2,1,0:T(1,128)} %broadcast_in_dim.49), calls=%async_computation | async-start | bytes 16384 | tf_op jit(solution)/shard_map/all_to_all | solution.py:20
  21.5 207.9 %all-gather.5.cloned.1.call-start = ((), (), s32[]{:S(2)}) async-start(), calls=%async_computation.8 | async-start | bytes 1114112 | tf_op jit(solution)/shard_map/all_gather | solution.py:54
  118.8 39.4 %copy-start.6 = (s32[2]{0:T(128)S(1)}, s32[2]{0:T(128)}, u32[]{:S(2)}) copy-start(s32[2]{0:T(128)} %param.28) | copy-start | bytes 28
  118.8 39.4 %copy-start.5 = (s32[4,64]{1,0:T(4,128)S(1)}, s32[4,64]{1,0:T(4,128)}, u32[]{:S(2)}) copy-start(s32[4,64]{1,0:T(4,128)} %param.29) | copy-start | bytes 3076
  118.8 39.7 %copy-start.1 = (bf16[512,256]{1,0:T(8,128)(2,1)S(1)}, bf16[512,256]{1,0:T(8,128)(2,1)}, u32[]{:S(2)}) copy-start(bf16[512,256]{1,0:T(8,128)(2,1)} %param.21) | copy-start | bytes 786436
  161.9 70.1 %copy-start.2 = (bf16[16,256]{1,0:T(8,128)(2,1)}, bf16[16,256]{1,0:T(8,128)(2,1)S(1)}, u32[]{:S(2)}) copy-start(bf16[16,256]{1,0:T(8,128)(2,1)S(1)} %slice.43) | copy-start | bytes 24580
  237.5 29.2 %all-to-all-start.2 = ((f32[32,4,512,2]{2,1,3,0:T(4,128)}), f32[32,4,512,2]{2,1,3,0:T(4,128)S(1)}, u32[]{:S(2)}, u32[]{:S(2)}) async-start(f32[32,4,512,2]{2,1,3,0:T(4,128)} %broadcast_in_dim.55), calls=%async_computation.2 | async-start | bytes 1048576 | tf_op jit(solution)/shard_map/all_to_all | solution.py:20
  245.5 103.5 %reduce-scatter.3.cloned.1.call-start = ((), (), s32[]{:S(2)}) async-start(), calls=%async_computation.9 | async-start | bytes 2228224 | tf_op jit(solution)/shard_map/reduce_scatter | solution.py:75
  249.1 23.8 %copy-start.3 = (bf16[16,256]{1,0:T(8,128)(2,1)}, bf16[16,256]{1,0:T(8,128)(2,1)S(1)}, u32[]{:S(2)}) copy-start(bf16[16,256]{1,0:T(8,128)(2,1)S(1)} %slice.46) | copy-start | bytes 24580
  281.6 114.8 %reduce-scatter.5.cloned.1.call-start = ((), (), s32[]{:S(2)}) async-start(), calls=%async_computation.10 | async-start | bytes 196608 | tf_op jit(solution)/shard_map/reduce_scatter | solution.py:75
  284.9 112.3 %slice-start = ((bf16[5120,1024]{1,0:T(8,128)(2,1)}), bf16[5120,256]{1,0:T(8,128)(2,1)S(1)}, s32[]{:S(2)}) async-start(bf16[5120,1024]{1,0:T(8,128)(2,1)} %all-gather.3.cloned.1.call-done), calls=%async_computation.11 | async-start | bytes 5242880 | tf_op jit(solution)/shard_map/slice | solution.py:45
  397.3 67.3 %copy-start = (f32[4,16,320]{2,1,0:T(8,128)S(1)}, f32[4,16,320]{2,1,0:T(8,128)}, u32[]{:S(2)}) copy-start(f32[4,16,320]{2,1,0:T(8,128)} %param.15) | copy-start | bytes 245764
  397.3 67.3 %copy-start.4 = (f32[320]{0:T(512)S(1)}, f32[320]{0:T(512)}, u32[]{:S(2)}) copy-start(f32[320]{0:T(512)} %param.25) | copy-start | bytes 3844
  453.0 11.4 %all-to-all-start.4 = ((f32[16,1,64]{2,1,0:T(1,128)}), f32[16,1,64]{2,1,0:T(1,128)S(1)}, u32[]{:S(2)}, u32[]{:S(2)}) async-start(f32[16,1,64]{2,1,0:T(1,128)} %broadcast_in_dim.99), calls=%async_computation.6 | async-start | bytes 16384 | tf_op jit(solution)/shard_map/all_to_all | solution.py:20
Sparse Core Ops, SparseCore 0:
  10.1 142.0 all-gather.2
  158.3 71.0 all-gather.4
  281.7 67.2 reduce-scatter.2
  351.6 28.6 reduce-scatter.4
where the time goes:
time: 473 us; the launch traced here: 472 us
  blocking collectives  193 us (41%)
  waiting for transfers between devices  188 us (40%)
  starting transfers between devices  22.9 us (5%)
  matrix products  20.4 us (4%)
  local copies, waits for them, and re-layouts  18.8 us (4%)
  between operations  14.8 us (3%)
  other arithmetic  13.8 us (3%)
    all_to_all x1, blocking collectives, sent_to_all(): lax.all_to_all(jnp.broadcast_to(array[None], (devices, *array.shape)), ax...  89.2 us
    all_gather x1, waiting for transfers between devices, stacked_from(): tiles = lax.all_gather(tiles, axes[k], axis=0, tiled=True)  67.4 us
    reduce_scatter x2, waiting for transfers between devices, reduced_to_own(): tiles = lax.psum_scatter(tiles, axes[k], scatter_dimension=0, tiled=True)  58.9 us
    all_to_all x1, blocking collectives, sent_and_summed(): lax.all_to_all(split_up(array, dim, devices), axis, 0, 0, tiled=True)  54 us
    unnamed x2, blocking collectives  46 us
    all_gather x1, waiting for transfers between devices, turned_gather(): lax.all_gather(both, axis, axis=0, tiled=True)  32.2 us
    all_to_all x3, waiting for transfers between devices, sent_to_all(): lax.all_to_all(jnp.broadcast_to(array[None], (devices, *array.shape)), ax...  29.7 us
    all_to_all x3, starting transfers between devices, sent_to_all(): lax.all_to_all(jnp.broadcast_to(array[None], (devices, *array.shape)), ax...  22.6 us
  transfers between devices with their start and end apart: 7, of which 6 were waited for; matrix products, arithmetic and copies ran while one was open for 5% of the time, Pallas kernels for 0%

commit v1 on v0

v1 whole, which is shorter than its diff:
```python
import functools
import math

import jax
import jax.numpy as jnp
from jax import lax
from jax.experimental import pallas as pl
from jax.experimental.pallas import tpu as pltpu
from jax.sharding import Mesh
from jax.sharding import PartitionSpec as P

D = 5120
HD = 128
SLOT = 256
EPSILON = 1e-06
VMEM_LIMIT = 48 * 1024 * 1024

CTX = ("xl", "z")
WIDE = ("y", "xh", "core")
BF16 = jnp.bfloat16
F32 = jnp.float32


def level_lookup(levels, indices):
    table = jnp.arange(levels.shape[0], dtype=jnp.int32)
    picked = (indices[:, None] == table[None, :]).astype(F32)
    return jnp.sum(picked * levels[None, :], axis=1)


def sent_to_all(array, axis):
    devices = lax.axis_size(axis)
    return lax.all_to_all(
        jnp.broadcast_to(array[None], (devices, *array.shape)), axis, 0, 0, tiled=True
    )


def swapped(blocks, axis):
    return lax.all_to_all(blocks, axis, 0, 0, tiled=True)


def by_head(matrix):
    return jnp.stack([matrix[:, :HD], matrix[:, HD:]])


def project_kernel(h_ref, w_ref, q_ref, k_ref, v_ref, vt_ref, acc):
    step = pl.program_id(0)

    @pl.when(step == 0)
    def _():
        acc[...] = jnp.zeros_like(acc)

    total = acc[...]
    for xh in range(2):
        for core in range(2):
            rows = h_ref[core, 0, xh].reshape(160, 320)
            at = 2 * (2 * xh + core)
            weights = w_ref[at : at + 2, 0].reshape(320, 3 * HD)
            total = total + jnp.dot(rows, weights, preferred_element_type=F32)
    acc[...] = total

    @pl.when(step == pl.num_programs(0) - 1)
    def _():
        q_ref[0:64, :] = total[0:64, 0:HD].astype(BF16)
        q_ref[64:128, :] = total[80:144, 0:HD].astype(BF16)
        k_ref[...] = total[:, HD : 2 * HD].astype(BF16)
        v_ref[...] = total[:, 2 * HD :].astype(BF16)
        vt_ref[...] = total[:, 2 * HD :].T.astype(BF16)


def project(features, weights):
    shapes = ((128, HD), (160, HD), (160, HD), (HD, 160))
    return pl.pallas_call(
        project_kernel,
        grid=(4,),
        in_specs=[
            pl.BlockSpec((2, 1, 2, 2, 80, 320), lambda s: (0, s, 0, 0, 0, 0)),
            pl.BlockSpec((8, 1, 160, 3 * HD), lambda s: (s % 2, s // 2, 0, 0)),
        ],
        out_specs=[pl.BlockSpec(shape, lambda s: (0, 0)) for shape in shapes],
        out_shape=[jax.ShapeDtypeStruct(shape, BF16) for shape in shapes],
        scratch_shapes=[pltpu.VMEM((160, 3 * HD), F32)],
        compiler_params=pltpu.CompilerParams(vmem_limit_bytes=VMEM_LIMIT),
        cost_estimate=pl.CostEstimate(
            flops=2 * 160 * D * 384, bytes_accessed=6 * 2**20, transcendentals=0
        ),
    )(features, weights)


def in_three(value):
    high = value.astype(BF16).astype(F32)
    middle = (value - high).astype(BF16).astype(F32)
    return [high, middle, value - high - middle]


def attend_kernel(q_ref, kv_ref, vt_ref, kf_ref, vft_ref, out_ref):
    scale = 1.0 / math.sqrt(HD)
    queries = q_ref[...]
    lanes = queries.shape[0]
    across = (((1,), (1,)), ((), ()))

    def scores(keys):
        return lax.dot_general(keys, queries, across, preferred_element_type=F32) * scale

    parts = []
    for side in range(2):
        seen = kv_ref[side, 1024:1040, :].astype(F32)
        hidden = jnp.where(seen > 0.5, 0.0, -jnp.inf)
        hidden = jnp.concatenate([hidden] * (lanes // HD), axis=1)
        for slot in range(2):
            keys = kv_ref[side, slot * SLOT : (slot + 1) * SLOT, :]
            parts.append(scores(keys) + hidden[slot : slot + 1, :])
    token = lax.broadcasted_iota(jnp.int32, (160, lanes), 0)
    lane = lax.broadcasted_iota(jnp.int32, (160, lanes), 1)
    token = jnp.where(token >= 80, token - 80, token)
    visible = (token >= 64) | ((token >> 4) <= ((lane & 63) >> 4))
    parts.append(jnp.where(visible, scores(kf_ref[...]), -jnp.inf))

    peak = functools.reduce(
        jnp.maximum, [jnp.max(part, axis=0, keepdims=True) for part in parts]
    )
    numer = jnp.zeros((HD, lanes), F32)
    denom = jnp.zeros((1, lanes), F32)
    for i, part in enumerate(parts):
        weights = jnp.exp(part - peak).astype(BF16)
        denom = denom + jnp.sum(weights.astype(F32), axis=0, keepdims=True)
        if i < 4:
            values = vt_ref[i // 2, :, (i % 2) * SLOT : (i % 2 + 1) * SLOT]
        else:
            values = vft_ref[...]
        numer = numer + jnp.dot(values, weights, preferred_element_type=F32)
    mean = (numer / denom).astype(BF16)
    totals = jnp.concatenate(
        [*in_three(peak), *in_three(denom), jnp.zeros((10, lanes), F32)], axis=0
    ).astype(BF16)
    for block in range(lanes // HD):
        at = slice(block * HD, (block + 1) * HD)
        out_ref[block, 0:HD, :] = mean[:, at]
        out_ref[block, HD : HD + 16, :] = totals[:, at]


def attend(queries, kv, values_t, fresh_k, fresh_vt):
    step = 256
    rows = queries.shape[0]

    def whole(array):
        return pl.BlockSpec(array.shape, lambda s: (0,) * array.ndim)

    return pl.pallas_call(
        attend_kernel,
        grid=(rows // step,),
        in_specs=[
            pl.BlockSpec((step, HD), lambda s: (s, 0)),
            whole(kv),
            whole(values_t),
            whole(fresh_k),
            whole(fresh_vt),
        ],
        out_specs=pl.BlockSpec((step // HD, HD + 16, HD), lambda s: (s, 0, 0)),
        out_shape=jax.ShapeDtypeStruct((rows // HD, HD + 16, HD), BF16),
        compiler_params=pltpu.CompilerParams(vmem_limit_bytes=VMEM_LIMIT),
        cost_estimate=pl.CostEstimate(
            flops=4 * rows * 1184 * HD,
            bytes_accessed=3 * 2**20,
            transcendentals=rows * 1184,
        ),
    )(queries, kv, values_t, fresh_k, fresh_vt)


def combine_kernel(in_ref, out_ref):
    totals = in_ref[:, HD : HD + 16, :].astype(F32)
    peak = totals[:, 0, :] + totals[:, 1, :] + totals[:, 2, :]
    denom = totals[:, 3, :] + totals[:, 4, :] + totals[:, 5, :]
    top = jnp.max(peak, axis=0, keepdims=True)
    share = denom * jnp.exp(peak - top)
    share = share / jnp.sum(share, axis=0, keepdims=True)
    mixed = jnp.zeros((HD, HD), F32)
    for i in range(in_ref.shape[0]):
        mixed = mixed + in_ref[i, 0:HD, :].astype(F32) * share[i : i + 1, :]
    out_ref[...] = mixed.T.astype(BF16)


def combine(parts):
    return pl.pallas_call(
        combine_kernel,
        out_shape=jax.ShapeDtypeStruct((HD, HD), BF16),
        compiler_params=pltpu.CompilerParams(vmem_limit_bytes=VMEM_LIMIT),
    )(parts)


def output_kernel(att_ref, w_ref, y_ref):
    attention = jnp.concatenate([att_ref[0], att_ref[1]], axis=1)
    for z in range(16):
        part = jnp.dot(attention, w_ref[z], preferred_element_type=F32)
        for xl in range(2):
            j = 8 * xl + z // 2
            at = 160 * (z % 2)
            y_ref[j % 2, j // 2, :, at : at + 160] = part[:, 160 * xl : 160 * (xl + 1)]


def output_projection(attention, weights):
    return pl.pallas_call(
        output_kernel,
        out_shape=jax.ShapeDtypeStruct((2, 8, 64, 320), F32),
        compiler_params=pltpu.CompilerParams(vmem_limit_bytes=VMEM_LIMIT),
    )(attention, weights)


def local(
    state,
    clean_tokens,
    w_query,
    w_key,
    w_value,
    w_out,
    cache_keys,
    cache_values,
    norm_gain,
    mod_gain,
    out_gain,
    levels,
    noise_index,
    placement,
    group_mask,
):
    flight, ch_dev, width = state.shape
    rows_count = flight * ch_dev

    w_heads = jnp.concatenate([by_head(w) for w in (w_query, w_key, w_value)], axis=2)
    w_heads = swapped(w_heads, "xl")
    w_full = lax.all_gather(w_heads.reshape(320, 3 * HD), "z", axis=0, tiled=True)
    w_full = w_full.reshape(16, 2, 160, 3 * HD)

    current = level_lookup(levels, noise_index)
    following = level_lookup(levels, noise_index + 1)
    rows = jnp.concatenate(
        [state.reshape(rows_count, width), clean_tokens.astype(F32)], axis=0
    )
    sigma_rows = jnp.concatenate(
        [jnp.repeat(current, ch_dev), jnp.zeros((ch_dev,), F32)]
    )
    squares = sent_to_all(jnp.sum(rows * rows, axis=1), WIDE).sum(axis=0)
    inverse = lax.rsqrt(squares / D + EPSILON)
    features = (
        rows
        * inverse[:, None]
        * norm_gain[None, :]
        * (1.0 + sigma_rows[:, None] * mod_gain[None, :])
    ).astype(BF16)
    features = sent_to_all(features, ("y", "xh", "xl"))
    features = sent_to_all(features, "core").reshape(2, 4, 2, 2, 80, width)

    table = jnp.arange(group_mask.shape[1], dtype=jnp.int32)
    held = (placement[:, None] == table[None, :]).astype(jnp.int32)
    seen = jnp.sum(held[None, :, :] * group_mask[:, None, :], axis=2) != 0
    seen = jnp.repeat(seen.T.astype(BF16), ch_dev, axis=1)
    seen = jnp.pad(jnp.concatenate([seen, seen], axis=1), ((0, 14), (0, 0)))
    kv = jnp.concatenate(
        [
            by_head(cache_keys),
            by_head(cache_values),
            jnp.broadcast_to(seen[None], (2, *seen.shape)),
        ],
        axis=1,
    )
    kv = swapped(kv, "xl")
    values_t = jnp.transpose(kv[:, 512:1024], (0, 2, 1))

    q, k, v, vt = project(features, w_full)

    w_out_pair = sent_to_all(w_out, "xl")
    w_out_pair = jnp.concatenate([w_out_pair[0], w_out_pair[1]], axis=1)
    w_out_full = lax.all_gather(w_out_pair, "z", axis=0, tiled=False)

    queries = lax.all_gather(q, "z", axis=0, tiled=True)
    parts = attend(queries, kv, values_t, k, vt)
    parts = swapped(parts, "z")
    attention = combine(parts).reshape(2, rows_count, HD)
    attention = swapped(attention, "xl")

    finished = jnp.stack([k.reshape(2, 80, HD)[:, 64:], v.reshape(2, 80, HD)[:, 64:]], 1)
    finished = swapped(finished, "xl")
    new_keys = jnp.concatenate([finished[0, 0], finished[1, 0]], axis=1)
    new_values = jnp.concatenate([finished[0, 1], finished[1, 1]], axis=1)

    y = output_projection(attention, w_out_full)
    y = swapped(y, "core").sum(axis=0)
    y = swapped(y, ("y", "xh")).sum(axis=0)
    y_squares = sent_to_all(jnp.sum(y * y, axis=1), WIDE).sum(axis=0)
    velocity = y * lax.rsqrt(y_squares / D + EPSILON)[:, None] * out_gain[None, :]
    new_state = state + (following - current)[:, None, None] * velocity.reshape(
        flight, ch_dev, width
    )
    return new_state, new_keys, new_values


def solution(mesh):
    fine = Mesh(mesh.devices.reshape(4, 2, 16, 2, 2), ("y", "xl", "z", "xh", "core"))
    in_specs = (
        P(None, CTX, WIDE),
        P(CTX, WIDE),
        P(CTX, WIDE),
        P(CTX, WIDE),
        P(CTX, WIDE),
        P(WIDE, CTX),
        P(CTX, WIDE),
        P(CTX, WIDE),
        P(WIDE),
        P(WIDE),
        P(WIDE),
        P(),
        P(),
        P(CTX),
        P(),
    )
    out_specs = (P(None, CTX, WIDE), P(CTX, WIDE), P(CTX, WIDE))
    return jax.shard_map(local, mesh=fine, in_specs=in_specs, out_specs=out_specs, check_vma=False)
```

time: 473 us -> 267 us (0.56)
  blocking collectives: 193 us -> 58.9 us
  waiting for transfers between devices: 188 us -> 117 us
  starting transfers between devices: 22.9 us -> 45.6 us
  matrix products: 20.4 us -> 0 us
  Pallas kernels: 0 us -> 13 us
  local copies, waits for them, and re-layouts: 18.8 us -> 10.3 us
  other arithmetic: 13.8 us -> 6.14 us
    all_to_all x1 -> x2, blocking collectives: 89.2 us -> 14.7 us  [sent_to_all(): lax.all_to_all(jnp.broadcast_to(array[None], (devices, *array.shape)), ax...]
    reduce_scatter x2 -> x0, waiting for transfers between devices: 58.9 us -> none  [reduced_to_own(): tiles = lax.psum_scatter(tiles, axes[k], scatter_dimension=0, tiled=True)]
    unnamed x2 -> x0, blocking collectives: 46 us -> none
    all_to_all x1 -> x2, blocking collectives: 54 us -> 21.3 us  [swapped(): return lax.all_to_all(blocks, axis, 0, 0, tiled=True)]
    all_gather x2, waiting for transfers between devices: 99.6 us -> 68.1 us  [the longest x1 57.4 us: local(): w_out_full = lax.all_gather(w_out_pair, 'z', axis=0, tiled=False)]
    all_to_all x0 -> x5, starting transfers between devices: none -> 24.4 us  [swapped(): return lax.all_to_all(blocks, axis, 0, 0, tiled=True)]
    all_to_all x0 -> x5, waiting for transfers between devices: none -> 23.1 us  [swapped(): return lax.all_to_all(blocks, axis, 0, 0, tiled=True)]
    dot_general x10 -> x0, matrix products: 20.4 us -> none  [the longest x1 5.86 us: local(): jnp.einsum('fqhst,sthd->fqhd', cache_p, cache_v, preferred_element_type=j...]
  transfers between devices with their start and end apart: 7 -> 10, of which waited for: 6 -> 9; matrix products, arithmetic and copies ran while one was open for 5% -> 4% of each run, Pallas kernels for 0% -> 4%
where the time goes in v1:
time: 267 us; the launch traced here: 266 us
  waiting for transfers between devices  117 us (44%)
  blocking collectives  58.9 us (22%)
  starting transfers between devices  45.6 us (17%)
  between operations  14.4 us (5%)
  Pallas kernels  13 us (5%)
  local copies, waits for them, and re-layouts  10.3 us (4%)
  other arithmetic  6.14 us (2%)
    all_gather x1, waiting for transfers between devices, local(): w_out_full = lax.all_gather(w_out_pair, 'z', axis=0, tiled=False)  57.4 us
    all_to_all x3, waiting for transfers between devices, sent_to_all(): lax.all_to_all(jnp.broadcast_to(array[None], (devices, *array.shape)), ax...  25.9 us
    all_to_all x5, starting transfers between devices, swapped(): return lax.all_to_all(blocks, axis, 0, 0, tiled=True)  24.4 us
    all_to_all x5, waiting for transfers between devices, swapped(): return lax.all_to_all(blocks, axis, 0, 0, tiled=True)  23.1 us
    all_gather x1, blocking collectives, local(): queries = lax.all_gather(q, 'z', axis=0, tiled=True)  22.8 us
    all_to_all x2, blocking collectives, swapped(): return lax.all_to_all(blocks, axis, 0, 0, tiled=True)  21.3 us
    all_to_all x3, starting transfers between devices, sent_to_all(): lax.all_to_all(jnp.broadcast_to(array[None], (devices, *array.shape)), ax...  21.1 us
    all_to_all x2, blocking collectives, sent_to_all(): lax.all_to_all(jnp.broadcast_to(array[None], (devices, *array.shape)), ax...  14.7 us
  transfers between devices with their start and end apart: 10, of which 9 were waited for; matrix products, arithmetic and copies ran while one was open for 4% of the time, Pallas kernels for 4%

profile of v1, /device:TPU:1, one launch (start us, length us, event | category | flops | bytes accessed | tf_op | source)
XLA Modules:
  0.0 265.6 jit_solution(12626346513691966833)
XLA Ops:
  9.0 7.7 %all_to_all.62 = bf16[2,160,384]{2,1,0:T(8,128)(2,1)} all-to-all(bf16[2,160,384]{2,1,0:T(8,128)(2,1)S(1)} %maximum_maximum_fusion), channel_id=1, replica_groups=mesh['y'=4,'xl'=2,'z'=16,'xh'=2,'core'=2] {'xl'}, dimensions={0} | all-to-all | bytes 491520 | tf_op jit(solution)/shard_map/all_to_all | solution.py:38
  16.9 6.9 %all_to_all.63 = bf16[2,256,160]{1,2,0:T(8,128)(2,1)S(1)} all-to-all(bf16[2,256,160]{1,2,0:T(8,128)(2,1)S(1)} %broadcast_in_dim.22), channel_id=1, replica_groups=mesh['y'=4,'xl'=2,'z'=16,'xh'=2,'core'=2] {'xl'}, dimensions={0} | all-to-all | bytes 327680 | tf_op jit(solution)/shard_map/all_to_all | solution.py:32
  25.2 11.4 %all-to-all-start = ((f32[16,1,80]{2,1,0:T(1,128)}), f32[16,1,80]{2,1,0:T(1,128)S(1)}, u32[]{:S(2)}, u32[]{:S(2)}) async-start(f32[16,1,80]{2,1,0:T(1,128)} %broadcast_in_dim.16), calls=%async_computation | async-start | bytes 16384 | tf_op jit(solution)/shard_map/all_to_all | solution.py:32
  38.6 5.1 %all-to-all-done = f32[16,1,80]{2,1,0:T(1,128)S(1)} async-done(((f32[16,1,80]{2,1,0:T(1,128)}), f32[16,1,80]{2,1,0:T(1,128)S(1)}, u32[]{:S(2)}, u32[]{:S(2)}) %all-to-all-start) | async-done | bytes 5152 | tf_op jit(solution)/shard_map/all_to_all | solution.py:32
  43.7 3.5 %all-to-all-start.4 = ((bf16[2,1040,128]{2,1,0:T(8,128)(2,1)}), bf16[2,1040,128]{2,1,0:T(8,128)(2,1)S(1)}, u32[]{:S(2)}, u32[]{:S(2)}) async-start(bf16[2,1040,128]{2,1,0:T(8,128)(2,1)} %pad_maximum_fusion), calls=%async_computation.4 | async-start | bytes 1064960 | tf_op jit(solution)/shard_map/all_to_all | solution.py:38
  47.3 7.3 %all-to-all-done.4.kv_ref = bf16[2,1040,128]{2,1,0:T(8,128)(2,1)S(1)} async-done(((bf16[2,1040,128]{2,1,0:T(8,128)(2,1)}), bf16[2,1040,128]{2,1,0:T(8,128)(2,1)S(1)}, u32[]{:S(2)}, u32[]{:S(2)}) %all-to-all-start.4) | async-done | bytes 532512 | tf_op jit(solution)/shard_map/all_to_all | solution.py:38
  55.7 3.6 %all-to-all-start.1 = ((bf16[16,80,320]{2,1,0:T(8,128)(2,1)}), bf16[16,80,320]{2,1,0:T(8,128)(2,1)S(1)}, u32[]{:S(2)}, u32[]{:S(2)}) async-start(bf16[16,80,320]{2,1,0:T(8,128)(2,1)} %broadcast_in_dim.18), calls=%async_computation.1 | async-start | bytes 1966080 | tf_op jit(solution)/shard_map/all_to_all | solution.py:32
  59.5 14.5 %all-to-all-done.1 = bf16[16,80,320]{2,1,0:T(8,128)(2,1)S(1)} async-done(((bf16[16,80,320]{2,1,0:T(8,128)(2,1)}), bf16[16,80,320]{2,1,0:T(8,128)(2,1)S(1)}, u32[]{:S(2)}, u32[]{:S(2)}) %all-to-all-start.1) | async-done | bytes 819232 | tf_op jit(solution)/shard_map/all_to_all | solution.py:32
  74.2 7.8 %all_to_all.64 = bf16[2,16,80,320]{3,2,1,0:T(8,128)(2,1)S(1)} all-to-all(bf16[2,16,80,320]{3,2,1,0:T(8,128)(2,1)S(1)} %broadcast_in_dim.19), channel_id=1, replica_groups=mesh['y'=4,'xl'=2,'z'=16,'xh'=2,'core'=2] {'core'}, dimensions={0} | all-to-all | bytes 3276800 | tf_op jit(solution)/shard_map/all_to_all | solution.py:32
  82.0 10.8 %all-gather.4.cloned.1.call-done = bf16[5120,384]{1,0:T(8,128)(2,1)} async-done(((bf16[320,384]{1,0:T(8,128)(2,1)}), bf16[5120,384]{1,0:T(8,128)(2,1)}) %all-gather.4.cloned.1.call-update) | async-done | bytes 3932176 | tf_op jit(solution)/shard_map/all_gather | solution.py:230
  94.9 2.7 shard_map.166
  97.5 22.8 %all_gather.13.q_ref = bf16[2048,128]{1,0:T(8,128)(2,1)S(1)} all-gather(bf16[128,128]{1,0:T(8,128)(2,1)S(1)} %get-tuple-element.7), channel_id=1, replica_groups=mesh['y'=4,'xl'=2,'z'=16,'xh'=2,'core'=2] {'z'}, dimensions={0}, use_global_device_ids=true | all-gather | bytes 557056 | tf_op jit(solution)/shard_map/all_gather | solution.py:274
  120.3 7.9 %shard_map.167 = bf16[16,144,128]{2,1,0:T(8,128)(2,1)} custom-call(bf16[2048,128]{1,0:T(8,128)(2,1)S(1)} %all_gather.13.q_ref, bf16[2,1040,128]{2,1,0:T(8,128)(2,1)S(1)} %all-to-all-done.4.kv_ref, bf16[2,128,512]{2,1,0:T(8,128)(2,1)S(1)} %bitcast.53, bf16[160,128]{1,0:T(8,128)(2,1)S(1)} %get-tuple-element.8.kf_ref, bf16[128,160]{1,0:T(8,128)(2,1)S(1)} %get-tuple-element.9.vft_ref), custom_call_target="tpu_custom_call" | custom-call | flops 1241513984 | bytes 3145728 | tf_op jit(solution)/shard_map/pallas_call | solution.py:148
  128.2 7.4 %all-to-all-start.5 = ((bf16[16,144,128]{2,1,0:T(8,128)(2,1)}), bf16[16,144,128]{2,1,0:T(8,128)(2,1)}, u32[]{:S(2)}, u32[]{:S(2)}) async-start(bf16[16,144,128]{2,1,0:T(8,128)(2,1)} %shard_map.167), calls=%async_computation.5 | async-start | bytes 1179648 | tf_op jit(solution)/shard_map/all_to_all | solution.py:38
  135.6 57.4 %all-gather.6.cloned.1.call-done = bf16[4096,320]{0,1:T(8,128)(2,1)} async-done(((bf16[256,320]{0,1:T(8,128)(2,1)}), bf16[4096,320]{0,1:T(8,128)(2,1)}) %all-gather.6.cloned.1.call-update) | async-done | bytes 2621456 | tf_op jit(solution)/shard_map/all_gather | solution.py:272
  193.0 3.3 %copy.31 = bf16[4096,320]{1,0:T(8,128)(2,1)S(1)} copy(bf16[4096,320]{0,1:T(8,128)(2,1)} %all-gather.6.cloned.1.call-done) | data formatting | bytes 5242880 | tf_op jit(solution)/shard_map/all_gather | solution.py:272
  198.3 3.3 %all-to-all-start.6 = ((bf16[2,64,128]{2,1,0:T(8,128)(2,1)}), bf16[2,64,128]{2,1,0:T(8,128)(2,1)S(1)}, u32[]{:S(2)}, u32[]{:S(2)}) async-start(bf16[2,64,128]{2,1,0:T(8,128)(2,1)} %bitcast.17), calls=%async_computation.6 | async-start | bytes 65536 | tf_op jit(solution)/shard_map/all_to_all | solution.py:38
  202.2 2.2 all-to-all-done.6.att_ref
  205.0 13.6 %all_to_all.65 = f32[2,8,64,320]{3,2,1,0:T(8,128)S(1)} all-to-all(f32[2,8,64,320]{3,2,1,0:T(8,128)S(1)} %shard_map.169), channel_id=1, replica_groups=mesh['y'=4,'xl'=2,'z'=16,'xh'=2,'core'=2] {'core'}, dimensions={0} | all-to-all | bytes 2621440 | tf_op jit(solution)/shard_map/all_to_all | solution.py:38
  218.6 3.2 %all-to-all-start.11 = ((bf16[2,2,16,128]{3,2,1,0:T(8,128)(2,1)}), bf16[2,2,16,128]{3,2,1,0:T(8,128)(2,1)S(1)}, u32[]{:S(2)}, u32[]{:S(2)}) async-start(bf16[2,2,16,128]{3,2,1,0:T(8,128)(2,1)} %pad_maximum_fusion.3), calls=%async_computation.11 | async-start | bytes 32768 | tf_op jit(solution)/shard_map/all_to_all | solution.py:38
  224.5 7.0 %all-to-all-start.9 = ((f32[8,64,320]{2,1,0:T(8,128)}), f32[8,64,320]{2,1,0:T(8,128)S(1)}, u32[]{:S(2)}, u32[]{:S(2)}) async-start(f32[8,64,320]{2,1,0:T(8,128)} %reduce_sum.88), calls=%async_computation.9 | async-start | bytes 1572864 | tf_op jit(solution)/shard_map/all_to_all | solution.py:38
  232.1 12.0 %all-to-all-done.9 = f32[8,64,320]{2,1,0:T(8,128)S(1)} async-done(((f32[8,64,320]{2,1,0:T(8,128)}), f32[8,64,320]{2,1,0:T(8,128)S(1)}, u32[]{:S(2)}, u32[]{:S(2)}) %all-to-all-start.9) | async-done | bytes 655392 | tf_op jit(solution)/shard_map/all_to_all | solution.py:38
  244.9 6.0 %all-to-all-start.10 = ((f32[16,1,64]{2,1,0:T(1,128)}), f32[16,1,64]{2,1,0:T(1,128)S(1)}, u32[]{:S(2)}, u32[]{:S(2)}) async-start(f32[16,1,64]{2,1,0:T(1,128)} %broadcast_in_dim.23), calls=%async_computation.10 | async-start | bytes 16384 | tf_op jit(solution)/shard_map/all_to_all | solution.py:32
  251.5 6.4 %all-to-all-done.10 = f32[16,1,64]{2,1,0:T(1,128)S(1)} async-done(((f32[16,1,64]{2,1,0:T(1,128)}), f32[16,1,64]{2,1,0:T(1,128)S(1)}, u32[]{:S(2)}, u32[]{:S(2)}) %all-to-all-start.10) | async-done | bytes 4128 | tf_op jit(solution)/shard_map/all_to_all | solution.py:32
  (79 shorter events, 17.4 us)
Async XLA Ops:
  7.2 9.7 %copy-start.4 = (bf16[256,160]{0,1:T(8,128)(2,1)S(1)}, bf16[256,160]{0,1:T(8,128)(2,1)}, u32[]{:S(2)}) copy-start(bf16[256,160]{0,1:T(8,128)(2,1)} %param.20) | copy-start | bytes 245764
  7.2 85.6 %all-gather.4.cloned.1.call-start = ((), (), s32[]{:S(2)}) async-start(), calls=%async_computation.12 | async-start | bytes 4177920 | tf_op jit(solution)/shard_map/all_gather | solution.py:230
  8.9 15.6 %copy-start.5 = (bf16[16,320]{1,0:T(8,128)(2,1)S(1)}, bf16[16,320]{1,0:T(8,128)(2,1)}, u32[]{:S(2)}) copy-start(bf16[16,320]{1,0:T(8,128)(2,1)} %param.16) | copy-start | bytes 30724
  8.9 15.6 %copy-start.1 = (f32[4,16,320]{2,1,0:T(8,128)S(1)}, f32[4,16,320]{2,1,0:T(8,128)}, u32[]{:S(2)}) copy-start(f32[4,16,320]{2,1,0:T(8,128)} %param.15) | copy-start | bytes 245764
  8.9 27.7 %copy-start.12 = (s32[2]{0:T(128)S(1)}, s32[2]{0:T(128)}, u32[]{:S(2)}) copy-start(s32[2]{0:T(128)} %param.28) | copy-start | bytes 28
  9.0 27.8 %copy-start.9 = (s32[4,64]{1,0:T(4,128)S(1)}, s32[4,64]{1,0:T(4,128)}, u32[]{:S(2)}) copy-start(s32[4,64]{1,0:T(4,128)} %param.29) | copy-start | bytes 3076
  9.0 28.2 %copy-start.11 = (s32[4]{0:T(128)S(1)}, s32[4]{0:T(128)}, u32[]{:S(2)}) copy-start(s32[4]{0:T(128)} %param.27) | copy-start | bytes 52
  9.0 28.2 %copy-start.2 = (bf16[512,256]{1,0:T(8,128)(2,1)S(1)}, bf16[512,256]{1,0:T(8,128)(2,1)}, u32[]{:S(2)}) copy-start(bf16[512,256]{1,0:T(8,128)(2,1)} %param.22) | copy-start | bytes 786436
  9.0 28.2 %copy-start.3 = (bf16[512,256]{1,0:T(8,128)(2,1)S(1)}, bf16[512,256]{1,0:T(8,128)(2,1)}, u32[]{:S(2)}) copy-start(bf16[512,256]{1,0:T(8,128)(2,1)} %param.21) | copy-start | bytes 786436
  16.8 176.2 %all-gather.6.cloned.1.call-start = ((), (), s32[]{:S(2)}) async-start(), calls=%async_computation.13 | async-start | bytes 2785280 | tf_op jit(solution)/shard_map/all_gather | solution.py:272
  25.2 18.4 %all-to-all-start = ((f32[16,1,80]{2,1,0:T(1,128)}), f32[16,1,80]{2,1,0:T(1,128)S(1)}, u32[]{:S(2)}, u32[]{:S(2)}) async-start(f32[16,1,80]{2,1,0:T(1,128)} %broadcast_in_dim.16), calls=%async_computation | async-start | bytes 16384 | tf_op jit(solution)/shard_map/all_to_all | solution.py:32
  37.2 1.0 copy-start.10
  37.3 9.9 %copy-start.6 = (f32[320]{0:T(512)S(1)}, f32[320]{0:T(512)}, u32[]{:S(2)}) copy-start(f32[320]{0:T(512)} %param.24) | copy-start | bytes 3844
  37.3 9.9 %copy-start.7 = (f32[320]{0:T(512)S(1)}, f32[320]{0:T(512)}, u32[]{:S(2)}) copy-start(f32[320]{0:T(512)} %param.23) | copy-start | bytes 3844
  43.7 11.0 %all-to-all-start.4 = ((bf16[2,1040,128]{2,1,0:T(8,128)(2,1)}), bf16[2,1040,128]{2,1,0:T(8,128)(2,1)S(1)}, u32[]{:S(2)}, u32[]{:S(2)}) async-start(bf16[2,1040,128]{2,1,0:T(8,128)(2,1)} %pad_maximum_fusion), calls=%async_computation.4 | async-start | bytes 1064960 | tf_op jit(solution)/shard_map/all_to_all | solution.py:38
  55.7 18.3 %all-to-all-start.1 = ((bf16[16,80,320]{2,1,0:T(8,128)(2,1)}), bf16[16,80,320]{2,1,0:T(8,128)(2,1)S(1)}, u32[]{:S(2)}, u32[]{:S(2)}) async-start(bf16[16,80,320]{2,1,0:T(8,128)(2,1)} %broadcast_in_dim.18), calls=%async_computation.1 | async-start | bytes 1966080 | tf_op jit(solution)/shard_map/all_to_all | solution.py:32
  92.8 2.1 copy-start
  128.2 68.2 %all-to-all-start.5 = ((bf16[16,144,128]{2,1,0:T(8,128)(2,1)}), bf16[16,144,128]{2,1,0:T(8,128)(2,1)}, u32[]{:S(2)}, u32[]{:S(2)}) async-start(bf16[16,144,128]{2,1,0:T(8,128)(2,1)} %shard_map.167), calls=%async_computation.5 | async-start | bytes 1179648 | tf_op jit(solution)/shard_map/all_to_all | solution.py:38
  198.3 6.0 %all-to-all-start.6 = ((bf16[2,64,128]{2,1,0:T(8,128)(2,1)}), bf16[2,64,128]{2,1,0:T(8,128)(2,1)S(1)}, u32[]{:S(2)}, u32[]{:S(2)}) async-start(bf16[2,64,128]{2,1,0:T(8,128)(2,1)} %bitcast.17), calls=%async_computation.6 | async-start | bytes 65536 | tf_op jit(solution)/shard_map/all_to_all | solution.py:38
  218.6 5.9 %all-to-all-start.11 = ((bf16[2,2,16,128]{3,2,1,0:T(8,128)(2,1)}), bf16[2,2,16,128]{3,2,1,0:T(8,128)(2,1)S(1)}, u32[]{:S(2)}, u32[]{:S(2)}) async-start(bf16[2,2,16,128]{3,2,1,0:T(8,128)(2,1)} %pad_maximum_fusion.3), calls=%async_computation.11 | async-start | bytes 32768 | tf_op jit(solution)/shard_map/all_to_all | solution.py:38
  222.9 35.1 %copy-start.8 = (f32[320]{0:T(512)S(1)}, f32[320]{0:T(512)}, u32[]{:S(2)}) copy-start(f32[320]{0:T(512)} %param.25) | copy-start | bytes 3844
  224.5 19.6 %all-to-all-start.9 = ((f32[8,64,320]{2,1,0:T(8,128)}), f32[8,64,320]{2,1,0:T(8,128)S(1)}, u32[]{:S(2)}, u32[]{:S(2)}) async-start(f32[8,64,320]{2,1,0:T(8,128)} %reduce_sum.88), calls=%async_computation.9 | async-start | bytes 1572864 | tf_op jit(solution)/shard_map/all_to_all | solution.py:38
  244.9 13.0 %all-to-all-start.10 = ((f32[16,1,64]{2,1,0:T(1,128)}), f32[16,1,64]{2,1,0:T(1,128)S(1)}, u32[]{:S(2)}, u32[]{:S(2)}) async-start(f32[16,1,64]{2,1,0:T(1,128)} %broadcast_in_dim.23), calls=%async_computation.10 | async-start | bytes 16384 | tf_op jit(solution)/shard_map/all_to_all | solution.py:32
Sparse Core Ops, SparseCore 0:
  16.9 75.8 all-gather.3
  94.8 98.2 all-gather.5

commit v2 on v1

--- a/solution.py
+++ b/solution.py
@@ -13,7 +13,7 @@
 HD = 128
 SLOT = 256
 EPSILON = 1e-06
-VMEM_LIMIT = 48 * 1024 * 1024
+VMEM_LIMIT = 56 * 1024 * 1024
 
 CTX = ("xl", "z")
 WIDE = ("y", "xh", "core")
@@ -54,7 +54,7 @@
         for core in range(2):
             rows = h_ref[core, 0, xh].reshape(160, 320)
             at = 2 * (2 * xh + core)
-            weights = w_ref[at : at + 2, 0].reshape(320, 3 * HD)
+            weights = w_ref[at : at + 2].reshape(320, 3 * HD)
             total = total + jnp.dot(rows, weights, preferred_element_type=F32)
     acc[...] = total
 
@@ -74,7 +74,7 @@
         grid=(4,),
         in_specs=[
             pl.BlockSpec((2, 1, 2, 2, 80, 320), lambda s: (0, s, 0, 0, 0, 0)),
-            pl.BlockSpec((8, 1, 160, 3 * HD), lambda s: (s % 2, s // 2, 0, 0)),
+            pl.BlockSpec((8, 160, 3 * HD), lambda s: (s % 2, s // 2, 0)),
         ],
         out_specs=[pl.BlockSpec(shape, lambda s: (0, 0)) for shape in shapes],
         out_shape=[jax.ShapeDtypeStruct(shape, BF16) for shape in shapes],
@@ -187,20 +187,40 @@
     )(parts)
 
 
+def spread_kernel(w_ref, out_ref):
+    for m in range(8):
+        block = w_ref[2 * m : 2 * m + 2].reshape(320, HD)
+        out_ref[2 * m] = block
+        out_ref[2 * m + 1] = block
+
+
+def spread(weights):
+    return pl.pallas_call(
+        spread_kernel,
+        grid=(2,),
+        in_specs=[pl.BlockSpec((16, 160, HD), lambda s: (0, s, 3))],
+        out_specs=pl.BlockSpec((16, 320, HD), lambda s: (s, 0, 0)),
+        out_shape=jax.ShapeDtypeStruct((32, 320, HD), BF16),
+        compiler_params=pltpu.CompilerParams(vmem_limit_bytes=VMEM_LIMIT),
+        cost_estimate=pl.CostEstimate(flops=0, bytes_accessed=4 * 2**20, transcendentals=0),
+    )(weights)
+
+
 def output_kernel(att_ref, w_ref, y_ref):
-    attention = jnp.concatenate([att_ref[0], att_ref[1]], axis=1)
-    for z in range(16):
-        part = jnp.dot(attention, w_ref[z], preferred_element_type=F32)
-        for xl in range(2):
-            j = 8 * xl + z // 2
-            at = 160 * (z % 2)
-            y_ref[j % 2, j // 2, :, at : at + 160] = part[:, 160 * xl : 160 * (xl + 1)]
+    total = jnp.zeros(y_ref.shape, F32)
+    for i in range(16):
+        attention = jnp.concatenate([att_ref[2 * i], att_ref[2 * i + 1]], axis=1)
+        weights = jnp.concatenate([w_ref[2 * i], w_ref[2 * i + 1]], axis=1)
+        total = total + lax.dot_general(
+            attention, weights, (((1,), (1,)), ((), ())), preferred_element_type=F32
+        )
+    y_ref[...] = total
 
 
 def output_projection(attention, weights):
     return pl.pallas_call(
         output_kernel,
-        out_shape=jax.ShapeDtypeStruct((2, 8, 64, 320), F32),
+        out_shape=jax.ShapeDtypeStruct((64, 320), F32),
         compiler_params=pltpu.CompilerParams(vmem_limit_bytes=VMEM_LIMIT),
     )(attention, weights)
 
@@ -225,10 +245,10 @@
     flight, ch_dev, width = state.shape
     rows_count = flight * ch_dev
 
-    w_heads = jnp.concatenate([by_head(w) for w in (w_query, w_key, w_value)], axis=2)
-    w_heads = swapped(w_heads, "xl")
-    w_full = lax.all_gather(w_heads.reshape(320, 3 * HD), "z", axis=0, tiled=True)
-    w_full = w_full.reshape(16, 2, 160, 3 * HD)
+    parts = [by_head(w) for w in (w_query, w_key, w_value)]
+    parts.append(jnp.transpose(w_out.reshape(2, HD, 160), (0, 2, 1)))
+    shard = swapped(jnp.concatenate(parts, axis=2), "xl").reshape(320, 4 * HD)
+    w_full = lax.all_gather(shard, "z", axis=0, tiled=False)
 
     current = level_lookup(levels, noise_index)
     following = level_lookup(levels, noise_index + 1)
@@ -265,17 +285,20 @@
     kv = swapped(kv, "xl")
     values_t = jnp.transpose(kv[:, 512:1024], (0, 2, 1))
 
+    w_full, values_t = lax.optimization_barrier((w_full, values_t))
     q, k, v, vt = project(features, w_full)
 
-    w_out_pair = sent_to_all(w_out, "xl")
-    w_out_pair = jnp.concatenate([w_out_pair[0], w_out_pair[1]], axis=1)
-    w_out_full = lax.all_gather(w_out_pair, "z", axis=0, tiled=False)
+    w_out_blocks = spread(w_full)
+    q, w_out_blocks = lax.optimization_barrier((q, w_out_blocks))
+    w_out_full = swapped(w_out_blocks, (*WIDE, "xl"))
 
     queries = lax.all_gather(q, "z", axis=0, tiled=True)
     parts = attend(queries, kv, values_t, k, vt)
+    parts, w_out_full = lax.optimization_barrier((parts, w_out_full))
     parts = swapped(parts, "z")
-    attention = combine(parts).reshape(2, rows_count, HD)
-    attention = swapped(attention, "xl")
+    attention = combine(parts).reshape(1, 2, rows_count, HD)
+    attention = jnp.broadcast_to(attention, (16, 2, rows_count, HD))
+    attention = swapped(attention.reshape(32, rows_count, HD), (*WIDE, "xl"))
 
     finished = jnp.stack([k.reshape(2, 80, HD)[:, 64:], v.reshape(2, 80, HD)[:, 64:]], 1)
     finished = swapped(finished, "xl")
@@ -283,8 +306,6 @@
     new_values = jnp.concatenate([finished[0, 1], finished[1, 1]], axis=1)
 
     y = output_projection(attention, w_out_full)
-    y = swapped(y, "core").sum(axis=0)
-    y = swapped(y, ("y", "xh")).sum(axis=0)
     y_squares = sent_to_all(jnp.sum(y * y, axis=1), WIDE).sum(axis=0)
     velocity = y * lax.rsqrt(y_squares / D + EPSILON)[:, None] * out_gain[None, :]
     new_state = state + (following - current)[:, None, None] * velocity.reshape(

time: 267 us -> 252 us (0.944)
  waiting for transfers between devices: 117 us -> 88.1 us
  starting transfers between devices: 45.6 us -> 70.9 us
  blocking collectives: 58.9 us -> 35.8 us
  Pallas kernels: 13 us -> 22.4 us
  local copies, waits for them, and re-layouts: 10.3 us -> 13.1 us
    all_gather x2 -> x1, waiting for transfers between devices: 68.1 us -> 24 us  [local(): w_full = lax.all_gather(shard, 'z', axis=0, tiled=False)]
    all_to_all x5, starting transfers between devices: 24.4 us -> 44.7 us  [swapped(): return lax.all_to_all(blocks, axis, 0, 0, tiled=True)]
    all_to_all x5, waiting for transfers between devices: 23.1 us -> 38.8 us  [swapped(): return lax.all_to_all(blocks, axis, 0, 0, tiled=True)]
    all_to_all x2 -> x0, blocking collectives: 14.7 us -> none  [sent_to_all(): lax.all_to_all(jnp.broadcast_to(array[None], (devices, *array.shape)), ax...]
    all_to_all x2 -> x1, blocking collectives: 21.3 us -> 8.06 us  [swapped(): return lax.all_to_all(blocks, axis, 0, 0, tiled=True)]
    pallas_call x1 -> x2, Pallas kernels: 0.63 us -> 6.17 us  [the longest x1 3.4 us: output_projection(): pl.pallas_call(output_kernel, out_shape=jax.ShapeDtypeStruct((64, 320), F...]
    all_to_all x3 -> x4, starting transfers between devices: 21.1 us -> 26.2 us  [sent_to_all(): lax.all_to_all(jnp.broadcast_to(array[None], (devices, *array.shape)), ax...]
    all_gather x1, blocking collectives: 22.8 us -> 27.8 us  [local(): queries = lax.all_gather(q, 'z', axis=0, tiled=True)]
  transfers between devices with their start and end apart: 10 -> 10, of which waited for: 9 -> 8; matrix products, arithmetic and copies ran while one was open for 4% -> 4% of each run, Pallas kernels for 4% -> 6%
where the time goes in v2:
time: 252 us; the launch traced here: 251 us
  waiting for transfers between devices  88.1 us (35%)
  starting transfers between devices  70.9 us (28%)
  blocking collectives  35.8 us (14%)
  Pallas kernels  22.4 us (9%)
  between operations  14.3 us (6%)
  local copies, waits for them, and re-layouts  13.1 us (5%)
  other arithmetic  6.16 us (2%)
    all_to_all x5, starting transfers between devices, swapped(): return lax.all_to_all(blocks, axis, 0, 0, tiled=True)  44.7 us
    all_to_all x5, waiting for transfers between devices, swapped(): return lax.all_to_all(blocks, axis, 0, 0, tiled=True)  38.8 us
    all_gather x1, blocking collectives, local(): queries = lax.all_gather(q, 'z', axis=0, tiled=True)  27.8 us
    all_to_all x4, starting transfers between devices, sent_to_all(): lax.all_to_all(jnp.broadcast_to(array[None], (devices, *array.shape)), ax...  26.2 us
    all_to_all x4, waiting for transfers between devices, sent_to_all(): lax.all_to_all(jnp.broadcast_to(array[None], (devices, *array.shape)), ax...  25.3 us
    all_gather x1, waiting for transfers between devices, local(): w_full = lax.all_gather(shard, 'z', axis=0, tiled=False)  24 us
    pallas_call x1, Pallas kernels, attend(): pl.pallas_call(attend_kernel, grid=(rows // step,), in_specs=[pl.BlockSpe...  9.2 us
    all_to_all x1, blocking collectives, swapped(): return lax.all_to_all(blocks, axis, 0, 0, tiled=True)  8.06 us
  transfers between devices with their start and end apart: 10, of which 8 were waited for; matrix products, arithmetic and copies ran while one was open for 4% of the time, Pallas kernels for 6%

profile of v2, /device:TPU:1, one launch (start us, length us, event | category | flops | bytes accessed | tf_op | source)
XLA Modules:
  0.0 250.9 jit_solution(3653950360999012602)
XLA Ops:
  9.9 8.1 %all_to_all.52 = bf16[2,160,512]{2,1,0:T(8,128)(2,1)} all-to-all(bf16[2,160,512]{2,1,0:T(8,128)(2,1)S(1)} %pad_maximum_fusion.1), channel_id=1, replica_groups=mesh['y'=4,'xl'=2,'z'=16,'xh'=2,'core'=2] {'xl'}, dimensions={0} | all-to-all | bytes 655360 | tf_op jit(solution)/shard_map/all_to_all | solution.py:38
  18.8 10.7 %all-to-all-start = ((f32[16,1,80]{2,1,0:T(1,128)}), f32[16,1,80]{2,1,0:T(1,128)S(1)}, u32[]{:S(2)}, u32[]{:S(2)}) async-start(f32[16,1,80]{2,1,0:T(1,128)} %broadcast_in_dim.18), calls=%async_computation | async-start | bytes 16384 | tf_op jit(solution)/shard_map/all_to_all | solution.py:32
  31.4 5.1 %all-to-all-done = f32[16,1,80]{2,1,0:T(1,128)S(1)} async-done(((f32[16,1,80]{2,1,0:T(1,128)}), f32[16,1,80]{2,1,0:T(1,128)S(1)}, u32[]{:S(2)}, u32[]{:S(2)}) %all-to-all-start) | async-done | bytes 5152 | tf_op jit(solution)/shard_map/all_to_all | solution.py:32
  36.5 3.5 %all-to-all-start.4 = ((bf16[2,1040,128]{2,1,0:T(8,128)(2,1)}), bf16[2,1040,128]{2,1,0:T(8,128)(2,1)S(1)}, u32[]{:S(2)}, u32[]{:S(2)}) async-start(bf16[2,1040,128]{2,1,0:T(8,128)(2,1)} %pad_maximum_fusion), calls=%async_computation.4 | async-start | bytes 1064960 | tf_op jit(solution)/shard_map/all_to_all | solution.py:38
  40.1 7.4 %all-to-all-done.4.kv_ref = bf16[2,1040,128]{2,1,0:T(8,128)(2,1)S(1)} async-done(((bf16[2,1040,128]{2,1,0:T(8,128)(2,1)}), bf16[2,1040,128]{2,1,0:T(8,128)(2,1)S(1)}, u32[]{:S(2)}, u32[]{:S(2)}) %all-to-all-start.4) | async-done | bytes 532512 | tf_op jit(solution)/shard_map/all_to_all | solution.py:38
  48.7 3.6 %all-to-all-start.1 = ((bf16[16,80,320]{2,1,0:T(8,128)(2,1)}), bf16[16,80,320]{2,1,0:T(8,128)(2,1)S(1)}, u32[]{:S(2)}, u32[]{:S(2)}) async-start(bf16[16,80,320]{2,1,0:T(8,128)(2,1)} %broadcast_in_dim.20), calls=%async_computation.1 | async-start | bytes 1966080 | tf_op jit(solution)/shard_map/all_to_all | solution.py:32
  53.3 13.9 %all-to-all-done.1 = bf16[16,80,320]{2,1,0:T(8,128)(2,1)S(1)} async-done(((bf16[16,80,320]{2,1,0:T(8,128)(2,1)}), bf16[16,80,320]{2,1,0:T(8,128)(2,1)S(1)}, u32[]{:S(2)}, u32[]{:S(2)}) %all-to-all-start.1) | async-done | bytes 819232 | tf_op jit(solution)/shard_map/all_to_all | solution.py:32
  68.6 6.6 %all-to-all-start.2 = ((bf16[2,16,80,320]{3,2,1,0:T(8,128)(2,1)}), bf16[2,16,80,320]{3,2,1,0:T(8,128)(2,1)S(1)}, u32[]{:S(2)}, u32[]{:S(2)}) async-start(bf16[2,16,80,320]{3,2,1,0:T(8,128)(2,1)} %broadcast_in_dim.21), calls=%async_computation.2 | async-start | bytes 3932160 | tf_op jit(solution)/shard_map/all_to_all | solution.py:32
  75.2 24.0 %all-gather.2.cloned.1.call-done.w_ref = bf16[16,320,512]{2,1,0:T(8,128)(2,1)} async-done(((bf16[1,320,512]{2,1,0:T(8,128)(2,1)}), bf16[16,320,512]{2,1,0:T(8,128)(2,1)}) %all-gather.2.cloned.1.call-update) | async-done | bytes 5242896 | tf_op jit(solution)/shard_map/all_gather | solution.py:251
  99.2 2.8 %shard_map.167 = bf16[32,320,128]{2,1,0:T(8,128)(2,1)} custom-call(bf16[16,320,512]{2,1,0:T(8,128)(2,1)} %all-gather.2.cloned.1.call-done.w_ref), custom_call_target="tpu_custom_call" | custom-call | bytes 4194304 | tf_op jit(solution)/shard_map/pallas_call | solution.py:198
  103.3 5.1 %shard_map.166 = (bf16[128,128]{1,0:T(8,128)(2,1)}, bf16[160,128]{1,0:T(8,128)(2,1)}, bf16[160,128]{1,0:T(8,128)(2,1)}, bf16[128,160]{1,0:T(8,128)(2,1)}) custom-call(bf16[2,4,2,2,80,320]{5,4,3,2,1,0:T(8,128)(2,1)} %bitcast.52, bf16[16,320,512]{2,1,0:T(8,128)(2,1)} %all-gather.2.cloned.1.call-done.w_ref), custom_call_target="tpu_custom_call" | custom-call | flops 629145600 | bytes 6291456 | tf_op jit(solution)/shard_map/pallas_call | solution.py:72
  108.4 14.2 %all-to-all-start.5 = ((bf16[32,320,128]{2,1,0:T(8,128)(2,1)}), bf16[32,320,128]{2,1,0:T(8,128)(2,1)S(1)}, u32[]{:S(2)}, u32[]{:S(2)}) async-start(bf16[32,320,128]{2,1,0:T(8,128)(2,1)} %shard_map.167), calls=%async_computation.5 | async-start | bytes 5242880 | tf_op jit(solution)/shard_map/all_to_all | solution.py:38
  122.6 27.8 %all_gather.7.q_ref = bf16[2048,128]{1,0:T(8,128)(2,1)} all-gather(bf16[128,128]{1,0:T(8,128)(2,1)S(1)} %copy-done.9), channel_id=1, replica_groups=mesh['y'=4,'xl'=2,'z'=16,'xh'=2,'core'=2] {'z'}, dimensions={0}, use_global_device_ids=true | all-gather | bytes 557056 | tf_op jit(solution)/shard_map/all_gather | solution.py:295
  150.4 9.2 %shard_map.168 = bf16[16,144,128]{2,1,0:T(8,128)(2,1)} custom-call(bf16[2048,128]{1,0:T(8,128)(2,1)} %all_gather.7.q_ref, bf16[2,1040,128]{2,1,0:T(8,128)(2,1)} %copy-done.5, bf16[2,128,512]{2,1,0:T(8,128)(2,1)} %bitcast.58, bf16[160,128]{1,0:T(8,128)(2,1)} %get-tuple-element.17.kf_ref, bf16[128,160]{1,0:T(8,128)(2,1)} %get-tuple-element.18.vft_ref), custom_call_target="tpu_custom_call" | custom-call | flops 1241513984 | bytes 3145728 | tf_op jit(solution)/shard_map/pallas_call | solution.py:148
  159.6 6.5 %all-to-all-start.6 = ((bf16[16,144,128]{2,1,0:T(8,128)(2,1)}), bf16[16,144,128]{2,1,0:T(8,128)(2,1)S(1)}, u32[]{:S(2)}, u32[]{:S(2)}) async-start(bf16[16,144,128]{2,1,0:T(8,128)(2,1)} %shard_map.168), calls=%async_computation.6 | async-start | bytes 1179648 | tf_op jit(solution)/shard_map/all_to_all | solution.py:38
  168.2 20.5 %all-to-all-done.6.in_ref = bf16[16,144,128]{2,1,0:T(8,128)(2,1)S(1)} async-done(((bf16[16,144,128]{2,1,0:T(8,128)(2,1)}), bf16[16,144,128]{2,1,0:T(8,128)(2,1)S(1)}, u32[]{:S(2)}, u32[]{:S(2)}) %all-to-all-start.6) | async-done | bytes 589856 | tf_op jit(solution)/shard_map/all_to_all | solution.py:38
  188.7 3.2 %all-to-all-start.9 = ((bf16[2,2,16,128]{3,2,1,0:T(8,128)(2,1)}), bf16[2,2,16,128]{3,2,1,0:T(8,128)(2,1)S(1)}, u32[]{:S(2)}, u32[]{:S(2)}) async-start(bf16[2,2,16,128]{3,2,1,0:T(8,128)(2,1)} %pad_maximum_fusion.3), calls=%async_computation.9 | async-start | bytes 32768 | tf_op jit(solution)/shard_map/all_to_all | solution.py:38
  192.0 1.9 shard_map.169
  195.0 1.7 broadcast_in_dim.25
  196.7 17.2 %all-to-all-start.7 = ((bf16[32,64,128]{2,1,0:T(8,128)(2,1)}), bf16[32,64,128]{2,1,0:T(8,128)(2,1)S(1)}, u32[]{:S(2)}, u32[]{:S(2)}) async-start(bf16[32,64,128]{2,1,0:T(8,128)(2,1)} %bitcast.53), calls=%async_computation.7 | async-start | bytes 1048576 | tf_op jit(solution)/shard_map/all_to_all | solution.py:38
  214.5 9.8 %all-to-all-done.7.att_ref = bf16[32,64,128]{2,1,0:T(8,128)(2,1)S(1)} async-done(((bf16[32,64,128]{2,1,0:T(8,128)(2,1)}), bf16[32,64,128]{2,1,0:T(8,128)(2,1)S(1)}, u32[]{:S(2)}, u32[]{:S(2)}) %all-to-all-start.7) | async-done | bytes 524320 | tf_op jit(solution)/shard_map/all_to_all | solution.py:38
  225.0 3.4 %shard_map.170 = f32[64,320]{1,0:T(8,128)} custom-call(bf16[32,64,128]{2,1,0:T(8,128)(2,1)} %copy-done.4, bf16[32,320,128]{2,1,0:T(8,128)(2,1)} %copy-done.1), custom_call_target="tpu_custom_call" | custom-call | tf_op jit(solution)/shard_map/pallas_call | solution.py:221
  230.0 5.3 %all-to-all-start.8 = ((f32[16,1,64]{2,1,0:T(1,128)}), f32[16,1,64]{2,1,0:T(1,128)S(1)}, u32[]{:S(2)}, u32[]{:S(2)}) async-start(f32[16,1,64]{2,1,0:T(1,128)} %broadcast_in_dim.26), calls=%async_computation.8 | async-start | bytes 16384 | tf_op jit(solution)/shard_map/all_to_all | solution.py:32
  235.9 6.4 %all-to-all-done.8 = f32[16,1,64]{2,1,0:T(1,128)S(1)} async-done(((f32[16,1,64]{2,1,0:T(1,128)}), f32[16,1,64]{2,1,0:T(1,128)S(1)}, u32[]{:S(2)}, u32[]{:S(2)}) %all-to-all-start.8) | async-done | bytes 4128 | tf_op jit(solution)/shard_map/all_to_all | solution.py:32
  (82 shorter events, 18.8 us)
Async XLA Ops:
  7.2 92.0 %all-gather.2.cloned.1.call-start = ((), (), s32[]{:S(2)}) async-start(), calls=%async_computation.10 | async-start | bytes 5570560 | tf_op jit(solution)/shard_map/all_gather | solution.py:251
  8.1 10.0 %copy-start.10 = (bf16[16,320]{1,0:T(8,128)(2,1)S(1)}, bf16[16,320]{1,0:T(8,128)(2,1)}, u32[]{:S(2)}) copy-start(bf16[16,320]{1,0:T(8,128)(2,1)} %param.16) | copy-start | bytes 30724
  8.1 10.0 %copy-start.6 = (f32[4,16,320]{2,1,0:T(8,128)S(1)}, f32[4,16,320]{2,1,0:T(8,128)}, u32[]{:S(2)}) copy-start(f32[4,16,320]{2,1,0:T(8,128)} %param.15) | copy-start | bytes 245764
  8.9 20.6 %copy-start.17 = (s32[2]{0:T(128)S(1)}, s32[2]{0:T(128)}, u32[]{:S(2)}) copy-start(s32[2]{0:T(128)} %param.28) | copy-start | bytes 28
  8.9 20.6 %copy-start.14 = (s32[4,64]{1,0:T(4,128)S(1)}, s32[4,64]{1,0:T(4,128)}, u32[]{:S(2)}) copy-start(s32[4,64]{1,0:T(4,128)} %param.29) | copy-start | bytes 3076
  8.9 21.0 %copy-start.16 = (s32[4]{0:T(128)S(1)}, s32[4]{0:T(128)}, u32[]{:S(2)}) copy-start(s32[4]{0:T(128)} %param.27) | copy-start | bytes 52
  8.9 21.0 %copy-start.7 = (bf16[512,256]{1,0:T(8,128)(2,1)S(1)}, bf16[512,256]{1,0:T(8,128)(2,1)}, u32[]{:S(2)}) copy-start(bf16[512,256]{1,0:T(8,128)(2,1)} %param.22) | copy-start | bytes 786436
  9.0 21.0 %copy-start.8 = (bf16[512,256]{1,0:T(8,128)(2,1)S(1)}, bf16[512,256]{1,0:T(8,128)(2,1)}, u32[]{:S(2)}) copy-start(bf16[512,256]{1,0:T(8,128)(2,1)} %param.21) | copy-start | bytes 786436
  18.8 17.7 %all-to-all-start = ((f32[16,1,80]{2,1,0:T(1,128)}), f32[16,1,80]{2,1,0:T(1,128)S(1)}, u32[]{:S(2)}, u32[]{:S(2)}) async-start(f32[16,1,80]{2,1,0:T(1,128)} %broadcast_in_dim.18), calls=%async_computation | async-start | bytes 16384 | tf_op jit(solution)/shard_map/all_to_all | solution.py:32
  30.1 9.9 %copy-start.11 = (f32[320]{0:T(512)S(1)}, f32[320]{0:T(512)}, u32[]{:S(2)}) copy-start(f32[320]{0:T(512)} %param.24) | copy-start | bytes 3844
  30.1 9.9 %copy-start.12 = (f32[320]{0:T(512)S(1)}, f32[320]{0:T(512)}, u32[]{:S(2)}) copy-start(f32[320]{0:T(512)} %param.23) | copy-start | bytes 3844
  36.5 11.1 %all-to-all-start.4 = ((bf16[2,1040,128]{2,1,0:T(8,128)(2,1)}), bf16[2,1040,128]{2,1,0:T(8,128)(2,1)S(1)}, u32[]{:S(2)}, u32[]{:S(2)}) async-start(bf16[2,1040,128]{2,1,0:T(8,128)(2,1)} %pad_maximum_fusion), calls=%async_computation.4 | async-start | bytes 1064960 | tf_op jit(solution)/shard_map/all_to_all | solution.py:38
  47.5 4.8 %copy-start.5 = (bf16[2,1040,128]{2,1,0:T(8,128)(2,1)}, bf16[2,1040,128]{2,1,0:T(8,128)(2,1)S(1)}, u32[]{:S(2)}) copy-start(bf16[2,1040,128]{2,1,0:T(8,128)(2,1)S(1)} %all-to-all-done.4.kv_ref) | copy-start | bytes 1597444
  48.7 18.4 %all-to-all-start.1 = ((bf16[16,80,320]{2,1,0:T(8,128)(2,1)}), bf16[16,80,320]{2,1,0:T(8,128)(2,1)S(1)}, u32[]{:S(2)}, u32[]{:S(2)}) async-start(bf16[16,80,320]{2,1,0:T(8,128)(2,1)} %broadcast_in_dim.20), calls=%async_computation.1 | async-start | bytes 1966080 | tf_op jit(solution)/shard_map/all_to_all | solution.py:32
  68.6 33.4 %all-to-all-start.2 = ((bf16[2,16,80,320]{3,2,1,0:T(8,128)(2,1)}), bf16[2,16,80,320]{3,2,1,0:T(8,128)(2,1)S(1)}, u32[]{:S(2)}, u32[]{:S(2)}) async-start(bf16[2,16,80,320]{3,2,1,0:T(8,128)(2,1)} %broadcast_in_dim.21), calls=%async_computation.2 | async-start | bytes 3932160 | tf_op jit(solution)/shard_map/all_to_all | solution.py:32
  108.4 14.2 %copy-start.9 = (bf16[128,128]{1,0:T(8,128)(2,1)S(1)}, bf16[128,128]{1,0:T(8,128)(2,1)}, u32[]{:S(2)}) copy-start(bf16[128,128]{1,0:T(8,128)(2,1)} %get-tuple-element.15) | copy-start | bytes 98308
  108.4 51.2 %all-to-all-start.5 = ((bf16[32,320,128]{2,1,0:T(8,128)(2,1)}), bf16[32,320,128]{2,1,0:T(8,128)(2,1)S(1)}, u32[]{:S(2)}, u32[]{:S(2)}) async-start(bf16[32,320,128]{2,1,0:T(8,128)(2,1)} %shard_map.167), calls=%async_computation.5 | async-start | bytes 5242880 | tf_op jit(solution)/shard_map/all_to_all | solution.py:38
  159.6 64.6 %copy-start.1 = (bf16[32,320,128]{2,1,0:T(8,128)(2,1)}, bf16[32,320,128]{2,1,0:T(8,128)(2,1)S(1)}, u32[]{:S(2)}) copy-start(bf16[32,320,128]{2,1,0:T(8,128)(2,1)S(1)} %all-to-all-done.5.w_ref) | copy-start | bytes 7864324
  159.6 29.1 %all-to-all-start.6 = ((bf16[16,144,128]{2,1,0:T(8,128)(2,1)}), bf16[16,144,128]{2,1,0:T(8,128)(2,1)S(1)}, u32[]{:S(2)}, u32[]{:S(2)}) async-start(bf16[16,144,128]{2,1,0:T(8,128)(2,1)} %shard_map.168), calls=%async_computation.6 | async-start | bytes 1179648 | tf_op jit(solution)/shard_map/all_to_all | solution.py:38
  188.7 3.2 %copy-start.3 = (bf16[16,144,128]{2,1,0:T(8,128)(2,1)}, bf16[16,144,128]{2,1,0:T(8,128)(2,1)S(1)}, u32[]{:S(2)}) copy-start(bf16[16,144,128]{2,1,0:T(8,128)(2,1)S(1)} %all-to-all-done.6.in_ref) | copy-start | bytes 1769476
  188.7 6.2 %all-to-all-start.9 = ((bf16[2,2,16,128]{3,2,1,0:T(8,128)(2,1)}), bf16[2,2,16,128]{3,2,1,0:T(8,128)(2,1)S(1)}, u32[]{:S(2)}, u32[]{:S(2)}) async-start(bf16[2,2,16,128]{3,2,1,0:T(8,128)(2,1)} %pad_maximum_fusion.3), calls=%async_computation.9 | async-start | bytes 32768 | tf_op jit(solution)/shard_map/all_to_all | solution.py:38
  196.7 27.6 %all-to-all-start.7 = ((bf16[32,64,128]{2,1,0:T(8,128)(2,1)}), bf16[32,64,128]{2,1,0:T(8,128)(2,1)S(1)}, u32[]{:S(2)}, u32[]{:S(2)}) async-start(bf16[32,64,128]{2,1,0:T(8,128)(2,1)} %bitcast.53), calls=%async_computation.7 | async-start | bytes 1048576 | tf_op jit(solution)/shard_map/all_to_all | solution.py:38
  214.5 27.9 %copy-start.13 = (f32[320]{0:T(512)S(1)}, f32[320]{0:T(512)}, u32[]{:S(2)}) copy-start(f32[320]{0:T(512)} %param.25) | copy-start | bytes 3844
  230.0 12.3 %all-to-all-start.8 = ((f32[16,1,64]{2,1,0:T(1,128)}), f32[16,1,64]{2,1,0:T(1,128)S(1)}, u32[]{:S(2)}, u32[]{:S(2)}) async-start(f32[16,1,64]{2,1,0:T(1,128)} %broadcast_in_dim.26), calls=%async_computation.8 | async-start | bytes 16384 | tf_op jit(solution)/shard_map/all_to_all | solution.py:32
  (4 other events, 4.0 us)
Sparse Core Ops, SparseCore 0:
  18.1 81.0 all-gather.1

commit v3 on v2

--- a/solution.py
+++ b/solution.py
@@ -42,7 +42,7 @@
     return jnp.stack([matrix[:, :HD], matrix[:, HD:]])
 
 
-def project_kernel(h_ref, w_ref, q_ref, k_ref, v_ref, vt_ref, acc):
+def project_kernel(h_ref, w_ref, out_ref, acc):
     step = pl.program_id(0)
 
     @pl.when(step == 0)
@@ -60,15 +60,13 @@
 
     @pl.when(step == pl.num_programs(0) - 1)
     def _():
-        q_ref[0:64, :] = total[0:64, 0:HD].astype(BF16)
-        q_ref[64:128, :] = total[80:144, 0:HD].astype(BF16)
-        k_ref[...] = total[:, HD : 2 * HD].astype(BF16)
-        v_ref[...] = total[:, 2 * HD :].astype(BF16)
-        vt_ref[...] = total[:, 2 * HD :].T.astype(BF16)
+        out_ref[0:64, :] = total[0:64, 0:HD].astype(BF16)
+        out_ref[64:128, :] = total[80:144, 0:HD].astype(BF16)
+        out_ref[128:288, :] = total[:, HD : 2 * HD].astype(BF16)
+        out_ref[288:448, :] = total[:, 2 * HD :].astype(BF16)
 
 
 def project(features, weights):
-    shapes = ((128, HD), (160, HD), (160, HD), (HD, 160))
     return pl.pallas_call(
         project_kernel,
         grid=(4,),
@@ -76,8 +74,8 @@
             pl.BlockSpec((2, 1, 2, 2, 80, 320), lambda s: (0, s, 0, 0, 0, 0)),
             pl.BlockSpec((8, 160, 3 * HD), lambda s: (s % 2, s // 2, 0)),
         ],
-        out_specs=[pl.BlockSpec(shape, lambda s: (0, 0)) for shape in shapes],
-        out_shape=[jax.ShapeDtypeStruct(shape, BF16) for shape in shapes],
+        out_specs=pl.BlockSpec((448, HD), lambda s: (0, 0)),
+        out_shape=jax.ShapeDtypeStruct((448, HD), BF16),
         scratch_shapes=[pltpu.VMEM((160, 3 * HD), F32)],
         compiler_params=pltpu.CompilerParams(vmem_limit_bytes=VMEM_LIMIT),
         cost_estimate=pl.CostEstimate(
@@ -92,7 +90,11 @@
     return [high, middle, value - high - middle]
 
 
-def attend_kernel(q_ref, kv_ref, vt_ref, kf_ref, vft_ref, out_ref):
+def attend_kernel(q_ref, kv_ref, vt_ref, new_ref, out_ref, vft_ref):
+    @pl.when(pl.program_id(0) == 0)
+    def _():
+        vft_ref[...] = new_ref[288:448, :].astype(F32).T.astype(BF16)
+
     scale = 1.0 / math.sqrt(HD)
     queries = q_ref[...]
     lanes = queries.shape[0]
@@ -113,7 +115,7 @@
     lane = lax.broadcasted_iota(jnp.int32, (160, lanes), 1)
     token = jnp.where(token >= 80, token - 80, token)
     visible = (token >= 64) | ((token >> 4) <= ((lane & 63) >> 4))
-    parts.append(jnp.where(visible, scores(kf_ref[...]), -jnp.inf))
+    parts.append(jnp.where(visible, scores(new_ref[128:288, :]), -jnp.inf))
 
     peak = functools.reduce(
         jnp.maximum, [jnp.max(part, axis=0, keepdims=True) for part in parts]
@@ -138,7 +140,7 @@
         out_ref[block, HD : HD + 16, :] = totals[:, at]
 
 
-def attend(queries, kv, values_t, fresh_k, fresh_vt):
+def attend(queries, kv, values_t, fresh):
     step = 256
     rows = queries.shape[0]
 
@@ -152,18 +154,18 @@
             pl.BlockSpec((step, HD), lambda s: (s, 0)),
             whole(kv),
             whole(values_t),
-            whole(fresh_k),
-            whole(fresh_vt),
+            whole(fresh),
         ],
         out_specs=pl.BlockSpec((step // HD, HD + 16, HD), lambda s: (s, 0, 0)),
         out_shape=jax.ShapeDtypeStruct((rows // HD, HD + 16, HD), BF16),
+        scratch_shapes=[pltpu.VMEM((HD, 160), BF16)],
         compiler_params=pltpu.CompilerParams(vmem_limit_bytes=VMEM_LIMIT),
         cost_estimate=pl.CostEstimate(
             flops=4 * rows * 1184 * HD,
             bytes_accessed=3 * 2**20,
             transcendentals=rows * 1184,
         ),
-    )(queries, kv, values_t, fresh_k, fresh_vt)
+    )(queries, kv, values_t, fresh)
 
 
 def combine_kernel(in_ref, out_ref):
@@ -187,42 +189,48 @@
     )(parts)
 
 
-def spread_kernel(w_ref, out_ref):
-    for m in range(8):
-        block = w_ref[2 * m : 2 * m + 2].reshape(320, HD)
-        out_ref[2 * m] = block
-        out_ref[2 * m + 1] = block
-
-
-def spread(weights):
-    return pl.pallas_call(
-        spread_kernel,
-        grid=(2,),
-        in_specs=[pl.BlockSpec((16, 160, HD), lambda s: (0, s, 3))],
-        out_specs=pl.BlockSpec((16, 320, HD), lambda s: (s, 0, 0)),
-        out_shape=jax.ShapeDtypeStruct((32, 320, HD), BF16),
-        compiler_params=pltpu.CompilerParams(vmem_limit_bytes=VMEM_LIMIT),
-        cost_estimate=pl.CostEstimate(flops=0, bytes_accessed=4 * 2**20, transcendentals=0),
-    )(weights)
-
-
-def output_kernel(att_ref, w_ref, y_ref):
-    total = jnp.zeros(y_ref.shape, F32)
+def output_kernel(att_ref, w_ref, y_ref, square_ref):
+    total = jnp.zeros((320, 64), F32)
     for i in range(16):
         attention = jnp.concatenate([att_ref[2 * i], att_ref[2 * i + 1]], axis=1)
-        weights = jnp.concatenate([w_ref[2 * i], w_ref[2 * i + 1]], axis=1)
         total = total + lax.dot_general(
-            attention, weights, (((1,), (1,)), ((), ())), preferred_element_type=F32
+            w_ref[i], attention, (((1,), (1,)), ((), ())), preferred_element_type=F32
         )
-    y_ref[...] = total
+    y_ref[...] = total.T
+    squares = jnp.sum(total * total, axis=0, keepdims=True)
+    for i in range(16):
+        square_ref[i] = squares
 
 
 def output_projection(attention, weights):
     return pl.pallas_call(
         output_kernel,
-        out_shape=jax.ShapeDtypeStruct((64, 320), F32),
+        out_shape=(
+            jax.ShapeDtypeStruct((64, 320), F32),
+            jax.ShapeDtypeStruct((16, 1, 64), F32),
+        ),
         compiler_params=pltpu.CompilerParams(vmem_limit_bytes=VMEM_LIMIT),
     )(attention, weights)
+
+
+def turned(array):
+    def device(g, z):
+        return (g // 4 * 16 + z) * 4 + g % 4
+
+    pairs = [(device(g, c), device(c, g)) for g in range(16) for c in range(16)]
+    return lax.ppermute(array, ("y", "z", "xh", "core"), pairs)
+
+
+def to_owners(array):
+    def device(g, xl, z):
+        return ((g // 4 * 2 + xl) * 16 + z) * 4 + g % 4
+
+    pairs = [
+        (device(g, c // 16, c % 16), device(c // 2, c % 2, g))
+        for g in range(16)
+        for c in range(32)
+    ]
+    return lax.ppermute(array, ("y", "xl", "z", "xh", "core"), pairs)
 
 
 def local(
@@ -245,10 +253,10 @@
     flight, ch_dev, width = state.shape
     rows_count = flight * ch_dev
 
-    parts = [by_head(w) for w in (w_query, w_key, w_value)]
-    parts.append(jnp.transpose(w_out.reshape(2, HD, 160), (0, 2, 1)))
-    shard = swapped(jnp.concatenate(parts, axis=2), "xl").reshape(320, 4 * HD)
+    shard = jnp.concatenate([by_head(w) for w in (w_query, w_key, w_value)], axis=2)
+    shard = swapped(shard, "xl").reshape(320, 3 * HD)
     w_full = lax.all_gather(shard, "z", axis=0, tiled=False)
+    w_out_block = to_owners(w_out.T)
 
     current = level_lookup(levels, noise_index)
     following = level_lookup(levels, noise_index + 1)
@@ -282,31 +290,36 @@
         ],
         axis=1,
     )
-    kv = swapped(kv, "xl")
+    kv = turned(swapped(kv, "xl"))
     values_t = jnp.transpose(kv[:, 512:1024], (0, 2, 1))
 
+    w_out_block = sent_to_all(w_out_block, "xl").reshape(320, 2 * HD)
+    w_out_full = lax.all_gather(w_out_block, "z", axis=0, tiled=False)
+
     w_full, values_t = lax.optimization_barrier((w_full, values_t))
-    q, k, v, vt = project(features, w_full)
-
-    w_out_blocks = spread(w_full)
-    q, w_out_blocks = lax.optimization_barrier((q, w_out_blocks))
-    w_out_full = swapped(w_out_blocks, (*WIDE, "xl"))
-
-    queries = lax.all_gather(q, "z", axis=0, tiled=True)
-    parts = attend(queries, kv, values_t, k, vt)
-    parts, w_out_full = lax.optimization_barrier((parts, w_out_full))
-    parts = swapped(parts, "z")
-    attention = combine(parts).reshape(1, 2, rows_count, HD)
+    new = project(features, w_full)
+
+    fresh = turned(new)
+    queries = sent_to_all(fresh[:HD], WIDE).reshape(-1, HD)
+    parts = swapped(attend(queries, kv, values_t, fresh), WIDE)
+    attention = turned(combine(parts)).reshape(1, 2, rows_count, HD)
     attention = jnp.broadcast_to(attention, (16, 2, rows_count, HD))
     attention = swapped(attention.reshape(32, rows_count, HD), (*WIDE, "xl"))
 
-    finished = jnp.stack([k.reshape(2, 80, HD)[:, 64:], v.reshape(2, 80, HD)[:, 64:]], 1)
-    finished = swapped(finished, "xl")
-    new_keys = jnp.concatenate([finished[0, 0], finished[1, 0]], axis=1)
-    new_values = jnp.concatenate([finished[0, 1], finished[1, 1]], axis=1)
-
-    y = output_projection(attention, w_out_full)
-    y_squares = sent_to_all(jnp.sum(y * y, axis=1), WIDE).sum(axis=0)
+    finished = new[128:].reshape(2, 2, 80, HD)[:, :, 64:]
+    side = lax.axis_index("xl")
+    mine = jnp.where(side == 0, finished[:, 0], finished[:, 1])
+    other = jnp.where(side == 0, finished[:, 1], finished[:, 0])
+    other = lax.ppermute(other, "xl", [(0, 1), (1, 0)])
+    finished = jnp.where(
+        side == 0,
+        jnp.concatenate([mine, other], axis=2),
+        jnp.concatenate([other, mine], axis=2),
+    )
+    new_keys, new_values = finished[0], finished[1]
+
+    y, y_squares = output_projection(attention, w_out_full)
+    y_squares = swapped(y_squares, WIDE).sum(axis=(0, 1))
     velocity = y * lax.rsqrt(y_squares / D + EPSILON)[:, None] * out_gain[None, :]
     new_state = state + (following - current)[:, None, None] * velocity.reshape(
         flight, ch_dev, width

time: 252 us -> 317 us (1.26)
  starting transfers between devices: 70.9 us -> 121 us
  blocking collectives: 35.8 us -> 64.2 us
  waiting for transfers between devices: 88.1 us -> 83.3 us
    ppermute x0 -> x5, starting transfers between devices: none -> 60.7 us  [the longest x3 51.7 us: turned(): return lax.ppermute(array, ('y', 'z', 'xh', 'core'), pairs)]
    all_to_all x0 -> x2, blocking collectives: none -> 38.5 us  [sent_to_all(): lax.all_to_all(jnp.broadcast_to(array[None], (devices, *array.shape)), ax...]
    all_gather x1 -> x0, blocking collectives: 27.8 us -> none  [local(): queries = lax.all_gather(q, 'z', axis=0, tiled=True)]
    all_to_all x5 -> x3, waiting for transfers between devices: 38.8 us -> 16.1 us  [swapped(): return lax.all_to_all(blocks, axis, 0, 0, tiled=True)]
    all_to_all x5 -> x3, starting transfers between devices: 44.7 us -> 24.9 us  [swapped(): return lax.all_to_all(blocks, axis, 0, 0, tiled=True)]
    all_to_all x1 -> x2, blocking collectives: 8.06 us -> 25.8 us  [swapped(): return lax.all_to_all(blocks, axis, 0, 0, tiled=True)]
    ppermute x0 -> x5, waiting for transfers between devices: none -> 14.2 us  [the longest x3 5.55 us: turned(): return lax.ppermute(array, ('y', 'z', 'xh', 'core'), pairs)]
    all_gather x1, waiting for transfers between devices: 24 us -> 35.1 us  [local(): w_full = lax.all_gather(shard, 'z', axis=0, tiled=False)]
  transfers between devices with their start and end apart: 10 -> 13, of which waited for: 8 -> 10; matrix products, arithmetic and copies ran while one was open for 4% -> 2% of each run, Pallas kernels for 6% -> 5%
where the time goes in v3:
time: 317 us; the launch traced here: 316 us
  starting transfers between devices  121 us (38%)
  waiting for transfers between devices  83.3 us (26%)
  blocking collectives  64.2 us (20%)
  Pallas kernels  19.5 us (6%)
  between operations  14.4 us (5%)
  local copies, waits for them, and re-layouts  10.1 us (3%)
  other arithmetic  3.37 us (1%)
    ppermute x3, starting transfers between devices, turned(): return lax.ppermute(array, ('y', 'z', 'xh', 'core'), pairs)  51.7 us
    all_to_all x2, blocking collectives, sent_to_all(): lax.all_to_all(jnp.broadcast_to(array[None], (devices, *array.shape)), ax...  38.5 us
    all_to_all x3, starting transfers between devices, sent_to_all(): lax.all_to_all(jnp.broadcast_to(array[None], (devices, *array.shape)), ax...  35.4 us
    all_gather x1, waiting for transfers between devices, local(): w_full = lax.all_gather(shard, 'z', axis=0, tiled=False)  35.1 us
    all_to_all x2, blocking collectives, swapped(): return lax.all_to_all(blocks, axis, 0, 0, tiled=True)  25.8 us
    all_to_all x3, starting transfers between devices, swapped(): return lax.all_to_all(blocks, axis, 0, 0, tiled=True)  24.9 us
    all_to_all x3, waiting for transfers between devices, sent_to_all(): lax.all_to_all(jnp.broadcast_to(array[None], (devices, *array.shape)), ax...  17.9 us
    all_to_all x3, waiting for transfers between devices, swapped(): return lax.all_to_all(blocks, axis, 0, 0, tiled=True)  16.1 us
  transfers between devices with their start and end apart: 13, of which 10 were waited for; matrix products, arithmetic and copies ran while one was open for 2% of the time, Pallas kernels for 5%

profile of v3, /device:TPU:1, one launch (start us, length us, event | category | flops | bytes accessed | tf_op | source)
XLA Modules:
  0.0 316.0 jit_solution(4779627440015681347)
XLA Ops:
  9.0 7.7 %all_to_all.51 = bf16[2,160,384]{2,1,0:T(8,128)(2,1)} all-to-all(bf16[2,160,384]{2,1,0:T(8,128)(2,1)S(1)} %maximum_maximum_fusion), channel_id=1, replica_groups=mesh['y'=4,'xl'=2,'z'=16,'xh'=2,'core'=2] {'xl'}, dimensions={0} | all-to-all | bytes 491520 | tf_op jit(solution)/shard_map/all_to_all | solution.py:38
  16.8 5.7 %collective-permute-start.3 = (bf16[160,256]{1,0:T(8,128)(2,1)S(1)}, bf16[160,256]{1,0:T(8,128)(2,1)S(1)}, u32[]{:S(2)}, u32[]{:S(2)}) collective-permute-start(bf16[160,256]{1,0:T(8,128)(2,1)S(1)} %bitcast.65), channel_id=1, source_target_pairs={{0,0},{4,64},{8,1},{12,65},{16,2},{20,66},{24,3},{28,67},{32,128},... | collective-permute-start | bytes 245768 | tf_op jit(solution)/shard_map/ppermute | solution.py:233
  22.5 4.0 %collective-permute-done.3 = bf16[160,256]{1,0:T(8,128)(2,1)S(1)} collective-permute-done((bf16[160,256]{1,0:T(8,128)(2,1)S(1)}, bf16[160,256]{1,0:T(8,128)(2,1)S(1)}, u32[]{:S(2)}, u32[]{:S(2)}) %collective-permute-start.3) | collective-permute-done | bytes 81952 | tf_op jit(solution)/shard_map/ppermute | solution.py:233
  26.5 7.2 %all_to_all.52 = bf16[2,160,256]{2,1,0:T(8,128)(2,1)} all-to-all(bf16[2,160,256]{2,1,0:T(8,128)(2,1)S(1)} %broadcast_in_dim.29), channel_id=1, replica_groups=mesh['y'=4,'xl'=2,'z'=16,'xh'=2,'core'=2] {'xl'}, dimensions={0} | all-to-all | bytes 327680 | tf_op jit(solution)/shard_map/all_to_all | solution.py:32
  34.5 25.2 %all-to-all-start = ((f32[16,1,80]{2,1,0:T(1,128)}), f32[16,1,80]{2,1,0:T(1,128)S(1)}, u32[]{:S(2)}, u32[]{:S(2)}) async-start(f32[16,1,80]{2,1,0:T(1,128)} %broadcast_in_dim.20), calls=%async_computation | async-start | bytes 16384 | tf_op jit(solution)/shard_map/all_to_all | solution.py:32
  61.5 5.1 %all-to-all-done = f32[16,1,80]{2,1,0:T(1,128)S(1)} async-done(((f32[16,1,80]{2,1,0:T(1,128)}), f32[16,1,80]{2,1,0:T(1,128)S(1)}, u32[]{:S(2)}, u32[]{:S(2)}) %all-to-all-start) | async-done | bytes 5152 | tf_op jit(solution)/shard_map/all_to_all | solution.py:32
  66.6 3.5 %all-to-all-start.4 = ((bf16[2,1040,128]{2,1,0:T(8,128)(2,1)}), bf16[2,1040,128]{2,1,0:T(8,128)(2,1)S(1)}, u32[]{:S(2)}, u32[]{:S(2)}) async-start(bf16[2,1040,128]{2,1,0:T(8,128)(2,1)} %pad_maximum_fusion), calls=%async_computation.4 | async-start | bytes 1064960 | tf_op jit(solution)/shard_map/all_to_all | solution.py:38
  70.3 7.4 %all-to-all-done.4 = bf16[2,1040,128]{2,1,0:T(8,128)(2,1)S(1)} async-done(((bf16[2,1040,128]{2,1,0:T(8,128)(2,1)}), bf16[2,1040,128]{2,1,0:T(8,128)(2,1)S(1)}, u32[]{:S(2)}, u32[]{:S(2)}) %all-to-all-start.4) | async-done | bytes 532512 | tf_op jit(solution)/shard_map/all_to_all | solution.py:38
  78.7 3.6 %all-to-all-start.1 = ((bf16[16,80,320]{2,1,0:T(8,128)(2,1)}), bf16[16,80,320]{2,1,0:T(8,128)(2,1)S(1)}, u32[]{:S(2)}, u32[]{:S(2)}) async-start(bf16[16,80,320]{2,1,0:T(8,128)(2,1)} %broadcast_in_dim.22), calls=%async_computation.1 | async-start | bytes 1966080 | tf_op jit(solution)/shard_map/all_to_all | solution.py:32
  84.3 12.8 %all-to-all-done.1 = bf16[16,80,320]{2,1,0:T(8,128)(2,1)S(1)} async-done(((bf16[16,80,320]{2,1,0:T(8,128)(2,1)}), bf16[16,80,320]{2,1,0:T(8,128)(2,1)S(1)}, u32[]{:S(2)}, u32[]{:S(2)}) %all-to-all-start.1) | async-done | bytes 819232 | tf_op jit(solution)/shard_map/all_to_all | solution.py:32
  98.7 6.6 %all-to-all-start.2 = ((bf16[2,16,80,320]{3,2,1,0:T(8,128)(2,1)}), bf16[2,16,80,320]{3,2,1,0:T(8,128)(2,1)S(1)}, u32[]{:S(2)}, u32[]{:S(2)}) async-start(bf16[2,16,80,320]{3,2,1,0:T(8,128)(2,1)} %broadcast_in_dim.23), calls=%async_computation.2 | async-start | bytes 3932160 | tf_op jit(solution)/shard_map/all_to_all | solution.py:32
  106.2 35.1 %all-gather.3.cloned.1.call-done.w_ref = bf16[16,320,384]{2,1,0:T(8,128)(2,1)} async-done(((bf16[1,320,384]{2,1,0:T(8,128)(2,1)}), bf16[16,320,384]{2,1,0:T(8,128)(2,1)}) %all-gather.3.cloned.1.call-update) | async-done | bytes 3932176 | tf_op jit(solution)/shard_map/all_gather | solution.py:258
  142.6 4.9 %shard_map.166 = bf16[448,128]{1,0:T(8,128)(2,1)} custom-call(bf16[2,4,2,2,80,320]{5,4,3,2,1,0:T(8,128)(2,1)} %bitcast.54, bf16[16,320,384]{2,1,0:T(8,128)(2,1)} %all-gather.3.cloned.1.call-done.w_ref), custom_call_target="tpu_custom_call" | custom-call | flops 629145600 | bytes 6291456 | tf_op jit(solution)/shard_map/pallas_call | solution.py:70
  147.5 47.3 %collective-permute-start.1 = (bf16[448,128]{1,0:T(8,128)(2,1)}, bf16[448,128]{1,0:T(8,128)(2,1)S(1)}, u32[]{:S(2)}, u32[]{:S(2)}) collective-permute-start(bf16[448,128]{1,0:T(8,128)(2,1)} %shard_map.166), channel_id=1, source_target_pairs={{0,0},{4,1},{8,2},{12,3},{16,128},{20,129},{24,130},{28,131},{32,2... | collective-permute-start | bytes 344072 | tf_op jit(solution)/shard_map/ppermute | solution.py:221
  197.6 31.3 %all_to_all.53 = bf16[16,128,128]{2,1,0:T(8,128)(2,1)} all-to-all(bf16[16,128,128]{2,1,0:T(8,128)(2,1)S(1)} %broadcast_in_dim.26), channel_id=1, replica_groups=mesh['y'=4,'xl'=2,'z'=16,'xh'=2,'core'=2] {'y','xh','core'}, dimensions={0} | all-to-all | bytes 1048576 | tf_op jit(solution)/shard_map/all_to_all | solution.py:32
  228.9 9.2 %shard_map.167 = bf16[16,144,128]{2,1,0:T(8,128)(2,1)} custom-call(bf16[2048,128]{1,0:T(8,128)(2,1)} %bitcast.59, bf16[2,1040,128]{2,1,0:T(8,128)(2,1)} %copy-done.6, bf16[2,128,512]{2,1,0:T(8,128)(2,1)} %bitcast.61, bf16[448,128]{1,0:T(8,128)(2,1)} %copy-done.8), custom_call_target="tpu_custom_call" | custom-call | flops 1241513984 | bytes 3145728 | tf_op jit(solution)/shard_map/pallas_call | solution.py:150
  238.1 18.0 %all_to_all.54.in_ref = bf16[16,144,128]{2,1,0:T(8,128)(2,1)} all-to-all(bf16[16,144,128]{2,1,0:T(8,128)(2,1)} %shard_map.167), channel_id=1, replica_groups=mesh['y'=4,'xl'=2,'z'=16,'xh'=2,'core'=2] {'y','xh','core'}, dimensions={0} | all-to-all | bytes 1179648 | tf_op jit(solution)/shard_map/all_to_all | solution.py:38
  260.6 2.9 collective-permute-done.2
  264.4 16.1 %all-to-all-start.7 = ((bf16[32,64,128]{2,1,0:T(8,128)(2,1)}), bf16[32,64,128]{2,1,0:T(8,128)(2,1)S(1)}, u32[]{:S(2)}, u32[]{:S(2)}) async-start(bf16[32,64,128]{2,1,0:T(8,128)(2,1)} %bitcast.18), calls=%async_computation.7 | async-start | bytes 1048576 | tf_op jit(solution)/shard_map/all_to_all | solution.py:38
  280.6 3.3 %collective-permute-start.4 = (bf16[2,16,128]{2,1,0:T(8,128)(2,1)S(1)}, bf16[2,16,128]{2,1,0:T(8,128)(2,1)S(1)}, u32[]{:S(2)}, u32[]{:S(2)}) collective-permute-start(bf16[2,16,128]{2,1,0:T(8,128)(2,1)S(1)} %get-tuple-element.18), channel_id=1, source_target_pairs={{0,64},{64,0},{1,65},{65,1},{2,66},{66,2},{3,67},{67,3},{4,68},{68... | collective-permute-start | bytes 24584 | tf_op jit(solution)/shard_map/ppermute | solution.py:313
  283.9 4.7 %collective-permute-done.4 = bf16[2,16,128]{2,1,0:T(8,128)(2,1)S(1)} collective-permute-done((bf16[2,16,128]{2,1,0:T(8,128)(2,1)S(1)}, bf16[2,16,128]{2,1,0:T(8,128)(2,1)S(1)}, u32[]{:S(2)}, u32[]{:S(2)}) %collective-permute-start.4) | collective-permute-done | bytes 8224 | tf_op jit(solution)/shard_map/ppermute | solution.py:313
  291.7 3.4 %shard_map.169 = (f32[64,320]{1,0:T(8,128)}, f32[16,1,64]{2,1,0:T(1,128)}) custom-call(bf16[32,64,128]{2,1,0:T(8,128)(2,1)} %copy-done.1, bf16[16,320,256]{2,1,0:T(8,128)(2,1)} %all-gather.5.cloned.1.call-done.w_ref), custom_call_target="tpu_custom_call" | custom-call | tf_op jit(solution)/shard_map/pallas_call | solution.py:206
  295.2 5.3 %all-to-all-start.9 = ((f32[16,1,64]{2,1,0:T(1,128)}), f32[16,1,64]{2,1,0:T(1,128)S(1)}, u32[]{:S(2)}, u32[]{:S(2)}) async-start(f32[16,1,64]{2,1,0:T(1,128)} %get-tuple-element.10), calls=%async_computation.9 | async-start | bytes 16384 | tf_op jit(solution)/shard_map/all_to_all | solution.py:38
  301.1 6.4 %all-to-all-done.9 = f32[16,1,64]{2,1,0:T(1,128)S(1)} async-done(((f32[16,1,64]{2,1,0:T(1,128)}), f32[16,1,64]{2,1,0:T(1,128)S(1)}, u32[]{:S(2)}, u32[]{:S(2)}) %all-to-all-start.9) | async-done | bytes 4128 | tf_op jit(solution)/shard_map/all_to_all | solution.py:38
  (86 shorter events, 25.0 us)
Async XLA Ops:
  7.2 134.1 %all-gather.3.cloned.1.call-start = ((), (), s32[]{:S(2)}) async-start(), calls=%async_computation.10 | async-start | bytes 4177920 | tf_op jit(solution)/shard_map/all_gather | solution.py:258
  8.9 24.9 %copy-start.7 = (bf16[16,320]{1,0:T(8,128)(2,1)S(1)}, bf16[16,320]{1,0:T(8,128)(2,1)}, u32[]{:S(2)}) copy-start(bf16[16,320]{1,0:T(8,128)(2,1)} %param.16) | copy-start | bytes 30724
  8.9 24.9 %copy-start.2 = (f32[4,16,320]{2,1,0:T(8,128)S(1)}, f32[4,16,320]{2,1,0:T(8,128)}, u32[]{:S(2)}) copy-start(f32[4,16,320]{2,1,0:T(8,128)} %param.15) | copy-start | bytes 245764
  8.9 50.8 %copy-start.16 = (s32[2]{0:T(128)S(1)}, s32[2]{0:T(128)}, u32[]{:S(2)}) copy-start(s32[2]{0:T(128)} %param.28) | copy-start | bytes 28
  8.9 50.8 %copy-start.12 = (s32[4,64]{1,0:T(4,128)S(1)}, s32[4,64]{1,0:T(4,128)}, u32[]{:S(2)}) copy-start(s32[4,64]{1,0:T(4,128)} %param.29) | copy-start | bytes 3076
  8.9 51.2 %copy-start.14 = (s32[4]{0:T(128)S(1)}, s32[4]{0:T(128)}, u32[]{:S(2)}) copy-start(s32[4]{0:T(128)} %param.27) | copy-start | bytes 52
  8.9 51.2 %copy-start.4 = (bf16[512,256]{1,0:T(8,128)(2,1)S(1)}, bf16[512,256]{1,0:T(8,128)(2,1)}, u32[]{:S(2)}) copy-start(bf16[512,256]{1,0:T(8,128)(2,1)} %param.22) | copy-start | bytes 786436
  9.0 51.2 %copy-start.5 = (bf16[512,256]{1,0:T(8,128)(2,1)S(1)}, bf16[512,256]{1,0:T(8,128)(2,1)}, u32[]{:S(2)}) copy-start(bf16[512,256]{1,0:T(8,128)(2,1)} %param.21) | copy-start | bytes 786436
  16.8 271.8 %all-gather.5.cloned.1.call-start = ((), (), s32[]{:S(2)}) async-start(), calls=%async_computation.11 | async-start | bytes 2785280 | tf_op jit(solution)/shard_map/all_gather | solution.py:297
  16.8 9.7 %collective-permute-start.3 = (bf16[160,256]{1,0:T(8,128)(2,1)S(1)}, bf16[160,256]{1,0:T(8,128)(2,1)S(1)}, u32[]{:S(2)}, u32[]{:S(2)}) collective-permute-start(bf16[160,256]{1,0:T(8,128)(2,1)S(1)} %bitcast.65), channel_id=1, source_target_pairs={{0,0},{4,64},{8,1},{12,65},{16,2},{20,66},{24,3},{28,67},{32,128},... | collective-permute-start | bytes 245768 | tf_op jit(solution)/shard_map/ppermute | solution.py:233
  34.5 32.1 %all-to-all-start = ((f32[16,1,80]{2,1,0:T(1,128)}), f32[16,1,80]{2,1,0:T(1,128)S(1)}, u32[]{:S(2)}, u32[]{:S(2)}) async-start(f32[16,1,80]{2,1,0:T(1,128)} %broadcast_in_dim.20), calls=%async_computation | async-start | bytes 16384 | tf_op jit(solution)/shard_map/all_to_all | solution.py:32
  66.6 11.1 %all-to-all-start.4 = ((bf16[2,1040,128]{2,1,0:T(8,128)(2,1)}), bf16[2,1040,128]{2,1,0:T(8,128)(2,1)S(1)}, u32[]{:S(2)}, u32[]{:S(2)}) async-start(bf16[2,1040,128]{2,1,0:T(8,128)(2,1)} %pad_maximum_fusion), calls=%async_computation.4 | async-start | bytes 1064960 | tf_op jit(solution)/shard_map/all_to_all | solution.py:38
  78.7 18.4 %all-to-all-start.1 = ((bf16[16,80,320]{2,1,0:T(8,128)(2,1)}), bf16[16,80,320]{2,1,0:T(8,128)(2,1)S(1)}, u32[]{:S(2)}, u32[]{:S(2)}) async-start(bf16[16,80,320]{2,1,0:T(8,128)(2,1)} %broadcast_in_dim.22), calls=%async_computation.1 | async-start | bytes 1966080 | tf_op jit(solution)/shard_map/all_to_all | solution.py:32
  82.4 22.9 %collective-permute-start = (bf16[2,1040,128]{2,1,0:T(8,128)(2,1)S(1)}, bf16[2,1040,128]{2,1,0:T(8,128)(2,1)S(1)}, u32[]{:S(2)}, u32[]{:S(2)}) collective-permute-start(bf16[2,1040,128]{2,1,0:T(8,128)(2,1)S(1)} %all-to-all-done.4), channel_id=1, source_target_pairs={{0,0},{4,1},{8,2},{12,3},{16,128},{20,129},{24,130},{28,131},{32,2... | collective-permute-start | bytes 1597448 | tf_op jit(solution)/shard_map/ppermute | solution.py:221
  98.7 42.6 %all-to-all-start.2 = ((bf16[2,16,80,320]{3,2,1,0:T(8,128)(2,1)}), bf16[2,16,80,320]{3,2,1,0:T(8,128)(2,1)S(1)}, u32[]{:S(2)}, u32[]{:S(2)}) async-start(bf16[2,16,80,320]{3,2,1,0:T(8,128)(2,1)} %broadcast_in_dim.23), calls=%async_computation.2 | async-start | bytes 3932160 | tf_op jit(solution)/shard_map/all_to_all | solution.py:32
  105.2 42.3 %copy-start.6 = (bf16[2,1040,128]{2,1,0:T(8,128)(2,1)}, bf16[2,1040,128]{2,1,0:T(8,128)(2,1)S(1)}, u32[]{:S(2)}) copy-start(bf16[2,1040,128]{2,1,0:T(8,128)(2,1)S(1)} %collective-permute-done.kv_ref) | copy-start | bytes 1597444
  147.5 50.0 %collective-permute-start.1 = (bf16[448,128]{1,0:T(8,128)(2,1)}, bf16[448,128]{1,0:T(8,128)(2,1)S(1)}, u32[]{:S(2)}, u32[]{:S(2)}) collective-permute-start(bf16[448,128]{1,0:T(8,128)(2,1)} %shard_map.166), channel_id=1, source_target_pairs={{0,0},{4,1},{8,2},{12,3},{16,128},{20,129},{24,130},{28,131},{32,2... | collective-permute-start | bytes 344072 | tf_op jit(solution)/shard_map/ppermute | solution.py:221
  197.5 31.4 %copy-start.8 = (bf16[448,128]{1,0:T(8,128)(2,1)}, bf16[448,128]{1,0:T(8,128)(2,1)S(1)}, u32[]{:S(2)}) copy-start(bf16[448,128]{1,0:T(8,128)(2,1)S(1)} %collective-permute-done.1.new_ref) | copy-start | bytes 344068
  256.2 24.4 %copy-start.3 = (bf16[448,128]{1,0:T(8,128)(2,1)S(1)}, bf16[448,128]{1,0:T(8,128)(2,1)}, u32[]{:S(2)}) copy-start(bf16[448,128]{1,0:T(8,128)(2,1)} %shard_map.166) | copy-start | bytes 344068
  258.1 5.4 %collective-permute-start.2 = (bf16[128,128]{1,0:T(8,128)(2,1)}, bf16[128,128]{1,0:T(8,128)(2,1)S(1)}, u32[]{:S(2)}, u32[]{:S(2)}) collective-permute-start(bf16[128,128]{1,0:T(8,128)(2,1)} %shard_map.168), channel_id=1, source_target_pairs={{0,0},{4,1},{8,2},{12,3},{16,128},{20,129},{24,130},{28,131},{32,2... | collective-permute-start | bytes 98312 | tf_op jit(solution)/shard_map/ppermute | solution.py:221
  264.4 26.5 %all-to-all-start.7 = ((bf16[32,64,128]{2,1,0:T(8,128)(2,1)}), bf16[32,64,128]{2,1,0:T(8,128)(2,1)S(1)}, u32[]{:S(2)}, u32[]{:S(2)}) async-start(bf16[32,64,128]{2,1,0:T(8,128)(2,1)} %bitcast.18), calls=%async_computation.7 | async-start | bytes 1048576 | tf_op jit(solution)/shard_map/all_to_all | solution.py:38
  280.6 8.0 %collective-permute-start.4 = (bf16[2,16,128]{2,1,0:T(8,128)(2,1)S(1)}, bf16[2,16,128]{2,1,0:T(8,128)(2,1)S(1)}, u32[]{:S(2)}, u32[]{:S(2)}) collective-permute-start(bf16[2,16,128]{2,1,0:T(8,128)(2,1)S(1)} %get-tuple-element.18), channel_id=1, source_target_pairs={{0,64},{64,0},{1,65},{65,1},{2,66},{66,2},{3,67},{67,3},{4,68},{68... | collective-permute-start | bytes 24584 | tf_op jit(solution)/shard_map/ppermute | solution.py:313
  288.6 18.9 %copy-start.11 = (f32[320]{0:T(512)S(1)}, f32[320]{0:T(512)}, u32[]{:S(2)}) copy-start(f32[320]{0:T(512)} %param.25) | copy-start | bytes 3844
  295.2 12.3 %all-to-all-start.9 = ((f32[16,1,64]{2,1,0:T(1,128)}), f32[16,1,64]{2,1,0:T(1,128)S(1)}, u32[]{:S(2)}, u32[]{:S(2)}) async-start(f32[16,1,64]{2,1,0:T(1,128)} %get-tuple-element.10), calls=%async_computation.9 | async-start | bytes 16384 | tf_op jit(solution)/shard_map/all_to_all | solution.py:38
  (6 other events, 32.4 us)
Sparse Core Ops, SparseCore 0:
  16.9 124.3 all-gather.2
  143.3 103.5 all-gather.4

commit v4 on v3

v4 whole, which is shorter than its diff:
```python
import functools
import math

import jax
import jax.numpy as jnp
from jax import lax
from jax.experimental import pallas as pl
from jax.experimental.pallas import tpu as pltpu
from jax.sharding import Mesh
from jax.sharding import PartitionSpec as P

D = 5120
HD = 128
SLOT = 256
EPSILON = 1e-06
VMEM_LIMIT = 56 * 1024 * 1024

CTX = ("xl", "z")
WIDE = ("y", "xh", "core")
BF16 = jnp.bfloat16
F32 = jnp.float32


def level_lookup(levels, indices):
    table = jnp.arange(levels.shape[0], dtype=jnp.int32)
    picked = (indices[:, None] == table[None, :]).astype(F32)
    return jnp.sum(picked * levels[None, :], axis=1)


def sent_to_all(array, axis):
    devices = lax.axis_size(axis)
    return lax.all_to_all(
        jnp.broadcast_to(array[None], (devices, *array.shape)), axis, 0, 0, tiled=True
    )


def swapped(blocks, axis):
    return lax.all_to_all(blocks, axis, 0, 0, tiled=True)


def by_head(matrix):
    return jnp.stack([matrix[:, :HD], matrix[:, HD:]])


def project_kernel(h_ref, w_ref, out_ref, acc):
    step = pl.program_id(0)

    @pl.when(step == 0)
    def _():
        acc[...] = jnp.zeros_like(acc)

    total = acc[...]
    width = acc.shape[1]
    for xh in range(2):
        for core in range(2):
            rows = h_ref[core, 0, xh].reshape(160, 320)
            at = 2 * (2 * xh + core)
            weights = w_ref[at : at + 2].reshape(320, width)
            total = total + jnp.dot(rows, weights, preferred_element_type=F32)
    acc[...] = total

    @pl.when(step == pl.num_programs(0) - 1)
    def _():
        if width == HD:
            for xl in range(2):
                rows = total[80 * xl : 80 * xl + 64].astype(BF16)
                for i in range(8):
                    out_ref[2 * i + xl] = rows
        else:
            out_ref[0:160, :] = total[:, 0:HD].astype(BF16)
            out_ref[160:320, :] = total[:, HD:].astype(BF16)


def project(features, weights, block, width, shape):
    return pl.pallas_call(
        project_kernel,
        grid=(4,),
        in_specs=[
            pl.BlockSpec((2, 1, 2, 2, 80, 320), lambda s: (0, s, 0, 0, 0, 0)),
            pl.BlockSpec((8, 160, width), lambda s: (s % 2, s // 2, block)),
        ],
        out_specs=pl.BlockSpec(shape, lambda s: (0,) * len(shape)),
        out_shape=jax.ShapeDtypeStruct(shape, BF16),
        scratch_shapes=[pltpu.VMEM((160, width), F32)],
        compiler_params=pltpu.CompilerParams(vmem_limit_bytes=VMEM_LIMIT),
        cost_estimate=pl.CostEstimate(
            flops=2 * 160 * D * width, bytes_accessed=4 * 2**20, transcendentals=0
        ),
    )(features, weights)


def in_three(value):
    high = value.astype(BF16).astype(F32)
    middle = (value - high).astype(BF16).astype(F32)
    return [high, middle, value - high - middle]


def attend_kernel(q_ref, own_ref, other_ref, own_vt_ref, other_vt_ref, own_new, other_new, out_ref, fresh_vt):
    @pl.when(pl.program_id(0) == 0)
    def _():
        for i, new in enumerate((own_new, other_new)):
            fresh_vt[i] = new[160:320, :].astype(F32).T.astype(BF16)

    scale = 1.0 / math.sqrt(HD)
    queries = q_ref[...]
    lanes = queries.shape[0]
    across = (((1,), (1,)), ((), ()))

    def scores(keys):
        return lax.dot_general(keys, queries, across, preferred_element_type=F32) * scale

    token = lax.broadcasted_iota(jnp.int32, (160, lanes), 0)
    lane = lax.broadcasted_iota(jnp.int32, (160, lanes), 1)
    token = jnp.where(token >= 80, token - 80, token)
    visible = (token >= 64) | ((token >> 4) <= ((lane & 63) >> 4))

    parts, values = [], []
    for i, (kv_ref, vt_ref, new) in enumerate(
        ((own_ref, own_vt_ref, own_new), (other_ref, other_vt_ref, other_new))
    ):
        for side in range(2):
            seen = kv_ref[side, 1024:1040, :].astype(F32)
            hidden = jnp.where(seen > 0.5, 0.0, -jnp.inf)
            hidden = jnp.concatenate([hidden] * (lanes // HD), axis=1)
            for slot in range(2):
                at = slice(slot * SLOT, (slot + 1) * SLOT)
                parts.append(scores(kv_ref[side, at, :]) + hidden[slot : slot + 1, :])
                values.append(vt_ref[side, :, at])
        parts.append(jnp.where(visible, scores(new[0:160, :]), -jnp.inf))
        values.append(fresh_vt[i])

    peak = functools.reduce(
        jnp.maximum, [jnp.max(part, axis=0, keepdims=True) for part in parts]
    )
    numer = jnp.zeros((HD, lanes), F32)
    denom = jnp.zeros((1, lanes), F32)
    for part, value in zip(parts, values):
        weights = jnp.exp(part - peak).astype(BF16)
        denom = denom + jnp.sum(weights.astype(F32), axis=0, keepdims=True)
        numer = numer + jnp.dot(value, weights, preferred_element_type=F32)
    mean = (numer / denom).T.astype(BF16)
    totals = jnp.concatenate(
        [*in_three(peak), *in_three(denom), jnp.zeros((10, lanes), F32)], axis=0
    )
    for block in range(lanes // 64):
        at = slice(block * 64, (block + 1) * 64)
        out_ref[block, 0:64, :] = mean[at, :]
        out_ref[block, 64:80, :] = jnp.concatenate(
            [totals[:, at], totals[:, at]], axis=1
        ).astype(BF16)


def attend(queries, kv, values_t, fresh):
    step = 256
    rows = queries.shape[0]
    arrays = (*kv, *values_t, *fresh)

    def whole(array):
        return pl.BlockSpec(array.shape, lambda s: (0,) * array.ndim)

    return pl.pallas_call(
        attend_kernel,
        grid=(rows // step,),
        in_specs=[
            pl.BlockSpec((step, HD), lambda s: (s, 0)),
            *[whole(array) for array in arrays],
        ],
        out_specs=pl.BlockSpec((step // 64, 80, HD), lambda s: (s, 0, 0)),
        out_shape=jax.ShapeDtypeStruct((rows // 64, 80, HD), BF16),
        scratch_shapes=[pltpu.VMEM((2, HD, 160), BF16)],
        compiler_params=pltpu.CompilerParams(vmem_limit_bytes=VMEM_LIMIT),
        cost_estimate=pl.CostEstimate(
            flops=4 * rows * 2368 * HD,
            bytes_accessed=3 * 2**20,
            transcendentals=rows * 2368,
        ),
    )(queries, *arrays)


def combine_kernel(in_ref, out_ref):
    count = in_ref.shape[0]
    totals = in_ref[:, 64:80, :].astype(F32)
    peak = totals[:, 0, :] + totals[:, 1, :] + totals[:, 2, :]
    denom = totals[:, 3, :] + totals[:, 4, :] + totals[:, 5, :]
    even = lax.broadcasted_iota(jnp.int32, peak.shape, 0) % 2 == 0
    low = jnp.max(jnp.where(even, peak, -jnp.inf), axis=0, keepdims=True)
    high = jnp.max(jnp.where(even, -jnp.inf, peak), axis=0, keepdims=True)
    share = denom * jnp.exp(peak - jnp.where(even, low, high))
    low = jnp.sum(jnp.where(even, share, 0.0), axis=0, keepdims=True)
    high = jnp.sum(jnp.where(even, 0.0, share), axis=0, keepdims=True)
    share = (share / jnp.where(even, low, high)).T
    for xl in range(2):
        mixed = jnp.zeros((64, HD), F32)
        for i in range(xl, count, 2):
            mixed = mixed + in_ref[i, 0:64, :].astype(F32) * share[0:64, i : i + 1]
        mixed = mixed.astype(BF16)
        for i in range(16):
            out_ref[2 * i + xl] = mixed


def combine(parts):
    return pl.pallas_call(
        combine_kernel,
        out_shape=jax.ShapeDtypeStruct((32, 64, HD), BF16),
        compiler_params=pltpu.CompilerParams(vmem_limit_bytes=VMEM_LIMIT),
    )(parts)


def output_kernel(side_ref, att_ref, own_ref, other_ref, y_ref, square_ref):
    side = side_ref[0]
    total = jnp.zeros((320, 64), F32)
    for i in range(16):
        attention = jnp.concatenate(
            [att_ref[2 * i + side], att_ref[2 * i + 1 - side]], axis=1
        )
        weights = jnp.concatenate([own_ref[i], other_ref[i]], axis=1)
        total = total + lax.dot_general(
            weights, attention, (((1,), (1,)), ((), ())), preferred_element_type=F32
        )
    y_ref[...] = total.T
    squares = jnp.sum(total * total, axis=0, keepdims=True)
    for i in range(16):
        square_ref[i] = squares


def output_projection(side, attention, own, other):
    return pl.pallas_call(
        output_kernel,
        in_specs=[
            pl.BlockSpec(memory_space=pltpu.SMEM),
            *[pl.BlockSpec(memory_space=pltpu.VMEM)] * 3,
        ],
        out_shape=(
            jax.ShapeDtypeStruct((64, 320), F32),
            jax.ShapeDtypeStruct((16, 1, 64), F32),
        ),
        compiler_params=pltpu.CompilerParams(vmem_limit_bytes=VMEM_LIMIT),
    )(side, attention, own, other)


def to_owners(array, same):
    def device(g, xl, z):
        return ((g // 4 * 2 + xl) * 16 + z) * 4 + g % 4

    pairs = [
        (device(g, c // 16, c % 16), device(c // 2, c % 2 if same else 1 - c % 2, g))
        for g in range(16)
        for c in range(32)
    ]
    return lax.ppermute(array, ("y", "xl", "z", "xh", "core"), pairs)


def from_neighbour(array):
    return lax.ppermute(array, "z", [(z, z ^ 1) for z in range(16)])


def local(
    state,
    clean_tokens,
    w_query,
    w_key,
    w_value,
    w_out,
    cache_keys,
    cache_values,
    norm_gain,
    mod_gain,
    out_gain,
    levels,
    noise_index,
    placement,
    group_mask,
):
    flight, ch_dev, width = state.shape
    rows_count = flight * ch_dev

    side = lax.axis_index("xl")
    odd = lax.axis_index("z") % 2
    w_out_t = jnp.transpose(w_out)
    low, high = w_out_t[:, :HD], w_out_t[:, HD:]
    first = to_owners(jnp.where(odd == 0, low, high), True)
    second = to_owners(jnp.where(odd == 0, high, low), False)
    w_heads = jnp.concatenate([by_head(w) for w in (w_key, w_value, w_query)], axis=2)
    w_heads = swapped(w_heads, "xl").reshape(320, 3 * HD)
    w_columns = jnp.where(
        side == 0,
        jnp.concatenate([first, second], axis=0),
        jnp.concatenate([second, first], axis=0),
    )
    shard = jnp.concatenate([w_heads, w_columns], axis=1)
    w_full = lax.all_gather(shard, "z", axis=0, tiled=False)

    current = level_lookup(levels, noise_index)
    following = level_lookup(levels, noise_index + 1)
    rows = jnp.concatenate(
        [state.reshape(rows_count, width), clean_tokens.astype(F32)], axis=0
    )
    sigma_rows = jnp.concatenate(
        [jnp.repeat(current, ch_dev), jnp.zeros((ch_dev,), F32)]
    )
    squares = sent_to_all(jnp.sum(rows * rows, axis=1), WIDE).sum(axis=0)
    inverse = lax.rsqrt(squares / D + EPSILON)
    features = (
        rows
        * inverse[:, None]
        * norm_gain[None, :]
        * (1.0 + sigma_rows[:, None] * mod_gain[None, :])
    ).astype(BF16)
    features = sent_to_all(features, ("y", "xh", "xl"))
    features = sent_to_all(features, "core").reshape(2, 4, 2, 2, 80, width)

    table = jnp.arange(group_mask.shape[1], dtype=jnp.int32)
    held = (placement[:, None] == table[None, :]).astype(jnp.int32)
    seen = jnp.sum(held[None, :, :] * group_mask[:, None, :], axis=2) != 0
    seen = jnp.repeat(seen.T.astype(BF16), ch_dev, axis=1)
    seen = jnp.pad(jnp.concatenate([seen, seen], axis=1), ((0, 14), (0, 0)))
    kv = jnp.concatenate(
        [
            by_head(cache_keys),
            by_head(cache_values),
            jnp.broadcast_to(seen[None], (2, *seen.shape)),
        ],
        axis=1,
    )
    kv = swapped(kv, "xl")
    kv = (kv, from_neighbour(kv))
    values_t = [jnp.transpose(part[:, 512:1024], (0, 2, 1)) for part in kv]

    w_full, values_t = lax.optimization_barrier((w_full, values_t))
    queries = project(features, w_full, 2, HD, (16, 64, HD))
    queries = swapped(queries, "z").reshape(-1, HD)
    new = project(features, w_full, 0, 2 * HD, (320, HD))
    fresh = (new, from_neighbour(new))
    w_out_own = w_full[:, :, 3 * HD :]
    w_out_other = lax.ppermute(w_out_own, "xl", [(0, 1), (1, 0)])
    parts = attend(queries, kv, values_t, fresh)
    parts = swapped(parts, "z")
    attention = swapped(combine(parts), (*WIDE, "xl"))

    finished = new.reshape(2, 2, 80, HD)[:, :, 64:]
    mine = jnp.where(side == 0, finished[:, 0], finished[:, 1])
    other = jnp.where(side == 0, finished[:, 1], finished[:, 0])
    other = lax.ppermute(other, "xl", [(0, 1), (1, 0)])
    finished = jnp.where(
        side == 0,
        jnp.concatenate([mine, other], axis=2),
        jnp.concatenate([other, mine], axis=2),
    )
    new_keys, new_values = finished[0], finished[1]

    y, y_squares = output_projection(side.reshape(1), attention, w_out_own, w_out_other)
    y_squares = swapped(y_squares, WIDE).sum(axis=(0, 1))
    velocity = y * lax.rsqrt(y_squares / D + EPSILON)[:, None] * out_gain[None, :]
    new_state = state + (following - current)[:, None, None] * velocity.reshape(
        flight, ch_dev, width
    )
    return new_state, new_keys, new_values


def solution(mesh):
    fine = Mesh(mesh.devices.reshape(4, 2, 16, 2, 2), ("y", "xl", "z", "xh", "core"))
    in_specs = (
        P(None, CTX, WIDE),
        P(CTX, WIDE),
        P(CTX, WIDE),
        P(CTX, WIDE),
        P(CTX, WIDE),
        P(WIDE, CTX),
        P(CTX, WIDE),
        P(CTX, WIDE),
        P(WIDE),
        P(WIDE),
        P(WIDE),
        P(),
        P(),
        P(CTX),
        P(),
    )
    out_specs = (P(None, CTX, WIDE), P(CTX, WIDE), P(CTX, WIDE))
    return jax.shard_map(local, mesh=fine, in_specs=in_specs, out_specs=out_specs, check_vma=False)
```

time: 317 us -> 241 us (0.76)
  blocking collectives: 64.2 us -> 0 us
  starting transfers between devices: 121 us -> 99.3 us
  Pallas kernels: 19.5 us -> 23.5 us
    all_to_all x4 -> x0, blocking collectives: 64.2 us -> none  [the longest x2 38.5 us: sent_to_all(): lax.all_to_all(jnp.broadcast_to(array[None], (devices, *array.shape)), ax...]
    ppermute x3, starting transfers between devices: 51.7 us -> 9.54 us  [the longest x2 6.48 us: from_neighbour(): return lax.ppermute(array, 'z', [(z, z ^ 1) for z in range(16)])]
    all_to_all x3 -> x6, starting transfers between devices: 24.9 us -> 55.9 us  [swapped(): return lax.all_to_all(blocks, axis, 0, 0, tiled=True)]
    all_to_all x3, starting transfers between devices: 35.4 us -> 18.2 us  [sent_to_all(): lax.all_to_all(jnp.broadcast_to(array[None], (devices, *array.shape)), ax...]
    all_to_all x3 -> x6, waiting for transfers between devices: 16.1 us -> 29.1 us  [swapped(): return lax.all_to_all(blocks, axis, 0, 0, tiled=True)]
    all_gather x1, waiting for transfers between devices: 35.1 us -> 24 us  [local(): w_full = lax.all_gather(shard, 'z', axis=0, tiled=False)]
    ppermute x1 -> x2, starting transfers between devices: 5.69 us -> 12.3 us  [to_owners(): return lax.ppermute(array, ('y', 'xl', 'z', 'xh', 'core'), pairs)]
    ppermute x3, waiting for transfers between devices: 5.55 us -> 9.9 us  [the longest x2 9.89 us: from_neighbour(): return lax.ppermute(array, 'z', [(z, z ^ 1) for z in range(16)])]
  transfers between devices with their start and end apart: 13 -> 16, of which waited for: 10 -> 11; matrix products, arithmetic and copies ran while one was open for 2% -> 5% of each run, Pallas kernels for 5% -> 3%
where the time goes in v4:
time: 241 us; the launch traced here: 239 us
  starting transfers between devices  99.3 us (41%)
  waiting for transfers between devices  82.7 us (34%)
  Pallas kernels  23.5 us (10%)
  between operations  14.4 us (6%)
  local copies, waits for them, and re-layouts  12.8 us (5%)
  other arithmetic  6.41 us (3%)
    all_to_all x6, starting transfers between devices, swapped(): return lax.all_to_all(blocks, axis, 0, 0, tiled=True)  55.9 us
    all_to_all x6, waiting for transfers between devices, swapped(): return lax.all_to_all(blocks, axis, 0, 0, tiled=True)  29.1 us
    all_gather x1, waiting for transfers between devices, local(): w_full = lax.all_gather(shard, 'z', axis=0, tiled=False)  24 us
    all_to_all x3, starting transfers between devices, sent_to_all(): lax.all_to_all(jnp.broadcast_to(array[None], (devices, *array.shape)), ax...  18.2 us
    all_to_all x3, waiting for transfers between devices, sent_to_all(): lax.all_to_all(jnp.broadcast_to(array[None], (devices, *array.shape)), ax...  15.7 us
    ppermute x2, starting transfers between devices, to_owners(): return lax.ppermute(array, ('y', 'xl', 'z', 'xh', 'core'), pairs)  12.3 us
    ppermute x2, waiting for transfers between devices, from_neighbour(): return lax.ppermute(array, 'z', [(z, z ^ 1) for z in range(16)])  9.89 us
    pallas_call x1, Pallas kernels, attend(): pl.pallas_call(attend_kernel, grid=(rows // step,), in_specs=[pl.BlockSpe...  9.63 us
  transfers between devices with their start and end apart: 16, of which 11 were waited for; matrix products, arithmetic and copies ran while one was open for 5% of the time, Pallas kernels for 3%

profile of v4, /device:TPU:1, one launch (start us, length us, event | category | flops | bytes accessed | tf_op | source)
XLA Modules:
  0.0 239.1 jit_solution(4961626868809336025)
XLA Ops:
  8.0 5.9 %collective-permute-start.1 = (bf16[160,128]{1,0:T(8,128)(2,1)S(1)}, bf16[160,128]{1,0:T(8,128)(2,1)S(1)}, u32[]{:S(2)}, u32[]{:S(2)}) collective-permute-start(bf16[160,128]{1,0:T(8,128)(2,1)S(1)} %get-tuple-element.28), channel_id=1, source_target_pairs={{0,64},{4,0},{8,65},{12,1},{16,66},{20,2},{24,67},{28,3},{32,192},... | collective-permute-start | bytes 122888 | tf_op jit(solution)/shard_map/ppermute | solution.py:250
  13.9 6.5 %collective-permute-start = (bf16[160,128]{1,0:T(8,128)(2,1)S(1)}, bf16[160,128]{1,0:T(8,128)(2,1)S(1)}, u32[]{:S(2)}, u32[]{:S(2)}) collective-permute-start(bf16[160,128]{1,0:T(8,128)(2,1)S(1)} %get-tuple-element.27), channel_id=1, source_target_pairs={{0,0},{4,64},{8,1},{12,65},{16,2},{20,66},{24,3},{28,67},{32,128},... | collective-permute-start | bytes 122888 | tf_op jit(solution)/shard_map/ppermute | solution.py:250
  22.8 11.8 %all-to-all-start.3 = ((bf16[2,160,384]{2,1,0:T(8,128)(2,1)}), bf16[2,160,384]{2,1,0:T(8,128)(2,1)S(1)}, u32[]{:S(2)}, u32[]{:S(2)}) async-start(bf16[2,160,384]{2,1,0:T(8,128)(2,1)} %maximum_maximum_fusion), calls=%async_computation.3 | async-start | bytes 491520 | tf_op jit(solution)/shard_map/all_to_all | solution.py:38
  34.7 4.6 %all-to-all-done.3 = bf16[2,160,384]{2,1,0:T(8,128)(2,1)S(1)} async-done(((bf16[2,160,384]{2,1,0:T(8,128)(2,1)}), bf16[2,160,384]{2,1,0:T(8,128)(2,1)S(1)}, u32[]{:S(2)}, u32[]{:S(2)}) %all-to-all-start.3) | async-done | bytes 245792 | tf_op jit(solution)/shard_map/all_to_all | solution.py:38
  40.9 8.0 %all-to-all-start = ((f32[16,1,80]{2,1,0:T(1,128)}), f32[16,1,80]{2,1,0:T(1,128)S(1)}, u32[]{:S(2)}, u32[]{:S(2)}) async-start(f32[16,1,80]{2,1,0:T(1,128)} %broadcast_in_dim.12), calls=%async_computation | async-start | bytes 16384 | tf_op jit(solution)/shard_map/all_to_all | solution.py:32
  50.7 5.0 %all-to-all-done = f32[16,1,80]{2,1,0:T(1,128)S(1)} async-done(((f32[16,1,80]{2,1,0:T(1,128)}), f32[16,1,80]{2,1,0:T(1,128)S(1)}, u32[]{:S(2)}, u32[]{:S(2)}) %all-to-all-start) | async-done | bytes 5152 | tf_op jit(solution)/shard_map/all_to_all | solution.py:32
  55.7 3.5 %all-to-all-start.4 = ((bf16[2,1040,128]{2,1,0:T(8,128)(2,1)}), bf16[2,1040,128]{2,1,0:T(8,128)(2,1)S(1)}, u32[]{:S(2)}, u32[]{:S(2)}) async-start(bf16[2,1040,128]{2,1,0:T(8,128)(2,1)} %pad_maximum_fusion), calls=%async_computation.4 | async-start | bytes 1064960 | tf_op jit(solution)/shard_map/all_to_all | solution.py:38
  59.4 7.4 %all-to-all-done.4.own_ref = bf16[2,1040,128]{2,1,0:T(8,128)(2,1)S(1)} async-done(((bf16[2,1040,128]{2,1,0:T(8,128)(2,1)}), bf16[2,1040,128]{2,1,0:T(8,128)(2,1)S(1)}, u32[]{:S(2)}, u32[]{:S(2)}) %all-to-all-start.4) | async-done | bytes 532512 | tf_op jit(solution)/shard_map/all_to_all | solution.py:38
  68.0 3.6 %all-to-all-start.1 = ((bf16[16,80,320]{2,1,0:T(8,128)(2,1)}), bf16[16,80,320]{2,1,0:T(8,128)(2,1)S(1)}, u32[]{:S(2)}, u32[]{:S(2)}) async-start(bf16[16,80,320]{2,1,0:T(8,128)(2,1)} %broadcast_in_dim.14), calls=%async_computation.1 | async-start | bytes 1966080 | tf_op jit(solution)/shard_map/all_to_all | solution.py:32
  75.8 10.6 %all-to-all-done.1 = bf16[16,80,320]{2,1,0:T(8,128)(2,1)S(1)} async-done(((bf16[16,80,320]{2,1,0:T(8,128)(2,1)}), bf16[16,80,320]{2,1,0:T(8,128)(2,1)S(1)}, u32[]{:S(2)}, u32[]{:S(2)}) %all-to-all-start.1) | async-done | bytes 819232 | tf_op jit(solution)/shard_map/all_to_all | solution.py:32
  87.9 6.6 %all-to-all-start.2 = ((bf16[2,16,80,320]{3,2,1,0:T(8,128)(2,1)}), bf16[2,16,80,320]{3,2,1,0:T(8,128)(2,1)S(1)}, u32[]{:S(2)}, u32[]{:S(2)}) async-start(bf16[2,16,80,320]{3,2,1,0:T(8,128)(2,1)} %broadcast_in_dim.15), calls=%async_computation.2 | async-start | bytes 3932160 | tf_op jit(solution)/shard_map/all_to_all | solution.py:32
  94.4 3.9 %collective-permute-done.2.other_ref = bf16[2,1040,128]{2,1,0:T(8,128)(2,1)S(1)} collective-permute-done((bf16[2,1040,128]{2,1,0:T(8,128)(2,1)S(1)}, bf16[2,1040,128]{2,1,0:T(8,128)(2,1)S(1)}, u32[]{:S(2)}, u32[]{:S(2)}) %collective-permute-start.2) | collective-permute-done | bytes 532512 | tf_op jit(solution)/shard_map/ppermute | solution.py:254
  99.2 24.0 %all-gather.3.cloned.1.call-done = bf16[5120,512]{1,0:T(8,128)(2,1)} async-done(((bf16[320,512]{1,0:T(8,128)(2,1)}), bf16[5120,512]{1,0:T(8,128)(2,1)}) %all-gather.3.cloned.1.call-update) | async-done | bytes 5242896 | tf_op jit(solution)/shard_map/all_gather | solution.py:291
  124.5 4.0 %shard_map.166 = bf16[16,64,128]{2,1,0:T(8,128)(2,1)} custom-call(bf16[2,4,2,2,80,320]{5,4,3,2,1,0:T(8,128)(2,1)} %bitcast.57, bf16[16,320,512]{2,1,0:T(8,128)(2,1)} %bitcast.54), custom_call_target="tpu_custom_call" | custom-call | flops 209715200 | bytes 4194304 | tf_op jit(solution)/shard_map/pallas_call | solution.py:75
  128.5 7.1 %all-to-all-start.5 = ((bf16[16,64,128]{2,1,0:T(8,128)(2,1)}), bf16[16,64,128]{2,1,0:T(8,128)(2,1)S(1)}, u32[]{:S(2)}, u32[]{:S(2)}) async-start(bf16[16,64,128]{2,1,0:T(8,128)(2,1)} %shard_map.166), calls=%async_computation.5 | async-start | bytes 524288 | tf_op jit(solution)/shard_map/all_to_all | solution.py:38
  135.6 4.3 %shard_map.167.own_new = bf16[320,128]{1,0:T(8,128)(2,1)} custom-call(bf16[2,4,2,2,80,320]{5,4,3,2,1,0:T(8,128)(2,1)} %bitcast.58, bf16[16,320,512]{2,1,0:T(8,128)(2,1)} %bitcast.55), custom_call_target="tpu_custom_call" | custom-call | flops 419430400 | bytes 4194304 | tf_op jit(solution)/shard_map/pallas_call | solution.py:75
  143.2 6.0 %collective-permute-done.3.other_new = bf16[320,128]{1,0:T(8,128)(2,1)S(1)} collective-permute-done((bf16[320,128]{1,0:T(8,128)(2,1)}, bf16[320,128]{1,0:T(8,128)(2,1)S(1)}, u32[]{:S(2)}, u32[]{:S(2)}) %collective-permute-start.3) | collective-permute-done | bytes 81952 | tf_op jit(solution)/shard_map/ppermute | solution.py:254
  150.0 9.6 %shard_map.168 = bf16[16,80,128]{2,1,0:T(8,128)(2,1)} custom-call(bf16[1024,128]{1,0:T(8,128)(2,1)} %bitcast.65, bf16[2,1040,128]{2,1,0:T(8,128)(2,1)} %copy-done.5, bf16[2,1040,128]{2,1,0:T(8,128)(2,1)} %copy-done.10, bf16[2,128,512]{2,1,0:T(8,128)(2,1)} %bitcast.63, bf16[2,128,512]{2,1,0:T(8,128)(2,1)} %bitcast.64, bf16[320,128]{1,0:T(8,128)(2,1)} %shard_map.167.own_new, ...), custom_call_target="tpu_custom_call" | custom-call | flops 1241513984 | bytes 3145728 | tf_op jit(solution)/shard_map/pallas_call | solution.py:161
  159.6 12.1 %all-to-all-start.6 = ((bf16[16,80,128]{2,1,0:T(8,128)(2,1)}), bf16[16,80,128]{2,1,0:T(8,128)(2,1)S(1)}, u32[]{:S(2)}, u32[]{:S(2)}) async-start(bf16[16,80,128]{2,1,0:T(8,128)(2,1)} %shard_map.168), calls=%async_computation.6 | async-start | bytes 655360 | tf_op jit(solution)/shard_map/all_to_all | solution.py:38
  176.2 9.0 %all-to-all-done.6.in_ref = bf16[16,80,128]{2,1,0:T(8,128)(2,1)S(1)} async-done(((bf16[16,80,128]{2,1,0:T(8,128)(2,1)}), bf16[16,80,128]{2,1,0:T(8,128)(2,1)S(1)}, u32[]{:S(2)}, u32[]{:S(2)}) %all-to-all-start.6) | async-done | bytes 327712 | tf_op jit(solution)/shard_map/all_to_all | solution.py:38
  188.1 15.1 %all-to-all-start.7 = ((bf16[32,64,128]{2,1,0:T(8,128)(2,1)}), bf16[32,64,128]{2,1,0:T(8,128)(2,1)S(1)}, u32[]{:S(2)}, u32[]{:S(2)}) async-start(bf16[32,64,128]{2,1,0:T(8,128)(2,1)} %shard_map.169), calls=%async_computation.7 | async-start | bytes 1048576 | tf_op jit(solution)/shard_map/all_to_all | solution.py:38
  207.2 4.0 %collective-permute-done.5 = bf16[2,16,128]{2,1,0:T(8,128)(2,1)S(1)} collective-permute-done((bf16[2,16,128]{2,1,0:T(8,128)(2,1)S(1)}, bf16[2,16,128]{2,1,0:T(8,128)(2,1)S(1)}, u32[]{:S(2)}, u32[]{:S(2)}) %collective-permute-start.5) | collective-permute-done | bytes 8224 | tf_op jit(solution)/shard_map/ppermute | solution.py:343
  217.2 6.4 %all-to-all-start.8 = ((f32[16,1,64]{2,1,0:T(1,128)}), f32[16,1,64]{2,1,0:T(1,128)S(1)}, u32[]{:S(2)}, u32[]{:S(2)}) async-start(f32[16,1,64]{2,1,0:T(1,128)} %get-tuple-element.12), calls=%async_computation.8 | async-start | bytes 16384 | tf_op jit(solution)/shard_map/all_to_all | solution.py:38
  224.1 6.4 %all-to-all-done.8 = f32[16,1,64]{2,1,0:T(1,128)S(1)} async-done(((f32[16,1,64]{2,1,0:T(1,128)}), f32[16,1,64]{2,1,0:T(1,128)S(1)}, u32[]{:S(2)}, u32[]{:S(2)}) %all-to-all-start.8) | async-done | bytes 4128 | tf_op jit(solution)/shard_map/all_to_all | solution.py:38
  (95 shorter events, 39.4 us)
Async XLA Ops:
  8.0 26.6 %collective-permute-start.1 = (bf16[160,128]{1,0:T(8,128)(2,1)S(1)}, bf16[160,128]{1,0:T(8,128)(2,1)S(1)}, u32[]{:S(2)}, u32[]{:S(2)}) collective-permute-start(bf16[160,128]{1,0:T(8,128)(2,1)S(1)} %get-tuple-element.28), channel_id=1, source_target_pairs={{0,64},{4,0},{8,65},{12,1},{16,66},{20,2},{24,67},{28,3},{32,192},... | collective-permute-start | bytes 122888 | tf_op jit(solution)/shard_map/ppermute | solution.py:250
  13.9 20.8 %collective-permute-start = (bf16[160,128]{1,0:T(8,128)(2,1)S(1)}, bf16[160,128]{1,0:T(8,128)(2,1)S(1)}, u32[]{:S(2)}, u32[]{:S(2)}) collective-permute-start(bf16[160,128]{1,0:T(8,128)(2,1)S(1)} %get-tuple-element.27), channel_id=1, source_target_pairs={{0,0},{4,64},{8,1},{12,65},{16,2},{20,66},{24,3},{28,67},{32,128},... | collective-permute-start | bytes 122888 | tf_op jit(solution)/shard_map/ppermute | solution.py:250
  22.0 18.1 %copy-start.6 = (f32[4,16,320]{2,1,0:T(8,128)S(1)}, f32[4,16,320]{2,1,0:T(8,128)}, u32[]{:S(2)}) copy-start(f32[4,16,320]{2,1,0:T(8,128)} %param.15) | copy-start | bytes 245764
  22.0 26.8 %copy-start.19 = (s32[2]{0:T(128)S(1)}, s32[2]{0:T(128)}, u32[]{:S(2)}) copy-start(s32[2]{0:T(128)} %param.28) | copy-start | bytes 28
  22.0 26.9 %copy-start.15 = (s32[4,64]{1,0:T(4,128)S(1)}, s32[4,64]{1,0:T(4,128)}, u32[]{:S(2)}) copy-start(s32[4,64]{1,0:T(4,128)} %param.29) | copy-start | bytes 3076
  22.0 27.3 %copy-start.17 = (s32[4]{0:T(128)S(1)}, s32[4]{0:T(128)}, u32[]{:S(2)}) copy-start(s32[4]{0:T(128)} %param.27) | copy-start | bytes 52
  22.1 27.3 %copy-start.8 = (bf16[512,256]{1,0:T(8,128)(2,1)S(1)}, bf16[512,256]{1,0:T(8,128)(2,1)}, u32[]{:S(2)}) copy-start(bf16[512,256]{1,0:T(8,128)(2,1)} %param.22) | copy-start | bytes 786436
  22.1 27.3 %copy-start.9 = (bf16[512,256]{1,0:T(8,128)(2,1)S(1)}, bf16[512,256]{1,0:T(8,128)(2,1)}, u32[]{:S(2)}) copy-start(bf16[512,256]{1,0:T(8,128)(2,1)} %param.21) | copy-start | bytes 786436
  22.8 16.5 %all-to-all-start.3 = ((bf16[2,160,384]{2,1,0:T(8,128)(2,1)}), bf16[2,160,384]{2,1,0:T(8,128)(2,1)S(1)}, u32[]{:S(2)}, u32[]{:S(2)}) async-start(bf16[2,160,384]{2,1,0:T(8,128)(2,1)} %maximum_maximum_fusion), calls=%async_computation.3 | async-start | bytes 491520 | tf_op jit(solution)/shard_map/all_to_all | solution.py:38
  34.6 88.6 %all-gather.3.cloned.1.call-start = ((), (), s32[]{:S(2)}) async-start(), calls=%async_computation.9 | async-start | bytes 5570560 | tf_op jit(solution)/shard_map/all_gather | solution.py:291
  40.9 14.9 %all-to-all-start = ((f32[16,1,80]{2,1,0:T(1,128)}), f32[16,1,80]{2,1,0:T(1,128)S(1)}, u32[]{:S(2)}, u32[]{:S(2)}) async-start(f32[16,1,80]{2,1,0:T(1,128)} %broadcast_in_dim.12), calls=%async_computation | async-start | bytes 16384 | tf_op jit(solution)/shard_map/all_to_all | solution.py:32
  55.7 11.1 %all-to-all-start.4 = ((bf16[2,1040,128]{2,1,0:T(8,128)(2,1)}), bf16[2,1040,128]{2,1,0:T(8,128)(2,1)S(1)}, u32[]{:S(2)}, u32[]{:S(2)}) async-start(bf16[2,1040,128]{2,1,0:T(8,128)(2,1)} %pad_maximum_fusion), calls=%async_computation.4 | async-start | bytes 1064960 | tf_op jit(solution)/shard_map/all_to_all | solution.py:38
  68.0 18.4 %all-to-all-start.1 = ((bf16[16,80,320]{2,1,0:T(8,128)(2,1)}), bf16[16,80,320]{2,1,0:T(8,128)(2,1)S(1)}, u32[]{:S(2)}, u32[]{:S(2)}) async-start(bf16[16,80,320]{2,1,0:T(8,128)(2,1)} %broadcast_in_dim.14), calls=%async_computation.1 | async-start | bytes 1966080 | tf_op jit(solution)/shard_map/all_to_all | solution.py:32
  71.6 26.7 %collective-permute-start.2 = (bf16[2,1040,128]{2,1,0:T(8,128)(2,1)S(1)}, bf16[2,1040,128]{2,1,0:T(8,128)(2,1)S(1)}, u32[]{:S(2)}, u32[]{:S(2)}) collective-permute-start(bf16[2,1040,128]{2,1,0:T(8,128)(2,1)S(1)} %all-to-all-done.4.own_ref), channel_id=1, source_target_pairs={{0,4},{4,0},{8,12},{12,8},{16,20},{20,16},{24,28},{28,24},{32,36},... | collective-permute-start | bytes 1597448 | tf_op jit(solution)/shard_map/ppermute | solution.py:254
  87.9 35.4 %all-to-all-start.2 = ((bf16[2,16,80,320]{3,2,1,0:T(8,128)(2,1)}), bf16[2,16,80,320]{3,2,1,0:T(8,128)(2,1)S(1)}, u32[]{:S(2)}, u32[]{:S(2)}) async-start(bf16[2,16,80,320]{3,2,1,0:T(8,128)(2,1)} %broadcast_in_dim.15), calls=%async_computation.2 | async-start | bytes 3932160 | tf_op jit(solution)/shard_map/all_to_all | solution.py:32
  98.3 30.2 %copy-start.10 = (bf16[2,1040,128]{2,1,0:T(8,128)(2,1)}, bf16[2,1040,128]{2,1,0:T(8,128)(2,1)S(1)}, u32[]{:S(2)}) copy-start(bf16[2,1040,128]{2,1,0:T(8,128)(2,1)S(1)} %collective-permute-done.2.other_ref) | copy-start | bytes 1597444
  128.5 20.7 %all-to-all-start.5 = ((bf16[16,64,128]{2,1,0:T(8,128)(2,1)}), bf16[16,64,128]{2,1,0:T(8,128)(2,1)S(1)}, u32[]{:S(2)}, u32[]{:S(2)}) async-start(bf16[16,64,128]{2,1,0:T(8,128)(2,1)} %shard_map.166), calls=%async_computation.5 | async-start | bytes 524288 | tf_op jit(solution)/shard_map/all_to_all | solution.py:38
  139.9 9.3 %collective-permute-start.3 = (bf16[320,128]{1,0:T(8,128)(2,1)}, bf16[320,128]{1,0:T(8,128)(2,1)S(1)}, u32[]{:S(2)}, u32[]{:S(2)}) collective-permute-start(bf16[320,128]{1,0:T(8,128)(2,1)} %shard_map.167.own_new), channel_id=1, source_target_pairs={{0,4},{4,0},{8,12},{12,8},{16,20},{20,16},{24,28},{28,24},{32,36},... | collective-permute-start | bytes 245768 | tf_op jit(solution)/shard_map/ppermute | solution.py:254
  159.6 25.6 %all-to-all-start.6 = ((bf16[16,80,128]{2,1,0:T(8,128)(2,1)}), bf16[16,80,128]{2,1,0:T(8,128)(2,1)S(1)}, u32[]{:S(2)}, u32[]{:S(2)}) async-start(bf16[16,80,128]{2,1,0:T(8,128)(2,1)} %shard_map.168), calls=%async_computation.6 | async-start | bytes 655360 | tf_op jit(solution)/shard_map/all_to_all | solution.py:38
  173.1 39.8 %copy-start.1 = (bf16[16,320,128]{2,1,0:T(8,128)(2,1)}, bf16[16,320,128]{2,1,0:T(8,128)(2,1)S(1)}, u32[]{:S(2)}) copy-start(bf16[16,320,128]{2,1,0:T(8,128)(2,1)S(1)} %slice.76.own_ref) | copy-start | bytes 3932164
  173.1 38.1 %collective-permute-start.4 = (bf16[16,320,128]{2,1,0:T(8,128)(2,1)S(1)}, bf16[16,320,128]{2,1,0:T(8,128)(2,1)S(1)}, u32[]{:S(2)}, u32[]{:S(2)}) collective-permute-start(bf16[16,320,128]{2,1,0:T(8,128)(2,1)S(1)} %slice.76.own_ref), channel_id=1, source_target_pairs={{0,64},{64,0},{1,65},{65,1},{2,66},{66,2},{3,67},{67,3},{4,68},{68... | collective-permute-start | bytes 3932168 | tf_op jit(solution)/shard_map/ppermute | solution.py:335
  188.1 24.8 %all-to-all-start.7 = ((bf16[32,64,128]{2,1,0:T(8,128)(2,1)}), bf16[32,64,128]{2,1,0:T(8,128)(2,1)S(1)}, u32[]{:S(2)}, u32[]{:S(2)}) async-start(bf16[32,64,128]{2,1,0:T(8,128)(2,1)} %shard_map.169), calls=%async_computation.7 | async-start | bytes 1048576 | tf_op jit(solution)/shard_map/all_to_all | solution.py:38
  203.9 7.3 %collective-permute-start.5 = (bf16[2,16,128]{2,1,0:T(8,128)(2,1)S(1)}, bf16[2,16,128]{2,1,0:T(8,128)(2,1)S(1)}, u32[]{:S(2)}, u32[]{:S(2)}) collective-permute-start(bf16[2,16,128]{2,1,0:T(8,128)(2,1)S(1)} %get-tuple-element.20), channel_id=1, source_target_pairs={{0,64},{64,0},{1,65},{65,1},{2,66},{66,2},{3,67},{67,3},{4,68},{68... | collective-permute-start | bytes 24584 | tf_op jit(solution)/shard_map/ppermute | solution.py:343
  217.2 13.4 %all-to-all-start.8 = ((f32[16,1,64]{2,1,0:T(1,128)}), f32[16,1,64]{2,1,0:T(1,128)S(1)}, u32[]{:S(2)}, u32[]{:S(2)}) async-start(f32[16,1,64]{2,1,0:T(1,128)} %get-tuple-element.12), calls=%async_computation.8 | async-start | bytes 16384 | tf_op jit(solution)/shard_map/all_to_all | solution.py:38
  (12 other events, 69.5 us)
Sparse Core Ops, SparseCore 0:
  40.2 82.9 all-gather.2

commit v5 on v4

--- a/solution.py
+++ b/solution.py
@@ -53,7 +53,7 @@
     width = acc.shape[1]
     for xh in range(2):
         for core in range(2):
-            rows = h_ref[core, 0, xh].reshape(160, 320)
+            rows = h_ref[core, step, xh].reshape(160, 320)
             at = 2 * (2 * xh + core)
             weights = w_ref[at : at + 2].reshape(320, width)
             total = total + jnp.dot(rows, weights, preferred_element_type=F32)
@@ -76,7 +76,7 @@
         project_kernel,
         grid=(4,),
         in_specs=[
-            pl.BlockSpec((2, 1, 2, 2, 80, 320), lambda s: (0, s, 0, 0, 0, 0)),
+            pl.BlockSpec(memory_space=pltpu.VMEM),
             pl.BlockSpec((8, 160, width), lambda s: (s % 2, s // 2, block)),
         ],
         out_specs=pl.BlockSpec(shape, lambda s: (0,) * len(shape)),
@@ -95,19 +95,61 @@
     return [high, middle, value - high - middle]
 
 
-def attend_kernel(q_ref, own_ref, other_ref, own_vt_ref, other_vt_ref, own_new, other_new, out_ref, fresh_vt):
+def pack_kernel(side_ref, keys_ref, values_ref, seen_ref, own_ref, other_ref):
+    first = side_ref[0] == 0
+    for ref, at in ((keys_ref, 0), (values_ref, 512)):
+        low, high = ref[:, :HD], ref[:, HD:]
+        own_ref[at : at + 512, :] = jnp.where(first, low, high)
+        other_ref[at : at + 512, :] = jnp.where(first, high, low)
+    own_ref[1024:1040, :] = seen_ref[...]
+    other_ref[1024:1040, :] = seen_ref[...]
+
+
+def pack(side, keys, values, seen):
+    return pl.pallas_call(
+        pack_kernel,
+        in_specs=[
+            pl.BlockSpec(memory_space=pltpu.SMEM),
+            *[pl.BlockSpec(memory_space=pltpu.VMEM)] * 3,
+        ],
+        out_shape=(jax.ShapeDtypeStruct((1040, HD), BF16),) * 2,
+        compiler_params=pltpu.CompilerParams(vmem_limit_bytes=VMEM_LIMIT),
+        cost_estimate=pl.CostEstimate(flops=0, bytes_accessed=2**20, transcendentals=0),
+    )(side, keys, values, seen)
+
+
+def turn_kernel(own_ref, other_ref, out_ref):
+    ones = (lax.broadcasted_iota(jnp.int32, (16, 512), 0) == 0).astype(F32).astype(BF16)
+    for i, ref in enumerate((own_ref, other_ref)):
+        for side in range(2):
+            out_ref[i, side, 0:HD] = ref[side, 512:1024, :].astype(F32).T.astype(BF16)
+            out_ref[i, side, HD : HD + 16] = ones
+
+
+def turn(kv):
+    return pl.pallas_call(
+        turn_kernel,
+        out_shape=jax.ShapeDtypeStruct((2, 2, HD + 16, 512), BF16),
+        compiler_params=pltpu.CompilerParams(vmem_limit_bytes=VMEM_LIMIT),
+        cost_estimate=pl.CostEstimate(flops=0, bytes_accessed=2**20, transcendentals=0),
+    )(*kv)
+
+
+def attend_kernel(q_ref, own_ref, other_ref, vt_ref, own_new, other_new, out_ref, fresh_vt):
     @pl.when(pl.program_id(0) == 0)
     def _():
+        ones = (lax.broadcasted_iota(jnp.int32, (16, 160), 0) == 0).astype(F32)
         for i, new in enumerate((own_new, other_new)):
-            fresh_vt[i] = new[160:320, :].astype(F32).T.astype(BF16)
+            fresh_vt[i, 0:HD] = new[160:320, :].astype(F32).T.astype(BF16)
+            fresh_vt[i, HD : HD + 16] = ones.astype(BF16)
 
     scale = 1.0 / math.sqrt(HD)
     queries = q_ref[...]
     lanes = queries.shape[0]
     across = (((1,), (1,)), ((), ()))
 
-    def scores(keys):
-        return lax.dot_general(keys, queries, across, preferred_element_type=F32) * scale
+    def products(keys):
+        return lax.dot_general(keys, queries, across, preferred_element_type=F32)
 
     token = lax.broadcasted_iota(jnp.int32, (160, lanes), 0)
     lane = lax.broadcasted_iota(jnp.int32, (160, lanes), 1)
@@ -115,30 +157,29 @@
     visible = (token >= 64) | ((token >> 4) <= ((lane & 63) >> 4))
 
     parts, values = [], []
-    for i, (kv_ref, vt_ref, new) in enumerate(
-        ((own_ref, own_vt_ref, own_new), (other_ref, other_vt_ref, other_new))
-    ):
+    for i, (kv_ref, new) in enumerate(((own_ref, own_new), (other_ref, other_new))):
         for side in range(2):
             seen = kv_ref[side, 1024:1040, :].astype(F32)
             hidden = jnp.where(seen > 0.5, 0.0, -jnp.inf)
             hidden = jnp.concatenate([hidden] * (lanes // HD), axis=1)
             for slot in range(2):
                 at = slice(slot * SLOT, (slot + 1) * SLOT)
-                parts.append(scores(kv_ref[side, at, :]) + hidden[slot : slot + 1, :])
-                values.append(vt_ref[side, :, at])
-        parts.append(jnp.where(visible, scores(new[0:160, :]), -jnp.inf))
+                parts.append(products(kv_ref[side, at, :]) + hidden[slot : slot + 1, :])
+                values.append(vt_ref[i, side, :, at])
+        parts.append(jnp.where(visible, products(new[0:160, :]), -jnp.inf))
         values.append(fresh_vt[i])
 
-    peak = functools.reduce(
+    top = functools.reduce(
         jnp.maximum, [jnp.max(part, axis=0, keepdims=True) for part in parts]
     )
-    numer = jnp.zeros((HD, lanes), F32)
-    denom = jnp.zeros((1, lanes), F32)
+    factor = scale * math.log2(math.e)
+    shift = top * factor
+    total = jnp.zeros((HD + 16, lanes), F32)
     for part, value in zip(parts, values):
-        weights = jnp.exp(part - peak).astype(BF16)
-        denom = denom + jnp.sum(weights.astype(F32), axis=0, keepdims=True)
-        numer = numer + jnp.dot(value, weights, preferred_element_type=F32)
-    mean = (numer / denom).T.astype(BF16)
+        weights = jnp.exp2(part * factor - shift).astype(BF16)
+        total = total + jnp.dot(value, weights, preferred_element_type=F32)
+    peak, denom = top * scale, total[HD : HD + 1]
+    mean = (total[0:HD] / denom).T.astype(BF16)
     totals = jnp.concatenate(
         [*in_three(peak), *in_three(denom), jnp.zeros((10, lanes), F32)], axis=0
     )
@@ -153,7 +194,7 @@
 def attend(queries, kv, values_t, fresh):
     step = 256
     rows = queries.shape[0]
-    arrays = (*kv, *values_t, *fresh)
+    arrays = (*kv, values_t, *fresh)
 
     def whole(array):
         return pl.BlockSpec(array.shape, lambda s: (0,) * array.ndim)
@@ -167,7 +208,7 @@
         ],
         out_specs=pl.BlockSpec((step // 64, 80, HD), lambda s: (s, 0, 0)),
         out_shape=jax.ShapeDtypeStruct((rows // 64, 80, HD), BF16),
-        scratch_shapes=[pltpu.VMEM((2, HD, 160), BF16)],
+        scratch_shapes=[pltpu.VMEM((2, HD + 16, 160), BF16)],
         compiler_params=pltpu.CompilerParams(vmem_limit_bytes=VMEM_LIMIT),
         cost_estimate=pl.CostEstimate(
             flops=4 * rows * 2368 * HD,
@@ -206,16 +247,12 @@
     )(parts)
 
 
-def output_kernel(side_ref, att_ref, own_ref, other_ref, y_ref, square_ref):
-    side = side_ref[0]
+def output_kernel(att_ref, w_ref, y_ref, square_ref):
     total = jnp.zeros((320, 64), F32)
     for i in range(16):
-        attention = jnp.concatenate(
-            [att_ref[2 * i + side], att_ref[2 * i + 1 - side]], axis=1
-        )
-        weights = jnp.concatenate([own_ref[i], other_ref[i]], axis=1)
+        attention = jnp.concatenate([att_ref[2 * i], att_ref[2 * i + 1]], axis=1)
         total = total + lax.dot_general(
-            weights, attention, (((1,), (1,)), ((), ())), preferred_element_type=F32
+            w_ref[i], attention, (((1,), (1,)), ((), ())), preferred_element_type=F32
         )
     y_ref[...] = total.T
     squares = jnp.sum(total * total, axis=0, keepdims=True)
@@ -223,19 +260,15 @@
         square_ref[i] = squares
 
 
-def output_projection(side, attention, own, other):
+def output_projection(attention, weights):
     return pl.pallas_call(
         output_kernel,
-        in_specs=[
-            pl.BlockSpec(memory_space=pltpu.SMEM),
-            *[pl.BlockSpec(memory_space=pltpu.VMEM)] * 3,
-        ],
         out_shape=(
             jax.ShapeDtypeStruct((64, 320), F32),
             jax.ShapeDtypeStruct((16, 1, 64), F32),
         ),
         compiler_params=pltpu.CompilerParams(vmem_limit_bytes=VMEM_LIMIT),
-    )(side, attention, own, other)
+    )(attention, weights)
 
 
 def to_owners(array, same):
@@ -275,20 +308,12 @@
     rows_count = flight * ch_dev
 
     side = lax.axis_index("xl")
-    odd = lax.axis_index("z") % 2
-    w_out_t = jnp.transpose(w_out)
-    low, high = w_out_t[:, :HD], w_out_t[:, HD:]
-    first = to_owners(jnp.where(odd == 0, low, high), True)
-    second = to_owners(jnp.where(odd == 0, high, low), False)
     w_heads = jnp.concatenate([by_head(w) for w in (w_key, w_value, w_query)], axis=2)
-    w_heads = swapped(w_heads, "xl").reshape(320, 3 * HD)
-    w_columns = jnp.where(
-        side == 0,
-        jnp.concatenate([first, second], axis=0),
-        jnp.concatenate([second, first], axis=0),
-    )
-    shard = jnp.concatenate([w_heads, w_columns], axis=1)
-    w_full = lax.all_gather(shard, "z", axis=0, tiled=False)
+    w_heads, cache_keys, cache_values = lax.optimization_barrier(
+        (swapped(w_heads, "xl"), cache_keys, cache_values)
+    )
+    w_heads = w_heads.reshape(320, 3 * HD)
+    w_full = lax.all_gather(w_heads, "z", axis=0, tiled=False)
 
     current = level_lookup(levels, noise_index)
     following = level_lookup(levels, noise_index + 1)
@@ -306,7 +331,11 @@
         * norm_gain[None, :]
         * (1.0 + sigma_rows[:, None] * mod_gain[None, :])
     ).astype(BF16)
+    features, w_out = lax.optimization_barrier((features, w_out))
+    w_out = jnp.transpose(w_out)
+    first, second = to_owners(w_out, True), to_owners(w_out, False)
     features = sent_to_all(features, ("y", "xh", "xl"))
+    features, first, second = lax.optimization_barrier((features, first, second))
     features = sent_to_all(features, "core").reshape(2, 4, 2, 2, 80, width)
 
     table = jnp.arange(group_mask.shape[1], dtype=jnp.int32)
@@ -314,25 +343,24 @@
     seen = jnp.sum(held[None, :, :] * group_mask[:, None, :], axis=2) != 0
     seen = jnp.repeat(seen.T.astype(BF16), ch_dev, axis=1)
     seen = jnp.pad(jnp.concatenate([seen, seen], axis=1), ((0, 14), (0, 0)))
-    kv = jnp.concatenate(
-        [
-            by_head(cache_keys),
-            by_head(cache_values),
-            jnp.broadcast_to(seen[None], (2, *seen.shape)),
-        ],
-        axis=1,
-    )
-    kv = swapped(kv, "xl")
+    kv_own, kv_other = pack(side.reshape(1), cache_keys, cache_values, seen)
+    kv_other = lax.ppermute(kv_other, "xl", [(0, 1), (1, 0)])
+    kv = jnp.stack([kv_own, kv_other])
     kv = (kv, from_neighbour(kv))
-    values_t = [jnp.transpose(part[:, 512:1024], (0, 2, 1)) for part in kv]
+    values_t = turn(kv)
+
+    w_columns = jnp.where(
+        side == 0,
+        jnp.concatenate([first, second], axis=0),
+        jnp.concatenate([second, first], axis=0),
+    )
+    w_out_full = lax.all_gather(w_columns, "z", axis=0, tiled=False)
 
     w_full, values_t = lax.optimization_barrier((w_full, values_t))
     queries = project(features, w_full, 2, HD, (16, 64, HD))
     queries = swapped(queries, "z").reshape(-1, HD)
     new = project(features, w_full, 0, 2 * HD, (320, HD))
     fresh = (new, from_neighbour(new))
-    w_out_own = w_full[:, :, 3 * HD :]
-    w_out_other = lax.ppermute(w_out_own, "xl", [(0, 1), (1, 0)])
     parts = attend(queries, kv, values_t, fresh)
     parts = swapped(parts, "z")
     attention = swapped(combine(parts), (*WIDE, "xl"))
@@ -348,7 +376,7 @@
     )
     new_keys, new_values = finished[0], finished[1]
 
-    y, y_squares = output_projection(side.reshape(1), attention, w_out_own, w_out_other)
+    y, y_squares = output_projection(attention, w_out_full)
     y_squares = swapped(y_squares, WIDE).sum(axis=(0, 1))
     velocity = y * lax.rsqrt(y_squares / D + EPSILON)[:, None] * out_gain[None, :]
     new_state = state + (following - current)[:, None, None] * velocity.reshape(

time: 241 us -> 249 us (1.033)
  blocking collectives: 0 us -> 41.1 us
  starting transfers between devices: 99.3 us -> 73.4 us
  waiting for transfers between devices: 82.7 us -> 72.7 us
  Pallas kernels: 23.5 us -> 27.5 us
  local copies, waits for them, and re-layouts: 12.8 us -> 9.45 us
  other arithmetic: 6.41 us -> 9.44 us
    all_to_all x0 -> x2, blocking collectives: none -> 41.1 us  [swapped(): return lax.all_to_all(blocks, axis, 0, 0, tiled=True)]
    all_to_all x6 -> x3, starting transfers between devices: 55.9 us -> 32.3 us  [swapped(): return lax.all_to_all(blocks, axis, 0, 0, tiled=True)]
    ppermute x2, waiting for transfers between devices: 0.01 us -> 21.8 us  [to_owners(): return lax.ppermute(array, ('y', 'xl', 'z', 'xh', 'core'), pairs)]
    all_to_all x6 -> x3, waiting for transfers between devices: 29.1 us -> 8.88 us  [swapped(): return lax.all_to_all(blocks, axis, 0, 0, tiled=True)]
    all_gather x1 -> x2, waiting for transfers between devices: 24 us -> 6.86 us  [the longest x1 6.85 us: local(): w_full = lax.all_gather(w_heads, 'z', axis=0, tiled=False)]
    ppermute x2, waiting for transfers between devices: 9.89 us -> 21.4 us  [from_neighbour(): return lax.ppermute(array, 'z', [(z, z ^ 1) for z in range(16)])]
    all_to_all x3, waiting for transfers between devices: 15.7 us -> 5.27 us  [sent_to_all(): lax.all_to_all(jnp.broadcast_to(array[None], (devices, *array.shape)), ax...]
    pallas_call x3 -> x5, Pallas kernels: 11.7 us -> 16.6 us  [the longest x2 8.89 us: project(): pl.pallas_call(project_kernel, grid=(4,), in_specs=[pl.BlockSpec(memory_s...]
  transfers between devices with their start and end apart: 16 -> 14, of which waited for: 11 -> 11; matrix products, arithmetic and copies ran while one was open for 5% -> 5% of each run, Pallas kernels for 3% -> 10%
where the time goes in v5:
time: 249 us; the launch traced here: 248 us
  starting transfers between devices  73.4 us (29%)
  waiting for transfers between devices  72.7 us (29%)
  blocking collectives  41.1 us (17%)
  Pallas kernels  27.5 us (11%)
  between operations  14.3 us (6%)
  local copies, waits for them, and re-layouts  9.45 us (4%)
  other arithmetic  9.44 us (4%)
    all_to_all x2, blocking collectives, swapped(): return lax.all_to_all(blocks, axis, 0, 0, tiled=True)  41.1 us
    all_to_all x3, starting transfers between devices, swapped(): return lax.all_to_all(blocks, axis, 0, 0, tiled=True)  32.3 us
    ppermute x2, waiting for transfers between devices, to_owners(): return lax.ppermute(array, ('y', 'xl', 'z', 'xh', 'core'), pairs)  21.8 us
    ppermute x2, waiting for transfers between devices, from_neighbour(): return lax.ppermute(array, 'z', [(z, z ^ 1) for z in range(16)])  21.4 us
    all_to_all x3, starting transfers between devices, sent_to_all(): lax.all_to_all(jnp.broadcast_to(array[None], (devices, *array.shape)), ax...  18.1 us
    ppermute x2, starting transfers between devices, to_owners(): return lax.ppermute(array, ('y', 'xl', 'z', 'xh', 'core'), pairs)  9.81 us
    pallas_call x2, Pallas kernels, project(): pl.pallas_call(project_kernel, grid=(4,), in_specs=[pl.BlockSpec(memory_s...  8.89 us
    all_to_all x3, waiting for transfers between devices, swapped(): return lax.all_to_all(blocks, axis, 0, 0, tiled=True)  8.88 us
  transfers between devices with their start and end apart: 14, of which 11 were waited for; matrix products, arithmetic and copies ran while one was open for 5% of the time, Pallas kernels for 10%

profile of v5, /device:TPU:1, one launch (start us, length us, event | category | flops | bytes accessed | tf_op | source)
XLA Modules:
  0.0 247.9 jit_solution(1430560647727618859)
XLA Ops:
  8.9 7.6 %all_to_all.41 = bf16[2,160,384]{2,1,0:T(8,128)(2,1)} all-to-all(bf16[2,160,384]{2,1,0:T(8,128)(2,1)S(1)} %maximum_maximum_fusion), channel_id=1, replica_groups=mesh['y'=4,'xl'=2,'z'=16,'xh'=2,'core'=2] {'xl'}, dimensions={0} | all-to-all | bytes 491520 | tf_op jit(solution)/shard_map/all_to_all | solution.py:38
  18.9 10.7 %all-to-all-start = ((f32[16,1,80]{2,1,0:T(1,128)}), f32[16,1,80]{2,1,0:T(1,128)S(1)}, u32[]{:S(2)}, u32[]{:S(2)}) async-start(f32[16,1,80]{2,1,0:T(1,128)} %broadcast_in_dim.10), calls=%async_computation | async-start | bytes 16384 | tf_op jit(solution)/shard_map/all_to_all | solution.py:32
  31.3 5.3 %all-to-all-done = f32[16,1,80]{2,1,0:T(1,128)S(1)} async-done(((f32[16,1,80]{2,1,0:T(1,128)}), f32[16,1,80]{2,1,0:T(1,128)S(1)}, u32[]{:S(2)}, u32[]{:S(2)}) %all-to-all-start) | async-done | bytes 5152 | tf_op jit(solution)/shard_map/all_to_all | solution.py:32
  38.7 3.6 %all-to-all-start.1 = ((bf16[16,80,320]{2,1,0:T(8,128)(2,1)}), bf16[16,80,320]{2,1,0:T(8,128)(2,1)S(1)}, u32[]{:S(2)}, u32[]{:S(2)}) async-start(bf16[16,80,320]{2,1,0:T(8,128)(2,1)} %broadcast_in_dim.12), calls=%async_computation.1 | async-start | bytes 1966080 | tf_op jit(solution)/shard_map/all_to_all | solution.py:32
  44.9 7.3 %collective-permute-start.1 = (bf16[160,256]{1,0:T(8,128)(2,1)S(1)}, bf16[160,256]{1,0:T(8,128)(2,1)S(1)}, u32[]{:S(2)}, u32[]{:S(2)}) collective-permute-start(bf16[160,256]{1,0:T(8,128)(2,1)S(1)} %bitcast.61), channel_id=1, source_target_pairs={{0,64},{4,0},{8,65},{12,1},{16,66},{20,2},{24,67},{28,3},{32,192},... | collective-permute-start | bytes 245768 | tf_op jit(solution)/shard_map/ppermute | solution.py:283
  53.8 20.2 %collective-permute-done.1 = bf16[160,256]{1,0:T(8,128)(2,1)S(1)} collective-permute-done((bf16[160,256]{1,0:T(8,128)(2,1)S(1)}, bf16[160,256]{1,0:T(8,128)(2,1)S(1)}, u32[]{:S(2)}, u32[]{:S(2)}) %collective-permute-start.1) | collective-permute-done | bytes 81952 | tf_op jit(solution)/shard_map/ppermute | solution.py:283
  77.8 4.7 %collective-permute-start.2 = (bf16[1040,128]{1,0:T(8,128)(2,1)}, bf16[1040,128]{1,0:T(8,128)(2,1)S(1)}, u32[]{:S(2)}, u32[]{:S(2)}) collective-permute-start(bf16[1040,128]{1,0:T(8,128)(2,1)} %get-tuple-element.24), channel_id=1, source_target_pairs={{0,64},{64,0},{1,65},{65,1},{2,66},{66,2},{3,67},{67,3},{4,68},{68... | collective-permute-start | bytes 798728 | tf_op jit(solution)/shard_map/ppermute | solution.py:347
  82.5 4.4 %collective-permute-done.2 = bf16[1040,128]{1,0:T(8,128)(2,1)S(1)} collective-permute-done((bf16[1040,128]{1,0:T(8,128)(2,1)}, bf16[1040,128]{1,0:T(8,128)(2,1)S(1)}, u32[]{:S(2)}, u32[]{:S(2)}) %collective-permute-start.2) | collective-permute-done | bytes 266272 | tf_op jit(solution)/shard_map/ppermute | solution.py:347
  91.4 3.7 %all-to-all-start.2 = ((bf16[2,16,80,320]{3,2,1,0:T(8,128)(2,1)}), bf16[2,16,80,320]{3,2,1,0:T(8,128)(2,1)S(1)}, u32[]{:S(2)}, u32[]{:S(2)}) async-start(bf16[2,16,80,320]{3,2,1,0:T(8,128)(2,1)} %broadcast_in_dim.13), calls=%async_computation.2 | async-start | bytes 3932160 | tf_op jit(solution)/shard_map/all_to_all | solution.py:32
  95.1 16.8 %collective-permute-done.3.other_ref = bf16[2,1040,128]{2,1,0:T(8,128)(2,1)S(1)} collective-permute-done((bf16[2,1040,128]{2,1,0:T(8,128)(2,1)S(1)}, bf16[2,1040,128]{2,1,0:T(8,128)(2,1)S(1)}, u32[]{:S(2)}, u32[]{:S(2)}) %collective-permute-start.3) | collective-permute-done | bytes 532512 | tf_op jit(solution)/shard_map/ppermute | solution.py:287
  115.0 6.8 %all-gather.3.cloned.1.call-done.w_ref = bf16[16,320,384]{2,1,0:T(8,128)(2,1)} async-done(((bf16[1,320,384]{2,1,0:T(8,128)(2,1)}), bf16[16,320,384]{2,1,0:T(8,128)(2,1)}) %all-gather.3.cloned.1.call-update) | async-done | bytes 3932176 | tf_op jit(solution)/shard_map/all_gather | solution.py:316
  123.2 4.3 %shard_map.168 = bf16[16,64,128]{2,1,0:T(8,128)(2,1)} custom-call(bf16[2,4,2,2,80,320]{5,4,3,2,1,0:T(8,128)(2,1)} %bitcast.47, bf16[16,320,384]{2,1,0:T(8,128)(2,1)} %all-gather.3.cloned.1.call-done.w_ref), custom_call_target="tpu_custom_call" | custom-call | flops 209715200 | bytes 4194304 | tf_op jit(solution)/shard_map/pallas_call | solution.py:75
  127.5 5.7 %all-to-all-start.4 = ((bf16[16,64,128]{2,1,0:T(8,128)(2,1)}), bf16[16,64,128]{2,1,0:T(8,128)(2,1)S(1)}, u32[]{:S(2)}, u32[]{:S(2)}) async-start(bf16[16,64,128]{2,1,0:T(8,128)(2,1)} %shard_map.168), calls=%async_computation.4 | async-start | bytes 524288 | tf_op jit(solution)/shard_map/all_to_all | solution.py:38
  133.2 4.6 %shard_map.169.own_new = bf16[320,128]{1,0:T(8,128)(2,1)} custom-call(bf16[2,4,2,2,80,320]{5,4,3,2,1,0:T(8,128)(2,1)} %bitcast.48, bf16[16,320,384]{2,1,0:T(8,128)(2,1)} %all-gather.3.cloned.1.call-done.w_ref), custom_call_target="tpu_custom_call" | custom-call | flops 419430400 | bytes 4194304 | tf_op jit(solution)/shard_map/pallas_call | solution.py:75
  137.8 3.3 %collective-permute-start.4 = (bf16[320,128]{1,0:T(8,128)(2,1)}, bf16[320,128]{1,0:T(8,128)(2,1)S(1)}, u32[]{:S(2)}, u32[]{:S(2)}) collective-permute-start(bf16[320,128]{1,0:T(8,128)(2,1)} %shard_map.169.own_new), channel_id=1, source_target_pairs={{0,4},{4,0},{8,12},{12,8},{16,20},{20,16},{24,28},{28,24},{32,36},... | collective-permute-start | bytes 245768 | tf_op jit(solution)/shard_map/ppermute | solution.py:287
  141.1 4.7 %collective-permute-done.4.other_new = bf16[320,128]{1,0:T(8,128)(2,1)S(1)} collective-permute-done((bf16[320,128]{1,0:T(8,128)(2,1)}, bf16[320,128]{1,0:T(8,128)(2,1)S(1)}, u32[]{:S(2)}, u32[]{:S(2)}) %collective-permute-start.4) | collective-permute-done | bytes 81952 | tf_op jit(solution)/shard_map/ppermute | solution.py:287
  146.8 8.7 %shard_map.170 = bf16[16,80,128]{2,1,0:T(8,128)(2,1)} custom-call(bf16[1024,128]{1,0:T(8,128)(2,1)} %bitcast.55, bf16[2,1040,128]{2,1,0:T(8,128)(2,1)} %copy-done.1, bf16[2,1040,128]{2,1,0:T(8,128)(2,1)} %copy-done.4, bf16[2,2,144,512]{3,2,1,0:T(8,128)(2,1)} %shard_map.167.vt_ref, bf16[320,128]{1,0:T(8,128)(2,1)} %shard_map.169.own_new, ...), custom_call_target="tpu_custom_call" | custom-call | flops 1241513984 | bytes 3145728 | tf_op jit(solution)/shard_map/pallas_call | solution.py:202
  155.5 33.5 %all_to_all.42.in_ref = bf16[16,80,128]{2,1,0:T(8,128)(2,1)} all-to-all(bf16[16,80,128]{2,1,0:T(8,128)(2,1)} %shard_map.170), channel_id=1, replica_groups=mesh['y'=4,'xl'=2,'z'=16,'xh'=2,'core'=2] {'z'}, dimensions={0} | all-to-all | bytes 655360 | tf_op jit(solution)/shard_map/all_to_all | solution.py:38
  191.2 21.3 %all-to-all-start.6 = ((bf16[32,64,128]{2,1,0:T(8,128)(2,1)}), bf16[32,64,128]{2,1,0:T(8,128)(2,1)S(1)}, u32[]{:S(2)}, u32[]{:S(2)}) async-start(bf16[32,64,128]{2,1,0:T(8,128)(2,1)} %shard_map.171), calls=%async_computation.6 | async-start | bytes 1048576 | tf_op jit(solution)/shard_map/all_to_all | solution.py:38
  213.2 3.3 %collective-permute-start.5 = (bf16[2,16,128]{2,1,0:T(8,128)(2,1)S(1)}, bf16[2,16,128]{2,1,0:T(8,128)(2,1)S(1)}, u32[]{:S(2)}, u32[]{:S(2)}) collective-permute-start(bf16[2,16,128]{2,1,0:T(8,128)(2,1)S(1)} %get-tuple-element.34), channel_id=1, source_target_pairs={{0,64},{64,0},{1,65},{65,1},{2,66},{66,2},{3,67},{67,3},{4,68},{68... | collective-permute-start | bytes 24584 | tf_op jit(solution)/shard_map/ppermute | solution.py:371
  216.5 4.0 %collective-permute-done.5 = bf16[2,16,128]{2,1,0:T(8,128)(2,1)S(1)} collective-permute-done((bf16[2,16,128]{2,1,0:T(8,128)(2,1)S(1)}, bf16[2,16,128]{2,1,0:T(8,128)(2,1)S(1)}, u32[]{:S(2)}, u32[]{:S(2)}) %collective-permute-start.5) | collective-permute-done | bytes 8224 | tf_op jit(solution)/shard_map/ppermute | solution.py:371
  223.7 3.4 %shard_map.172 = (f32[64,320]{1,0:T(8,128)}, f32[16,1,64]{2,1,0:T(1,128)}) custom-call(bf16[32,64,128]{2,1,0:T(8,128)(2,1)} %copy-done.2, bf16[16,320,256]{2,1,0:T(8,128)(2,1)} %all-gather.5.cloned.1.call-done.w_ref), custom_call_target="tpu_custom_call" | custom-call | tf_op jit(solution)/shard_map/pallas_call | solution.py:264
  227.1 5.3 %all-to-all-start.7 = ((f32[16,1,64]{2,1,0:T(1,128)}), f32[16,1,64]{2,1,0:T(1,128)S(1)}, u32[]{:S(2)}, u32[]{:S(2)}) async-start(f32[16,1,64]{2,1,0:T(1,128)} %get-tuple-element.30), calls=%async_computation.7 | async-start | bytes 16384 | tf_op jit(solution)/shard_map/all_to_all | solution.py:38
  233.0 6.2 %all-to-all-done.7 = f32[16,1,64]{2,1,0:T(1,128)S(1)} async-done(((f32[16,1,64]{2,1,0:T(1,128)}), f32[16,1,64]{2,1,0:T(1,128)S(1)}, u32[]{:S(2)}, u32[]{:S(2)}) %all-to-all-start.7) | async-done | bytes 4128 | tf_op jit(solution)/shard_map/all_to_all | solution.py:38
  (69 shorter events, 34.2 us)
Async XLA Ops:
  7.2 35.2 %copy-start.8 = (bf16[256,160]{0,1:T(8,128)(2,1)S(1)}, bf16[256,160]{0,1:T(8,128)(2,1)}, u32[]{:S(2)}) copy-start(bf16[256,160]{0,1:T(8,128)(2,1)} %param.20) | copy-start | bytes 245764
  7.2 114.7 %all-gather.3.cloned.1.call-start = ((), (), s32[]{:S(2)}) async-start(), calls=%async_computation.8 | async-start | bytes 4177920 | tf_op jit(solution)/shard_map/all_gather | solution.py:316
  8.9 65.9 %copy-start.10 = (s32[2]{0:T(128)S(1)}, s32[2]{0:T(128)}, u32[]{:S(2)}) copy-start(s32[2]{0:T(128)} %param.28) | copy-start | bytes 28
  8.9 66.0 %copy-start.7 = (s32[4,64]{1,0:T(4,128)S(1)}, s32[4,64]{1,0:T(4,128)}, u32[]{:S(2)}) copy-start(s32[4,64]{1,0:T(4,128)} %param.29) | copy-start | bytes 3076
  18.9 17.7 %all-to-all-start = ((f32[16,1,80]{2,1,0:T(1,128)}), f32[16,1,80]{2,1,0:T(1,128)S(1)}, u32[]{:S(2)}, u32[]{:S(2)}) async-start(f32[16,1,80]{2,1,0:T(1,128)} %broadcast_in_dim.10), calls=%async_computation | async-start | bytes 16384 | tf_op jit(solution)/shard_map/all_to_all | solution.py:32
  38.7 35.4 %all-to-all-start.1 = ((bf16[16,80,320]{2,1,0:T(8,128)(2,1)}), bf16[16,80,320]{2,1,0:T(8,128)(2,1)S(1)}, u32[]{:S(2)}, u32[]{:S(2)}) async-start(bf16[16,80,320]{2,1,0:T(8,128)(2,1)} %broadcast_in_dim.12), calls=%async_computation.1 | async-start | bytes 1966080 | tf_op jit(solution)/shard_map/all_to_all | solution.py:32
  42.3 178.2 %all-gather.5.cloned.1.call-start = ((), (), s32[]{:S(2)}) async-start(), calls=%async_computation.9 | async-start | bytes 2785280 | tf_op jit(solution)/shard_map/all_gather | solution.py:357
  42.4 11.5 %collective-permute-start = (bf16[160,256]{1,0:T(8,128)(2,1)S(1)}, bf16[160,256]{1,0:T(8,128)(2,1)S(1)}, u32[]{:S(2)}, u32[]{:S(2)}) collective-permute-start(bf16[160,256]{1,0:T(8,128)(2,1)S(1)} %bitcast.60), channel_id=1, source_target_pairs={{0,0},{4,64},{8,1},{12,65},{16,2},{20,66},{24,3},{28,67},{32,128},... | collective-permute-start | bytes 245768 | tf_op jit(solution)/shard_map/ppermute | solution.py:283
  44.9 29.1 %collective-permute-start.1 = (bf16[160,256]{1,0:T(8,128)(2,1)S(1)}, bf16[160,256]{1,0:T(8,128)(2,1)S(1)}, u32[]{:S(2)}, u32[]{:S(2)}) collective-permute-start(bf16[160,256]{1,0:T(8,128)(2,1)S(1)} %bitcast.61), channel_id=1, source_target_pairs={{0,64},{4,0},{8,65},{12,1},{16,66},{20,2},{24,67},{28,3},{32,192},... | collective-permute-start | bytes 245768 | tf_op jit(solution)/shard_map/ppermute | solution.py:283
  77.8 9.1 %collective-permute-start.2 = (bf16[1040,128]{1,0:T(8,128)(2,1)}, bf16[1040,128]{1,0:T(8,128)(2,1)S(1)}, u32[]{:S(2)}, u32[]{:S(2)}) collective-permute-start(bf16[1040,128]{1,0:T(8,128)(2,1)} %get-tuple-element.24), channel_id=1, source_target_pairs={{0,64},{64,0},{1,65},{65,1},{2,66},{66,2},{3,67},{67,3},{4,68},{68... | collective-permute-start | bytes 798728 | tf_op jit(solution)/shard_map/ppermute | solution.py:347
  87.9 3.5 %copy-start.1 = (bf16[2,1040,128]{2,1,0:T(8,128)(2,1)}, bf16[2,1040,128]{2,1,0:T(8,128)(2,1)S(1)}, u32[]{:S(2)}) copy-start(bf16[2,1040,128]{2,1,0:T(8,128)(2,1)S(1)} %pad_maximum_fusion.own_ref) | copy-start | bytes 1597444
  87.9 23.9 %collective-permute-start.3 = (bf16[2,1040,128]{2,1,0:T(8,128)(2,1)S(1)}, bf16[2,1040,128]{2,1,0:T(8,128)(2,1)S(1)}, u32[]{:S(2)}, u32[]{:S(2)}) collective-permute-start(bf16[2,1040,128]{2,1,0:T(8,128)(2,1)S(1)} %pad_maximum_fusion.own_ref), channel_id=1, source_target_pairs={{0,4},{4,0},{8,12},{12,8},{16,20},{20,16},{24,28},{28,24},{32,36},... | collective-permute-start | bytes 1597448 | tf_op jit(solution)/shard_map/ppermute | solution.py:287
  91.4 30.5 %all-to-all-start.2 = ((bf16[2,16,80,320]{3,2,1,0:T(8,128)(2,1)}), bf16[2,16,80,320]{3,2,1,0:T(8,128)(2,1)S(1)}, u32[]{:S(2)}, u32[]{:S(2)}) async-start(bf16[2,16,80,320]{3,2,1,0:T(8,128)(2,1)} %broadcast_in_dim.13), calls=%async_computation.2 | async-start | bytes 3932160 | tf_op jit(solution)/shard_map/all_to_all | solution.py:32
  111.9 0.8 copy-start.4
  121.8 1.3 copy-start
  127.5 18.6 %all-to-all-start.4 = ((bf16[16,64,128]{2,1,0:T(8,128)(2,1)}), bf16[16,64,128]{2,1,0:T(8,128)(2,1)S(1)}, u32[]{:S(2)}, u32[]{:S(2)}) async-start(bf16[16,64,128]{2,1,0:T(8,128)(2,1)} %shard_map.168), calls=%async_computation.4 | async-start | bytes 524288 | tf_op jit(solution)/shard_map/all_to_all | solution.py:38
  137.8 7.9 %collective-permute-start.4 = (bf16[320,128]{1,0:T(8,128)(2,1)}, bf16[320,128]{1,0:T(8,128)(2,1)S(1)}, u32[]{:S(2)}, u32[]{:S(2)}) collective-permute-start(bf16[320,128]{1,0:T(8,128)(2,1)} %shard_map.169.own_new), channel_id=1, source_target_pairs={{0,4},{4,0},{8,12},{12,8},{16,20},{20,16},{24,28},{28,24},{32,36},... | collective-permute-start | bytes 245768 | tf_op jit(solution)/shard_map/ppermute | solution.py:287
  146.1 0.7 copy-start.5
  189.0 50.3 %copy-start.6 = (f32[320]{0:T(512)S(1)}, f32[320]{0:T(512)}, u32[]{:S(2)}) copy-start(f32[320]{0:T(512)} %param.25) | copy-start | bytes 3844
  189.0 51.3 %copy-start.3 = (f32[4,16,320]{2,1,0:T(8,128)S(1)}, f32[4,16,320]{2,1,0:T(8,128)}, u32[]{:S(2)}) copy-start(f32[4,16,320]{2,1,0:T(8,128)} %param.15) | copy-start | bytes 245764
  191.2 31.7 %all-to-all-start.6 = ((bf16[32,64,128]{2,1,0:T(8,128)(2,1)}), bf16[32,64,128]{2,1,0:T(8,128)(2,1)S(1)}, u32[]{:S(2)}, u32[]{:S(2)}) async-start(bf16[32,64,128]{2,1,0:T(8,128)(2,1)} %shard_map.171), calls=%async_computation.6 | async-start | bytes 1048576 | tf_op jit(solution)/shard_map/all_to_all | solution.py:38
  213.2 7.3 %collective-permute-start.5 = (bf16[2,16,128]{2,1,0:T(8,128)(2,1)S(1)}, bf16[2,16,128]{2,1,0:T(8,128)(2,1)S(1)}, u32[]{:S(2)}, u32[]{:S(2)}) collective-permute-start(bf16[2,16,128]{2,1,0:T(8,128)(2,1)S(1)} %get-tuple-element.34), channel_id=1, source_target_pairs={{0,64},{64,0},{1,65},{65,1},{2,66},{66,2},{3,67},{67,3},{4,68},{68... | collective-permute-start | bytes 24584 | tf_op jit(solution)/shard_map/ppermute | solution.py:371
  222.9 0.8 copy-start.2
  227.1 12.1 %all-to-all-start.7 = ((f32[16,1,64]{2,1,0:T(1,128)}), f32[16,1,64]{2,1,0:T(1,128)S(1)}, u32[]{:S(2)}, u32[]{:S(2)}) async-start(f32[16,1,64]{2,1,0:T(1,128)} %get-tuple-element.30), calls=%async_computation.7 | async-start | bytes 16384 | tf_op jit(solution)/shard_map/all_to_all | solution.py:38
  (1 other events, 0.6 us)
Sparse Core Ops, SparseCore 0:
  16.7 105.1 all-gather.2
  123.9 83.3 all-gather.4

commit v6 on v5

--- a/solution.py
+++ b/solution.py
@@ -42,25 +42,39 @@
     return jnp.stack([matrix[:, :HD], matrix[:, HD:]])
 
 
+def lay_out_kernel(h_ref, out_ref):
+    for j in range(16):
+        for xl in range(2):
+            rows = h_ref[j % 2, j // 4, j // 2 % 2, xl]
+            out_ref[80 * xl : 80 * (xl + 1), 320 * j : 320 * (j + 1)] = rows
+
+
+def lay_out(features):
+    return pl.pallas_call(
+        lay_out_kernel,
+        out_shape=jax.ShapeDtypeStruct((160, D), BF16),
+        compiler_params=pltpu.CompilerParams(vmem_limit_bytes=VMEM_LIMIT),
+        cost_estimate=pl.CostEstimate(flops=0, bytes_accessed=4 * 2**20, transcendentals=0),
+    )(features)
+
+
 def project_kernel(h_ref, w_ref, out_ref, acc):
     step = pl.program_id(0)
+    width = acc.shape[1]
+    weights = w_ref[...].reshape(D // 4, width)
+    part = jnp.dot(h_ref[...], weights, preferred_element_type=F32)
 
     @pl.when(step == 0)
     def _():
-        acc[...] = jnp.zeros_like(acc)
-
-    total = acc[...]
-    width = acc.shape[1]
-    for xh in range(2):
-        for core in range(2):
-            rows = h_ref[core, step, xh].reshape(160, 320)
-            at = 2 * (2 * xh + core)
-            weights = w_ref[at : at + 2].reshape(320, width)
-            total = total + jnp.dot(rows, weights, preferred_element_type=F32)
-    acc[...] = total
+        acc[...] = part
+
+    @pl.when(step > 0)
+    def _():
+        acc[...] += part
 
     @pl.when(step == pl.num_programs(0) - 1)
     def _():
+        total = acc[...]
         if width == HD:
             for xl in range(2):
                 rows = total[80 * xl : 80 * xl + 64].astype(BF16)
@@ -76,7 +90,7 @@
         project_kernel,
         grid=(4,),
         in_specs=[
-            pl.BlockSpec(memory_space=pltpu.VMEM),
+            pl.BlockSpec((160, D // 4), lambda s: (0, s)),
             pl.BlockSpec((8, 160, width), lambda s: (s % 2, s // 2, block)),
         ],
         out_specs=pl.BlockSpec(shape, lambda s: (0,) * len(shape)),
@@ -93,29 +107,6 @@
     high = value.astype(BF16).astype(F32)
     middle = (value - high).astype(BF16).astype(F32)
     return [high, middle, value - high - middle]
-
-
-def pack_kernel(side_ref, keys_ref, values_ref, seen_ref, own_ref, other_ref):
-    first = side_ref[0] == 0
-    for ref, at in ((keys_ref, 0), (values_ref, 512)):
-        low, high = ref[:, :HD], ref[:, HD:]
-        own_ref[at : at + 512, :] = jnp.where(first, low, high)
-        other_ref[at : at + 512, :] = jnp.where(first, high, low)
-    own_ref[1024:1040, :] = seen_ref[...]
-    other_ref[1024:1040, :] = seen_ref[...]
-
-
-def pack(side, keys, values, seen):
-    return pl.pallas_call(
-        pack_kernel,
-        in_specs=[
-            pl.BlockSpec(memory_space=pltpu.SMEM),
-            *[pl.BlockSpec(memory_space=pltpu.VMEM)] * 3,
-        ],
-        out_shape=(jax.ShapeDtypeStruct((1040, HD), BF16),) * 2,
-        compiler_params=pltpu.CompilerParams(vmem_limit_bytes=VMEM_LIMIT),
-        cost_estimate=pl.CostEstimate(flops=0, bytes_accessed=2**20, transcendentals=0),
-    )(side, keys, values, seen)
 
 
 def turn_kernel(own_ref, other_ref, out_ref):
@@ -234,53 +225,61 @@
         mixed = jnp.zeros((64, HD), F32)
         for i in range(xl, count, 2):
             mixed = mixed + in_ref[i, 0:64, :].astype(F32) * share[0:64, i : i + 1]
-        mixed = mixed.astype(BF16)
-        for i in range(16):
-            out_ref[2 * i + xl] = mixed
+        out_ref[64 * xl : 64 * (xl + 1)] = mixed.astype(BF16)
 
 
 def combine(parts):
     return pl.pallas_call(
         combine_kernel,
-        out_shape=jax.ShapeDtypeStruct((32, 64, HD), BF16),
+        out_shape=jax.ShapeDtypeStruct((HD, HD), BF16),
         compiler_params=pltpu.CompilerParams(vmem_limit_bytes=VMEM_LIMIT),
     )(parts)
 
 
-def output_kernel(att_ref, w_ref, y_ref, square_ref):
-    total = jnp.zeros((320, 64), F32)
-    for i in range(16):
-        attention = jnp.concatenate([att_ref[2 * i], att_ref[2 * i + 1]], axis=1)
-        total = total + lax.dot_general(
-            w_ref[i], attention, (((1,), (1,)), ((), ())), preferred_element_type=F32
-        )
-    y_ref[...] = total.T
-    squares = jnp.sum(total * total, axis=0, keepdims=True)
+def output_kernel(att_ref, w_ref, out_ref):
+    attention = att_ref[...]
+    for m in range(8):
+        weights = w_ref[2 * m : 2 * m + 2].reshape(320, HD)
+        part = lax.dot_general(
+            attention, weights, (((1,), (1,)), ((), ())), preferred_element_type=F32
+        ).astype(BF16)
+        out_ref[2 * m] = part[0:64]
+        out_ref[2 * m + 1] = part[64:128]
+
+
+def output_projection(attention, weights):
+    return pl.pallas_call(
+        output_kernel,
+        grid=(2,),
+        in_specs=[
+            pl.BlockSpec((HD, HD), lambda s: (0, 0)),
+            pl.BlockSpec((16, 160, HD), lambda s: (0, s, 3)),
+        ],
+        out_specs=pl.BlockSpec((16, 64, 320), lambda s: (s, 0, 0)),
+        out_shape=jax.ShapeDtypeStruct((32, 64, 320), BF16),
+        compiler_params=pltpu.CompilerParams(vmem_limit_bytes=VMEM_LIMIT),
+    )(attention, weights)
+
+
+def over_heads_kernel(in_ref, y_ref, square_ref):
+    total = in_ref[0].astype(F32)
+    for i in range(1, in_ref.shape[0]):
+        total = total + in_ref[i].astype(F32)
+    y_ref[...] = total
+    squares = jnp.sum((total * total).T, axis=0, keepdims=True)
     for i in range(16):
         square_ref[i] = squares
 
 
-def output_projection(attention, weights):
-    return pl.pallas_call(
-        output_kernel,
+def over_heads(parts):
+    return pl.pallas_call(
+        over_heads_kernel,
         out_shape=(
             jax.ShapeDtypeStruct((64, 320), F32),
             jax.ShapeDtypeStruct((16, 1, 64), F32),
         ),
         compiler_params=pltpu.CompilerParams(vmem_limit_bytes=VMEM_LIMIT),
-    )(attention, weights)
-
-
-def to_owners(array, same):
-    def device(g, xl, z):
-        return ((g // 4 * 2 + xl) * 16 + z) * 4 + g % 4
-
-    pairs = [
-        (device(g, c // 16, c % 16), device(c // 2, c % 2 if same else 1 - c % 2, g))
-        for g in range(16)
-        for c in range(32)
-    ]
-    return lax.ppermute(array, ("y", "xl", "z", "xh", "core"), pairs)
+    )(parts)
 
 
 def from_neighbour(array):
@@ -308,12 +307,10 @@
     rows_count = flight * ch_dev
 
     side = lax.axis_index("xl")
-    w_heads = jnp.concatenate([by_head(w) for w in (w_key, w_value, w_query)], axis=2)
-    w_heads, cache_keys, cache_values = lax.optimization_barrier(
-        (swapped(w_heads, "xl"), cache_keys, cache_values)
-    )
-    w_heads = w_heads.reshape(320, 3 * HD)
-    w_full = lax.all_gather(w_heads, "z", axis=0, tiled=False)
+    parts = [by_head(w) for w in (w_key, w_value, w_query)]
+    parts.append(jnp.transpose(w_out.reshape(2, HD, 160), (0, 2, 1)))
+    shard = swapped(jnp.concatenate(parts, axis=2), "xl").reshape(320, 4 * HD)
+    w_full = lax.all_gather(shard, "z", axis=0, tiled=False)
 
     current = level_lookup(levels, noise_index)
     following = level_lookup(levels, noise_index + 1)
@@ -331,39 +328,35 @@
         * norm_gain[None, :]
         * (1.0 + sigma_rows[:, None] * mod_gain[None, :])
     ).astype(BF16)
-    features, w_out = lax.optimization_barrier((features, w_out))
-    w_out = jnp.transpose(w_out)
-    first, second = to_owners(w_out, True), to_owners(w_out, False)
     features = sent_to_all(features, ("y", "xh", "xl"))
-    features, first, second = lax.optimization_barrier((features, first, second))
     features = sent_to_all(features, "core").reshape(2, 4, 2, 2, 80, width)
+    features = lay_out(features)
 
     table = jnp.arange(group_mask.shape[1], dtype=jnp.int32)
     held = (placement[:, None] == table[None, :]).astype(jnp.int32)
     seen = jnp.sum(held[None, :, :] * group_mask[:, None, :], axis=2) != 0
     seen = jnp.repeat(seen.T.astype(BF16), ch_dev, axis=1)
     seen = jnp.pad(jnp.concatenate([seen, seen], axis=1), ((0, 14), (0, 0)))
-    kv_own, kv_other = pack(side.reshape(1), cache_keys, cache_values, seen)
-    kv_other = lax.ppermute(kv_other, "xl", [(0, 1), (1, 0)])
-    kv = jnp.stack([kv_own, kv_other])
+    kv = jnp.concatenate(
+        [
+            by_head(cache_keys),
+            by_head(cache_values),
+            jnp.broadcast_to(seen[None], (2, *seen.shape)),
+        ],
+        axis=1,
+    )
+    kv = swapped(kv, "xl")
     kv = (kv, from_neighbour(kv))
     values_t = turn(kv)
 
-    w_columns = jnp.where(
-        side == 0,
-        jnp.concatenate([first, second], axis=0),
-        jnp.concatenate([second, first], axis=0),
-    )
-    w_out_full = lax.all_gather(w_columns, "z", axis=0, tiled=False)
-
-    w_full, values_t = lax.optimization_barrier((w_full, values_t))
+    w_full, values_t, features = lax.optimization_barrier((w_full, values_t, features))
     queries = project(features, w_full, 2, HD, (16, 64, HD))
     queries = swapped(queries, "z").reshape(-1, HD)
     new = project(features, w_full, 0, 2 * HD, (320, HD))
     fresh = (new, from_neighbour(new))
     parts = attend(queries, kv, values_t, fresh)
     parts = swapped(parts, "z")
-    attention = swapped(combine(parts), (*WIDE, "xl"))
+    parts = swapped(output_projection(combine(parts), w_full), (*WIDE, "xl"))
 
     finished = new.reshape(2, 2, 80, HD)[:, :, 64:]
     mine = jnp.where(side == 0, finished[:, 0], finished[:, 1])
@@ -376,7 +369,7 @@
     )
     new_keys, new_values = finished[0], finished[1]
 
-    y, y_squares = output_projection(attention, w_out_full)
+    y, y_squares = over_heads(parts)
     y_squares = swapped(y_squares, WIDE).sum(axis=(0, 1))
     velocity = y * lax.rsqrt(y_squares / D + EPSILON)[:, None] * out_gain[None, :]
     new_state = state + (following - current)[:, None, None] * velocity.reshape(

time: 249 us -> 238 us (0.956)
  starting transfers between devices: 73.4 us -> 55.2 us
  waiting for transfers between devices: 72.7 us -> 82.1 us
  other arithmetic: 9.44 us -> 4.1 us
    ppermute x3 -> x0, waiting for transfers between devices: 26.2 us -> none  [the longest x2 21.8 us: to_owners(): return lax.ppermute(array, ('y', 'xl', 'z', 'xh', 'core'), pairs)]
    all_gather x2 -> x1, waiting for transfers between devices: 6.86 us -> 28.4 us  [local(): w_full = lax.all_gather(shard, 'z', axis=0, tiled=False)]
    ppermute x2, waiting for transfers between devices: 21.4 us -> 5.15 us  [from_neighbour(): return lax.ppermute(array, 'z', [(z, z ^ 1) for z in range(16)])]
    ppermute x3 -> x0, starting transfers between devices: 14.5 us -> none  [the longest x2 9.81 us: to_owners(): return lax.ppermute(array, ('y', 'xl', 'z', 'xh', 'core'), pairs)]
    ppermute x1, waiting for transfers between devices: 4.01 us -> 16.2 us  [local(): other = lax.ppermute(other, 'xl', [(0, 1), (1, 0)])]
    all_to_all x3 -> x2, waiting for transfers between devices: 5.27 us -> 17.4 us  [sent_to_all(): lax.all_to_all(jnp.broadcast_to(array[None], (devices, *array.shape)), ax...]
    all_to_all x0 -> x1, blocking collectives: none -> 8.69 us  [sent_to_all(): lax.all_to_all(jnp.broadcast_to(array[None], (devices, *array.shape)), ax...]
    all_to_all x2, blocking collectives: 41.1 us -> 34.5 us  [swapped(): return lax.all_to_all(blocks, axis, 0, 0, tiled=True)]
  transfers between devices with their start and end apart: 14 -> 10, of which waited for: 11 -> 9; matrix products, arithmetic and copies ran while one was open for 5% -> 2% of each run, Pallas kernels for 10% -> 4%
where the time goes in v6:
time: 238 us; the launch traced here: 237 us
  waiting for transfers between devices  82.1 us (34%)
  starting transfers between devices  55.2 us (23%)
  blocking collectives  43.2 us (18%)
  Pallas kernels  29.3 us (12%)
  between operations  14.3 us (6%)
  local copies, waits for them, and re-layouts  8.34 us (4%)
  other arithmetic  4.1 us (2%)
    all_to_all x2, blocking collectives, swapped(): return lax.all_to_all(blocks, axis, 0, 0, tiled=True)  34.5 us
    all_to_all x4, starting transfers between devices, swapped(): return lax.all_to_all(blocks, axis, 0, 0, tiled=True)  31.9 us
    all_gather x1, waiting for transfers between devices, local(): w_full = lax.all_gather(shard, 'z', axis=0, tiled=False)  28.4 us
    all_to_all x2, waiting for transfers between devices, sent_to_all(): lax.all_to_all(jnp.broadcast_to(array[None], (devices, *array.shape)), ax...  17.4 us
    ppermute x1, waiting for transfers between devices, local(): other = lax.ppermute(other, 'xl', [(0, 1), (1, 0)])  16.2 us
    all_to_all x4, waiting for transfers between devices, swapped(): return lax.all_to_all(blocks, axis, 0, 0, tiled=True)  14.9 us
    all_to_all x2, starting transfers between devices, sent_to_all(): lax.all_to_all(jnp.broadcast_to(array[None], (devices, *array.shape)), ax...  14.4 us
    all_to_all x1, blocking collectives, sent_to_all(): lax.all_to_all(jnp.broadcast_to(array[None], (devices, *array.shape)), ax...  8.69 us
  transfers between devices with their start and end apart: 10, of which 9 were waited for; matrix products, arithmetic and copies ran while one was open for 2% of the time, Pallas kernels for 4%

profile of v6, /device:TPU:1, one launch (start us, length us, event | category | flops | bytes accessed | tf_op | source)
XLA Modules:
  0.0 236.6 jit_solution(3448900696901534693)
XLA Ops:
  9.9 8.0 %all_to_all.46 = bf16[2,160,512]{2,1,0:T(8,128)(2,1)} all-to-all(bf16[2,160,512]{2,1,0:T(8,128)(2,1)S(1)} %pad_maximum_fusion.1), channel_id=1, replica_groups=mesh['y'=4,'xl'=2,'z'=16,'xh'=2,'core'=2] {'xl'}, dimensions={0} | all-to-all | bytes 655360 | tf_op jit(solution)/shard_map/all_to_all | solution.py:38
  18.8 10.7 %all-to-all-start.2 = ((f32[16,1,80]{2,1,0:T(1,128)}), f32[16,1,80]{2,1,0:T(1,128)S(1)}, u32[]{:S(2)}, u32[]{:S(2)}) async-start(f32[16,1,80]{2,1,0:T(1,128)} %broadcast_in_dim.14), calls=%async_computation.2 | async-start | bytes 16384 | tf_op jit(solution)/shard_map/all_to_all | solution.py:32
  31.4 5.1 %all-to-all-done.2 = f32[16,1,80]{2,1,0:T(1,128)S(1)} async-done(((f32[16,1,80]{2,1,0:T(1,128)}), f32[16,1,80]{2,1,0:T(1,128)S(1)}, u32[]{:S(2)}, u32[]{:S(2)}) %all-to-all-start.2) | async-done | bytes 5152 | tf_op jit(solution)/shard_map/all_to_all | solution.py:32
  36.5 3.5 %all-to-all-start.1 = ((bf16[2,1040,128]{2,1,0:T(8,128)(2,1)}), bf16[2,1040,128]{2,1,0:T(8,128)(2,1)S(1)}, u32[]{:S(2)}, u32[]{:S(2)}) async-start(bf16[2,1040,128]{2,1,0:T(8,128)(2,1)} %pad_maximum_fusion), calls=%async_computation.1 | async-start | bytes 1064960 | tf_op jit(solution)/shard_map/all_to_all | solution.py:38
  40.1 7.4 %all-to-all-done.1.own_ref = bf16[2,1040,128]{2,1,0:T(8,128)(2,1)S(1)} async-done(((bf16[2,1040,128]{2,1,0:T(8,128)(2,1)}), bf16[2,1040,128]{2,1,0:T(8,128)(2,1)S(1)}, u32[]{:S(2)}, u32[]{:S(2)}) %all-to-all-start.1) | async-done | bytes 532512 | tf_op jit(solution)/shard_map/all_to_all | solution.py:38
  48.7 3.6 %all-to-all-start.3 = ((bf16[16,80,320]{2,1,0:T(8,128)(2,1)}), bf16[16,80,320]{2,1,0:T(8,128)(2,1)S(1)}, u32[]{:S(2)}, u32[]{:S(2)}) async-start(bf16[16,80,320]{2,1,0:T(8,128)(2,1)} %broadcast_in_dim.16), calls=%async_computation.3 | async-start | bytes 1966080 | tf_op jit(solution)/shard_map/all_to_all | solution.py:32
  52.3 2.4 %collective-permute-start = (bf16[2,1040,128]{2,1,0:T(8,128)(2,1)S(1)}, bf16[2,1040,128]{2,1,0:T(8,128)(2,1)S(1)}, u32[]{:S(2)}, u32[]{:S(2)}) collective-permute-start(bf16[2,1040,128]{2,1,0:T(8,128)(2,1)S(1)} %all-to-all-done.1.own_ref), channel_id=1, source_target_pairs={{0,4},{4,0},{8,12},{12,8},{16,20},{20,16},{24,28},{28,24},{32,36},... | collective-permute-start | bytes 1597448 | tf_op jit(solution)/shard_map/ppermute | solution.py:286
  54.8 12.3 %all-to-all-done.3 = bf16[16,80,320]{2,1,0:T(8,128)(2,1)S(1)} async-done(((bf16[16,80,320]{2,1,0:T(8,128)(2,1)}), bf16[16,80,320]{2,1,0:T(8,128)(2,1)S(1)}, u32[]{:S(2)}, u32[]{:S(2)}) %all-to-all-start.3) | async-done | bytes 819232 | tf_op jit(solution)/shard_map/all_to_all | solution.py:32
  67.3 8.7 %all_to_all.47 = bf16[2,16,80,320]{3,2,1,0:T(8,128)(2,1)} all-to-all(bf16[2,16,80,320]{3,2,1,0:T(8,128)(2,1)S(1)} %broadcast_in_dim.17), channel_id=1, replica_groups=mesh['y'=4,'xl'=2,'z'=16,'xh'=2,'core'=2] {'core'}, dimensions={0} | all-to-all | bytes 3276800 | tf_op jit(solution)/shard_map/all_to_all | solution.py:32
  76.0 3.3 %shard_map.167.h_ref = bf16[160,5120]{1,0:T(8,128)(2,1)} custom-call(bf16[2,4,2,2,80,320]{5,4,3,2,1,0:T(8,128)(2,1)} %bitcast.56), custom_call_target="tpu_custom_call" | custom-call | bytes 4194304 | tf_op jit(solution)/shard_map/pallas_call | solution.py:53
  82.3 28.4 %all-gather.2.cloned.1.call-done.w_ref = bf16[16,320,512]{2,1,0:T(8,128)(2,1)} async-done(((bf16[1,320,512]{2,1,0:T(8,128)(2,1)}), bf16[16,320,512]{2,1,0:T(8,128)(2,1)}) %all-gather.2.cloned.1.call-update) | async-done | bytes 5242896 | tf_op jit(solution)/shard_map/all_gather | solution.py:313
  110.7 3.9 %shard_map.168 = bf16[16,64,128]{2,1,0:T(8,128)(2,1)} custom-call(bf16[160,5120]{1,0:T(8,128)(2,1)} %shard_map.167.h_ref, bf16[16,320,512]{2,1,0:T(8,128)(2,1)} %all-gather.2.cloned.1.call-done.w_ref), custom_call_target="tpu_custom_call" | custom-call | flops 209715200 | bytes 4194304 | tf_op jit(solution)/shard_map/pallas_call | solution.py:89
  114.6 6.8 %all-to-all-start.5 = ((bf16[16,64,128]{2,1,0:T(8,128)(2,1)}), bf16[16,64,128]{2,1,0:T(8,128)(2,1)S(1)}, u32[]{:S(2)}, u32[]{:S(2)}) async-start(bf16[16,64,128]{2,1,0:T(8,128)(2,1)} %shard_map.168), calls=%async_computation.5 | async-start | bytes 524288 | tf_op jit(solution)/shard_map/all_to_all | solution.py:38
  121.4 4.2 %shard_map.169.own_new = bf16[320,128]{1,0:T(8,128)(2,1)} custom-call(bf16[160,5120]{1,0:T(8,128)(2,1)} %shard_map.167.h_ref, bf16[16,320,512]{2,1,0:T(8,128)(2,1)} %all-gather.2.cloned.1.call-done.w_ref), custom_call_target="tpu_custom_call" | custom-call | flops 419430400 | bytes 4194304 | tf_op jit(solution)/shard_map/pallas_call | solution.py:89
  125.6 3.3 %collective-permute-start.1 = (bf16[320,128]{1,0:T(8,128)(2,1)}, bf16[320,128]{1,0:T(8,128)(2,1)S(1)}, u32[]{:S(2)}, u32[]{:S(2)}) collective-permute-start(bf16[320,128]{1,0:T(8,128)(2,1)} %shard_map.169.own_new), channel_id=1, source_target_pairs={{0,4},{4,0},{8,12},{12,8},{16,20},{20,16},{24,28},{28,24},{32,36},... | collective-permute-start | bytes 245768 | tf_op jit(solution)/shard_map/ppermute | solution.py:286
  128.9 5.1 %collective-permute-done.1.other_new = bf16[320,128]{1,0:T(8,128)(2,1)S(1)} collective-permute-done((bf16[320,128]{1,0:T(8,128)(2,1)}, bf16[320,128]{1,0:T(8,128)(2,1)S(1)}, u32[]{:S(2)}, u32[]{:S(2)}) %collective-permute-start.1) | collective-permute-done | bytes 81952 | tf_op jit(solution)/shard_map/ppermute | solution.py:286
  135.0 8.7 %shard_map.170 = bf16[16,80,128]{2,1,0:T(8,128)(2,1)} custom-call(bf16[1024,128]{1,0:T(8,128)(2,1)} %bitcast.61, bf16[2,1040,128]{2,1,0:T(8,128)(2,1)} %copy-done.2, bf16[2,1040,128]{2,1,0:T(8,128)(2,1)} %copy-done.4, bf16[2,2,144,512]{3,2,1,0:T(8,128)(2,1)} %shard_map.166.vt_ref, bf16[320,128]{1,0:T(8,128)(2,1)} %shard_map.169.own_new, ...), custom_call_target="tpu_custom_call" | custom-call | flops 1241513984 | bytes 3145728 | tf_op jit(solution)/shard_map/pallas_call | solution.py:193
  143.7 26.4 %all_to_all.48.in_ref = bf16[16,80,128]{2,1,0:T(8,128)(2,1)} all-to-all(bf16[16,80,128]{2,1,0:T(8,128)(2,1)} %shard_map.170), channel_id=1, replica_groups=mesh['y'=4,'xl'=2,'z'=16,'xh'=2,'core'=2] {'z'}, dimensions={0} | all-to-all | bytes 655360 | tf_op jit(solution)/shard_map/all_to_all | solution.py:38
  172.1 2.8 %shard_map.172 = bf16[32,64,320]{2,1,0:T(8,128)(2,1)} custom-call(bf16[128,128]{1,0:T(8,128)(2,1)} %shard_map.171.att_ref, bf16[16,320,512]{2,1,0:T(8,128)(2,1)} %all-gather.2.cloned.1.call-done.w_ref), custom_call_target="tpu_custom_call" | custom-call | tf_op jit(solution)/shard_map/pallas_call | solution.py:251
  174.9 15.0 %all-to-all-start.7 = ((bf16[32,64,320]{2,1,0:T(8,128)(2,1)}), bf16[32,64,320]{2,1,0:T(8,128)(2,1)S(1)}, u32[]{:S(2)}, u32[]{:S(2)}) async-start(bf16[32,64,320]{2,1,0:T(8,128)(2,1)} %shard_map.172), calls=%async_computation.7 | async-start | bytes 3145728 | tf_op jit(solution)/shard_map/all_to_all | solution.py:38
  190.7 3.3 %collective-permute-start.2 = (bf16[2,16,128]{2,1,0:T(8,128)(2,1)S(1)}, bf16[2,16,128]{2,1,0:T(8,128)(2,1)S(1)}, u32[]{:S(2)}, u32[]{:S(2)}) collective-permute-start(bf16[2,16,128]{2,1,0:T(8,128)(2,1)S(1)} %get-tuple-element.20), channel_id=1, source_target_pairs={{0,64},{64,0},{1,65},{65,1},{2,66},{66,2},{3,67},{67,3},{4,68},{68... | collective-permute-start | bytes 24584 | tf_op jit(solution)/shard_map/ppermute | solution.py:364
  194.0 16.2 %collective-permute-done.2 = bf16[2,16,128]{2,1,0:T(8,128)(2,1)S(1)} collective-permute-done((bf16[2,16,128]{2,1,0:T(8,128)(2,1)S(1)}, bf16[2,16,128]{2,1,0:T(8,128)(2,1)S(1)}, u32[]{:S(2)}, u32[]{:S(2)}) %collective-permute-start.2) | collective-permute-done | bytes 8224 | tf_op jit(solution)/shard_map/ppermute | solution.py:364
  214.5 6.5 %all-to-all-start.8 = ((f32[16,1,64]{2,1,0:T(1,128)}), f32[16,1,64]{2,1,0:T(1,128)S(1)}, u32[]{:S(2)}, u32[]{:S(2)}) async-start(f32[16,1,64]{2,1,0:T(1,128)} %get-tuple-element.12), calls=%async_computation.8 | async-start | bytes 16384 | tf_op jit(solution)/shard_map/all_to_all | solution.py:38
  221.6 6.4 %all-to-all-done.8 = f32[16,1,64]{2,1,0:T(1,128)S(1)} async-done(((f32[16,1,64]{2,1,0:T(1,128)}), f32[16,1,64]{2,1,0:T(1,128)S(1)}, u32[]{:S(2)}, u32[]{:S(2)}) %all-to-all-start.8) | async-done | bytes 4128 | tf_op jit(solution)/shard_map/all_to_all | solution.py:38
  (76 shorter events, 20.2 us)
Async XLA Ops:
  7.2 0.9 copy-start
  7.2 103.5 %all-gather.2.cloned.1.call-start = ((), (), s32[]{:S(2)}) async-start(), calls=%async_computation.9 | async-start | bytes 5570560 | tf_op jit(solution)/shard_map/all_gather | solution.py:313
  8.1 9.9 %copy-start.8 = (bf16[16,320]{1,0:T(8,128)(2,1)S(1)}, bf16[16,320]{1,0:T(8,128)(2,1)}, u32[]{:S(2)}) copy-start(bf16[16,320]{1,0:T(8,128)(2,1)} %param.16) | copy-start | bytes 30724
  8.1 10.0 %copy-start.3 = (f32[4,16,320]{2,1,0:T(8,128)S(1)}, f32[4,16,320]{2,1,0:T(8,128)}, u32[]{:S(2)}) copy-start(f32[4,16,320]{2,1,0:T(8,128)} %param.15) | copy-start | bytes 245764
  8.9 20.6 %copy-start.16 = (s32[2]{0:T(128)S(1)}, s32[2]{0:T(128)}, u32[]{:S(2)}) copy-start(s32[2]{0:T(128)} %param.28) | copy-start | bytes 28
  8.9 20.6 %copy-start.12 = (s32[4,64]{1,0:T(4,128)S(1)}, s32[4,64]{1,0:T(4,128)}, u32[]{:S(2)}) copy-start(s32[4,64]{1,0:T(4,128)} %param.29) | copy-start | bytes 3076
  8.9 21.0 %copy-start.14 = (s32[4]{0:T(128)S(1)}, s32[4]{0:T(128)}, u32[]{:S(2)}) copy-start(s32[4]{0:T(128)} %param.27) | copy-start | bytes 52
  8.9 21.0 %copy-start.6 = (bf16[512,256]{1,0:T(8,128)(2,1)S(1)}, bf16[512,256]{1,0:T(8,128)(2,1)}, u32[]{:S(2)}) copy-start(bf16[512,256]{1,0:T(8,128)(2,1)} %param.22) | copy-start | bytes 786436
  9.0 21.0 %copy-start.7 = (bf16[512,256]{1,0:T(8,128)(2,1)S(1)}, bf16[512,256]{1,0:T(8,128)(2,1)}, u32[]{:S(2)}) copy-start(bf16[512,256]{1,0:T(8,128)(2,1)} %param.21) | copy-start | bytes 786436
  18.8 17.7 %all-to-all-start.2 = ((f32[16,1,80]{2,1,0:T(1,128)}), f32[16,1,80]{2,1,0:T(1,128)S(1)}, u32[]{:S(2)}, u32[]{:S(2)}) async-start(f32[16,1,80]{2,1,0:T(1,128)} %broadcast_in_dim.14), calls=%async_computation.2 | async-start | bytes 16384 | tf_op jit(solution)/shard_map/all_to_all | solution.py:32
  30.0 1.0 copy-start.13
  30.1 9.9 %copy-start.9 = (f32[320]{0:T(512)S(1)}, f32[320]{0:T(512)}, u32[]{:S(2)}) copy-start(f32[320]{0:T(512)} %param.24) | copy-start | bytes 3844
  30.1 9.9 %copy-start.10 = (f32[320]{0:T(512)S(1)}, f32[320]{0:T(512)}, u32[]{:S(2)}) copy-start(f32[320]{0:T(512)} %param.23) | copy-start | bytes 3844
  36.5 11.1 %all-to-all-start.1 = ((bf16[2,1040,128]{2,1,0:T(8,128)(2,1)}), bf16[2,1040,128]{2,1,0:T(8,128)(2,1)S(1)}, u32[]{:S(2)}, u32[]{:S(2)}) async-start(bf16[2,1040,128]{2,1,0:T(8,128)(2,1)} %pad_maximum_fusion), calls=%async_computation.1 | async-start | bytes 1064960 | tf_op jit(solution)/shard_map/all_to_all | solution.py:38
  47.5 4.8 %copy-start.2 = (bf16[2,1040,128]{2,1,0:T(8,128)(2,1)}, bf16[2,1040,128]{2,1,0:T(8,128)(2,1)S(1)}, u32[]{:S(2)}) copy-start(bf16[2,1040,128]{2,1,0:T(8,128)(2,1)S(1)} %all-to-all-done.1.own_ref) | copy-start | bytes 1597444
  48.7 18.4 %all-to-all-start.3 = ((bf16[16,80,320]{2,1,0:T(8,128)(2,1)}), bf16[16,80,320]{2,1,0:T(8,128)(2,1)S(1)}, u32[]{:S(2)}, u32[]{:S(2)}) async-start(bf16[16,80,320]{2,1,0:T(8,128)(2,1)} %broadcast_in_dim.16), calls=%async_computation.3 | async-start | bytes 1966080 | tf_op jit(solution)/shard_map/all_to_all | solution.py:32
  52.3 26.9 %collective-permute-start = (bf16[2,1040,128]{2,1,0:T(8,128)(2,1)S(1)}, bf16[2,1040,128]{2,1,0:T(8,128)(2,1)S(1)}, u32[]{:S(2)}, u32[]{:S(2)}) collective-permute-start(bf16[2,1040,128]{2,1,0:T(8,128)(2,1)S(1)} %all-to-all-done.1.own_ref), channel_id=1, source_target_pairs={{0,4},{4,0},{8,12},{12,8},{16,20},{20,16},{24,28},{28,24},{32,36},... | collective-permute-start | bytes 1597448 | tf_op jit(solution)/shard_map/ppermute | solution.py:286
  114.6 19.7 %all-to-all-start.5 = ((bf16[16,64,128]{2,1,0:T(8,128)(2,1)}), bf16[16,64,128]{2,1,0:T(8,128)(2,1)S(1)}, u32[]{:S(2)}, u32[]{:S(2)}) async-start(bf16[16,64,128]{2,1,0:T(8,128)(2,1)} %shard_map.168), calls=%async_computation.5 | async-start | bytes 524288 | tf_op jit(solution)/shard_map/all_to_all | solution.py:38
  125.6 8.4 %collective-permute-start.1 = (bf16[320,128]{1,0:T(8,128)(2,1)}, bf16[320,128]{1,0:T(8,128)(2,1)S(1)}, u32[]{:S(2)}, u32[]{:S(2)}) collective-permute-start(bf16[320,128]{1,0:T(8,128)(2,1)} %shard_map.169.own_new), channel_id=1, source_target_pairs={{0,4},{4,0},{8,12},{12,8},{16,20},{20,16},{24,28},{28,24},{32,36},... | collective-permute-start | bytes 245768 | tf_op jit(solution)/shard_map/ppermute | solution.py:286
  174.9 36.2 %all-to-all-start.7 = ((bf16[32,64,320]{2,1,0:T(8,128)(2,1)}), bf16[32,64,320]{2,1,0:T(8,128)(2,1)S(1)}, u32[]{:S(2)}, u32[]{:S(2)}) async-start(bf16[32,64,320]{2,1,0:T(8,128)(2,1)} %shard_map.172), calls=%async_computation.7 | async-start | bytes 3145728 | tf_op jit(solution)/shard_map/all_to_all | solution.py:38
  189.9 38.1 %copy-start.11 = (f32[320]{0:T(512)S(1)}, f32[320]{0:T(512)}, u32[]{:S(2)}) copy-start(f32[320]{0:T(512)} %param.25) | copy-start | bytes 3844
  190.7 19.5 %collective-permute-start.2 = (bf16[2,16,128]{2,1,0:T(8,128)(2,1)S(1)}, bf16[2,16,128]{2,1,0:T(8,128)(2,1)S(1)}, u32[]{:S(2)}, u32[]{:S(2)}) collective-permute-start(bf16[2,16,128]{2,1,0:T(8,128)(2,1)S(1)} %get-tuple-element.20), channel_id=1, source_target_pairs={{0,64},{64,0},{1,65},{65,1},{2,66},{66,2},{3,67},{67,3},{4,68},{68... | collective-permute-start | bytes 24584 | tf_op jit(solution)/shard_map/ppermute | solution.py:364
  211.1 1.2 copy-start.1
  214.5 13.5 %all-to-all-start.8 = ((f32[16,1,64]{2,1,0:T(1,128)}), f32[16,1,64]{2,1,0:T(1,128)S(1)}, u32[]{:S(2)}, u32[]{:S(2)}) async-start(f32[16,1,64]{2,1,0:T(1,128)} %get-tuple-element.12), calls=%async_computation.8 | async-start | bytes 16384 | tf_op jit(solution)/shard_map/all_to_all | solution.py:38
  (3 other events, 2.2 us)
Sparse Core Ops, SparseCore 0:
  18.1 92.5 all-gather.1

commit v7 on v6

--- a/solution.py
+++ b/solution.py
@@ -109,11 +109,12 @@
     return [high, middle, value - high - middle]
 
 
-def turn_kernel(own_ref, other_ref, out_ref):
+def turn_kernel(kv_ref, out_ref):
     ones = (lax.broadcasted_iota(jnp.int32, (16, 512), 0) == 0).astype(F32).astype(BF16)
-    for i, ref in enumerate((own_ref, other_ref)):
+    for i in range(2):
         for side in range(2):
-            out_ref[i, side, 0:HD] = ref[side, 512:1024, :].astype(F32).T.astype(BF16)
+            values = kv_ref[side, i, 512:1024, :].astype(F32)
+            out_ref[i, side, 0:HD] = values.T.astype(BF16)
             out_ref[i, side, HD : HD + 16] = ones
 
 
@@ -123,10 +124,10 @@
         out_shape=jax.ShapeDtypeStruct((2, 2, HD + 16, 512), BF16),
         compiler_params=pltpu.CompilerParams(vmem_limit_bytes=VMEM_LIMIT),
         cost_estimate=pl.CostEstimate(flops=0, bytes_accessed=2**20, transcendentals=0),
-    )(*kv)
-
-
-def attend_kernel(q_ref, own_ref, other_ref, vt_ref, own_new, other_new, out_ref, fresh_vt):
+    )(kv)
+
+
+def attend_kernel(q_ref, kv_ref, vt_ref, own_new, other_new, out_ref, fresh_vt):
     @pl.when(pl.program_id(0) == 0)
     def _():
         ones = (lax.broadcasted_iota(jnp.int32, (16, 160), 0) == 0).astype(F32)
@@ -148,14 +149,14 @@
     visible = (token >= 64) | ((token >> 4) <= ((lane & 63) >> 4))
 
     parts, values = [], []
-    for i, (kv_ref, new) in enumerate(((own_ref, own_new), (other_ref, other_new))):
+    for i, new in enumerate((own_new, other_new)):
         for side in range(2):
-            seen = kv_ref[side, 1024:1040, :].astype(F32)
+            seen = kv_ref[side, i, 1024:1040, :].astype(F32)
             hidden = jnp.where(seen > 0.5, 0.0, -jnp.inf)
             hidden = jnp.concatenate([hidden] * (lanes // HD), axis=1)
             for slot in range(2):
                 at = slice(slot * SLOT, (slot + 1) * SLOT)
-                parts.append(products(kv_ref[side, at, :]) + hidden[slot : slot + 1, :])
+                parts.append(products(kv_ref[side, i, at, :]) + hidden[slot : slot + 1, :])
                 values.append(vt_ref[i, side, :, at])
         parts.append(jnp.where(visible, products(new[0:160, :]), -jnp.inf))
         values.append(fresh_vt[i])
@@ -185,7 +186,7 @@
 def attend(queries, kv, values_t, fresh):
     step = 256
     rows = queries.shape[0]
-    arrays = (*kv, values_t, *fresh)
+    arrays = (kv, values_t, *fresh)
 
     def whole(array):
         return pl.BlockSpec(array.shape, lambda s: (0,) * array.ndim)
@@ -243,8 +244,13 @@
         part = lax.dot_general(
             attention, weights, (((1,), (1,)), ((), ())), preferred_element_type=F32
         ).astype(BF16)
-        out_ref[2 * m] = part[0:64]
-        out_ref[2 * m + 1] = part[64:128]
+        for xl in range(2):
+            block, at = part[64 * xl : 64 * (xl + 1)], 2 * m + xl
+            out_ref[at, 0:64] = block[:, 0:HD]
+            out_ref[at, 64:128] = block[:, HD : 2 * HD]
+            out_ref[at, 128:160] = jnp.concatenate(
+                [block[0:32, 2 * HD :], block[32:64, 2 * HD :]], axis=1
+            )
 
 
 def output_projection(attention, weights):
@@ -253,10 +259,10 @@
         grid=(2,),
         in_specs=[
             pl.BlockSpec((HD, HD), lambda s: (0, 0)),
-            pl.BlockSpec((16, 160, HD), lambda s: (0, s, 3)),
+            pl.BlockSpec((16, 160, HD), lambda s: (0, s, 0)),
         ],
-        out_specs=pl.BlockSpec((16, 64, 320), lambda s: (s, 0, 0)),
-        out_shape=jax.ShapeDtypeStruct((32, 64, 320), BF16),
+        out_specs=pl.BlockSpec((16, 160, HD), lambda s: (s, 0, 0)),
+        out_shape=jax.ShapeDtypeStruct((32, 160, HD), BF16),
         compiler_params=pltpu.CompilerParams(vmem_limit_bytes=VMEM_LIMIT),
     )(attention, weights)
 
@@ -265,8 +271,10 @@
     total = in_ref[0].astype(F32)
     for i in range(1, in_ref.shape[0]):
         total = total + in_ref[i].astype(F32)
-    y_ref[...] = total
-    squares = jnp.sum((total * total).T, axis=0, keepdims=True)
+    last = jnp.concatenate([total[128:160, 0:64], total[128:160, 64:128]], axis=0)
+    y = jnp.concatenate([total[0:64], total[64:128], last], axis=1)
+    y_ref[...] = y
+    squares = jnp.sum((y * y).T, axis=0, keepdims=True)
     for i in range(16):
         square_ref[i] = squares
 
@@ -306,11 +314,14 @@
     flight, ch_dev, width = state.shape
     rows_count = flight * ch_dev
 
+    near_keys, near_values = from_neighbour(cache_keys), from_neighbour(cache_values)
+
     side = lax.axis_index("xl")
-    parts = [by_head(w) for w in (w_key, w_value, w_query)]
-    parts.append(jnp.transpose(w_out.reshape(2, HD, 160), (0, 2, 1)))
-    shard = swapped(jnp.concatenate(parts, axis=2), "xl").reshape(320, 4 * HD)
-    w_full = lax.all_gather(shard, "z", axis=0, tiled=False)
+    w_heads = jnp.concatenate([by_head(w) for w in (w_key, w_value, w_query)], axis=2)
+    w_heads, w_out, near_keys, near_values = lax.optimization_barrier(
+        (swapped(w_heads, "xl"), w_out, near_keys, near_values)
+    )
+    w_full = lax.all_gather(w_heads.reshape(320, 3 * HD), "z", axis=0, tiled=False)
 
     current = level_lookup(levels, noise_index)
     following = level_lookup(levels, noise_index + 1)
@@ -342,12 +353,24 @@
             by_head(cache_keys),
             by_head(cache_values),
             jnp.broadcast_to(seen[None], (2, *seen.shape)),
+            by_head(near_keys),
+            by_head(near_values),
+            jnp.broadcast_to(from_neighbour(seen)[None], (2, *seen.shape)),
         ],
         axis=1,
     )
-    kv = swapped(kv, "xl")
-    kv = (kv, from_neighbour(kv))
+    kv = swapped(kv, "xl").reshape(2, 2, 1040, HD)
     values_t = turn(kv)
+
+    low, high = jnp.transpose(w_out[:HD]), jnp.transpose(w_out[HD:])
+    mine = jnp.where(side == 0, low, high)
+    other = lax.ppermute(jnp.where(side == 0, high, low), "xl", [(0, 1), (1, 0)])
+    w_columns = jnp.where(
+        side == 0,
+        jnp.concatenate([mine, other], axis=0),
+        jnp.concatenate([other, mine], axis=0),
+    )
+    w_out_full = lax.all_gather(w_columns, "z", axis=0, tiled=False)
 
     w_full, values_t, features = lax.optimization_barrier((w_full, values_t, features))
     queries = project(features, w_full, 2, HD, (16, 64, HD))
@@ -356,7 +379,7 @@
     fresh = (new, from_neighbour(new))
     parts = attend(queries, kv, values_t, fresh)
     parts = swapped(parts, "z")
-    parts = swapped(output_projection(combine(parts), w_full), (*WIDE, "xl"))
+    parts = swapped(output_projection(combine(parts), w_out_full), (*WIDE, "xl"))
 
     finished = new.reshape(2, 2, 80, HD)[:, :, 64:]
     mine = jnp.where(side == 0, finished[:, 0], finished[:, 1])

time: 238 us -> 239 us (level)
  waiting for transfers between devices: 82.1 us -> 64.3 us
  starting transfers between devices: 55.2 us -> 69.2 us
  other arithmetic: 4.1 us -> 6.8 us
    all_gather x1 -> x2, waiting for transfers between devices: 28.4 us -> 5.8 us  [the longest x1 5.02 us: local(): w_out_full = lax.all_gather(w_columns, 'z', axis=0, tiled=False)]
    ppermute x0 -> x1, waiting for transfers between devices: none -> 11.1 us  [local(): lax.ppermute(jnp.where(side == 0, high, low), 'xl', [(0, 1), (1, 0)])]
    ppermute x2 -> x4, starting transfers between devices: 5.68 us -> 13 us  [from_neighbour(): return lax.ppermute(array, 'z', [(z, z ^ 1) for z in range(16)])]
    all_to_all x4, waiting for transfers between devices: 14.9 us -> 8.06 us  [swapped(): return lax.all_to_all(blocks, axis, 0, 0, tiled=True)]
    all_to_all x4, starting transfers between devices: 31.9 us -> 36.3 us  [swapped(): return lax.all_to_all(blocks, axis, 0, 0, tiled=True)]
    ppermute x2 -> x4, waiting for transfers between devices: 5.15 us -> 8.94 us  [from_neighbour(): return lax.ppermute(array, 'z', [(z, z ^ 1) for z in range(16)])]
    ppermute x1, waiting for transfers between devices: 16.2 us -> 12.4 us  [local(): other = lax.ppermute(other, 'xl', [(0, 1), (1, 0)])]
    ppermute x0 -> x1, starting transfers between devices: none -> 3.29 us  [local(): lax.ppermute(jnp.where(side == 0, high, low), 'xl', [(0, 1), (1, 0)])]
  transfers between devices with their start and end apart: 10 -> 14, of which waited for: 9 -> 9; matrix products, arithmetic and copies ran while one was open for 2% -> 5% of each run, Pallas kernels for 4% -> 10%
where the time goes in v7:
time: 239 us; the launch traced here: 238 us
  starting transfers between devices  69.2 us (29%)
  waiting for transfers between devices  64.3 us (27%)
  blocking collectives  45.4 us (19%)
  Pallas kernels  29.1 us (12%)
  between operations  14.4 us (6%)
  local copies, waits for them, and re-layouts  8.52 us (4%)
  other arithmetic  6.8 us (3%)
    all_to_all x2, blocking collectives, swapped(): return lax.all_to_all(blocks, axis, 0, 0, tiled=True)  37.6 us
    all_to_all x4, starting transfers between devices, swapped(): return lax.all_to_all(blocks, axis, 0, 0, tiled=True)  36.3 us
    all_to_all x2, waiting for transfers between devices, sent_to_all(): lax.all_to_all(jnp.broadcast_to(array[None], (devices, *array.shape)), ax...  17.9 us
    all_to_all x2, starting transfers between devices, sent_to_all(): lax.all_to_all(jnp.broadcast_to(array[None], (devices, *array.shape)), ax...  13.2 us
    ppermute x4, starting transfers between devices, from_neighbour(): return lax.ppermute(array, 'z', [(z, z ^ 1) for z in range(16)])  13 us
    ppermute x1, waiting for transfers between devices, local(): other = lax.ppermute(other, 'xl', [(0, 1), (1, 0)])  12.4 us
    ppermute x1, waiting for transfers between devices, local(): lax.ppermute(jnp.where(side == 0, high, low), 'xl', [(0, 1), (1, 0)])  11.1 us
    ppermute x4, waiting for transfers between devices, from_neighbour(): return lax.ppermute(array, 'z', [(z, z ^ 1) for z in range(16)])  8.94 us
  transfers between devices with their start and end apart: 14, of which 9 were waited for; matrix products, arithmetic and copies ran while one was open for 5% of the time, Pallas kernels for 10%

profile of v7, /device:TPU:1, one launch (start us, length us, event | category | flops | bytes accessed | tf_op | source)
XLA Modules:
  0.0 237.7 jit_solution(16257392167828344550)
XLA Ops:
  7.3 4.5 %collective-permute-start = (bf16[512,256]{1,0:T(8,128)(2,1)}, bf16[512,256]{1,0:T(8,128)(2,1)S(1)}, u32[]{:S(2)}, u32[]{:S(2)}) collective-permute-start(bf16[512,256]{1,0:T(8,128)(2,1)} %param.21), channel_id=1, source_target_pairs={{0,4},{4,0},{8,12},{12,8},{16,20},{20,16},{24,28},{28,24},{32,36},... | collective-permute-start | bytes 786440 | tf_op jit(solution)/shard_map/ppermute | solution.py:294
  15.4 7.3 %all_to_all.46 = bf16[2,160,384]{2,1,0:T(8,128)(2,1)} all-to-all(bf16[2,160,384]{2,1,0:T(8,128)(2,1)S(1)} %maximum_maximum_fusion), channel_id=1, replica_groups=mesh['y'=4,'xl'=2,'z'=16,'xh'=2,'core'=2] {'xl'}, dimensions={0} | all-to-all | bytes 491520 | tf_op jit(solution)/shard_map/all_to_all | solution.py:38
  23.3 3.4 %collective-permute-start.2 = (bf16[16,128]{1,0:T(8,128)(2,1)S(1)}, bf16[16,128]{1,0:T(8,128)(2,1)S(1)}, u32[]{:S(2)}, u32[]{:S(2)}) collective-permute-start(bf16[16,128]{1,0:T(8,128)(2,1)S(1)} %fusion.2), channel_id=1, source_target_pairs={{0,4},{4,0},{8,12},{12,8},{16,20},{20,16},{24,28},{28,24},{32,36},... | collective-permute-start | bytes 12296 | tf_op jit(solution)/shard_map/ppermute | solution.py:294
  27.4 9.5 %all-to-all-start.2 = ((f32[16,1,80]{2,1,0:T(1,128)}), f32[16,1,80]{2,1,0:T(1,128)S(1)}, u32[]{:S(2)}, u32[]{:S(2)}) async-start(f32[16,1,80]{2,1,0:T(1,128)} %broadcast_in_dim.17), calls=%async_computation.2 | async-start | bytes 16384 | tf_op jit(solution)/shard_map/all_to_all | solution.py:32
  39.5 4.4 %all-to-all-done.2 = f32[16,1,80]{2,1,0:T(1,128)S(1)} async-done(((f32[16,1,80]{2,1,0:T(1,128)}), f32[16,1,80]{2,1,0:T(1,128)S(1)}, u32[]{:S(2)}, u32[]{:S(2)}) %all-to-all-start.2) | async-done | bytes 5152 | tf_op jit(solution)/shard_map/all_to_all | solution.py:32
  45.0 3.6 %all-to-all-start.3 = ((bf16[16,80,320]{2,1,0:T(8,128)(2,1)}), bf16[16,80,320]{2,1,0:T(8,128)(2,1)S(1)}, u32[]{:S(2)}, u32[]{:S(2)}) async-start(bf16[16,80,320]{2,1,0:T(8,128)(2,1)} %broadcast_in_dim.19), calls=%async_computation.3 | async-start | bytes 1966080 | tf_op jit(solution)/shard_map/all_to_all | solution.py:32
  50.8 13.5 %all-to-all-done.3 = bf16[16,80,320]{2,1,0:T(8,128)(2,1)S(1)} async-done(((bf16[16,80,320]{2,1,0:T(8,128)(2,1)}), bf16[16,80,320]{2,1,0:T(8,128)(2,1)S(1)}, u32[]{:S(2)}, u32[]{:S(2)}) %all-to-all-start.3) | async-done | bytes 819232 | tf_op jit(solution)/shard_map/all_to_all | solution.py:32
  64.4 7.9 %all_to_all.47 = bf16[2,16,80,320]{3,2,1,0:T(8,128)(2,1)} all-to-all(bf16[2,16,80,320]{3,2,1,0:T(8,128)(2,1)S(1)} %broadcast_in_dim.20), channel_id=1, replica_groups=mesh['y'=4,'xl'=2,'z'=16,'xh'=2,'core'=2] {'core'}, dimensions={0} | all-to-all | bytes 3276800 | tf_op jit(solution)/shard_map/all_to_all | solution.py:32
  72.3 3.7 %all-to-all-start.1 = ((bf16[2,2080,128]{2,1,0:T(8,128)(2,1)}), bf16[2,2080,128]{2,1,0:T(8,128)(2,1)S(1)}, u32[]{:S(2)}, u32[]{:S(2)}) async-start(bf16[2,2080,128]{2,1,0:T(8,128)(2,1)} %constant_dynamic-update-slice_fusion), calls=%async_computation.1 | async-start | bytes 2129920 | tf_op jit(solution)/shard_map/all_to_all | solution.py:38
  76.1 3.3 %collective-permute-start.4 = (bf16[160,128]{1,0:T(8,128)(2,1)S(1)}, bf16[160,128]{1,0:T(8,128)(2,1)S(1)}, u32[]{:S(2)}, u32[]{:S(2)}) collective-permute-start(bf16[160,128]{1,0:T(8,128)(2,1)S(1)} %get-tuple-element.34), channel_id=1, source_target_pairs={{0,64},{64,0},{1,65},{65,1},{2,66},{66,2},{3,67},{67,3},{4,68},{68... | collective-permute-start | bytes 122888 | tf_op jit(solution)/shard_map/ppermute | solution.py:367
  79.4 11.1 %collective-permute-done.4 = bf16[160,128]{1,0:T(8,128)(2,1)S(1)} collective-permute-done((bf16[160,128]{1,0:T(8,128)(2,1)S(1)}, bf16[160,128]{1,0:T(8,128)(2,1)S(1)}, u32[]{:S(2)}, u32[]{:S(2)}) %collective-permute-start.4) | collective-permute-done | bytes 40992 | tf_op jit(solution)/shard_map/ppermute | solution.py:367
  98.4 3.8 %shard_map.168 = bf16[16,64,128]{2,1,0:T(8,128)(2,1)} custom-call(bf16[160,5120]{1,0:T(8,128)(2,1)} %shard_map.167.h_ref, bf16[16,320,384]{2,1,0:T(8,128)(2,1)} %all-gather.3.cloned.1.call-done.w_ref), custom_call_target="tpu_custom_call" | custom-call | flops 209715200 | bytes 4194304 | tf_op jit(solution)/shard_map/pallas_call | solution.py:89
  102.2 13.2 %all-to-all-start.5 = ((bf16[16,64,128]{2,1,0:T(8,128)(2,1)}), bf16[16,64,128]{2,1,0:T(8,128)(2,1)S(1)}, u32[]{:S(2)}, u32[]{:S(2)}) async-start(bf16[16,64,128]{2,1,0:T(8,128)(2,1)} %shard_map.168), calls=%async_computation.5 | async-start | bytes 524288 | tf_op jit(solution)/shard_map/all_to_all | solution.py:38
  115.5 4.1 %shard_map.169.own_new = bf16[320,128]{1,0:T(8,128)(2,1)} custom-call(bf16[160,5120]{1,0:T(8,128)(2,1)} %shard_map.167.h_ref, bf16[16,320,384]{2,1,0:T(8,128)(2,1)} %all-gather.3.cloned.1.call-done.w_ref), custom_call_target="tpu_custom_call" | custom-call | flops 419430400 | bytes 4194304 | tf_op jit(solution)/shard_map/pallas_call | solution.py:89
  119.6 3.3 %collective-permute-start.3 = (bf16[320,128]{1,0:T(8,128)(2,1)}, bf16[320,128]{1,0:T(8,128)(2,1)S(1)}, u32[]{:S(2)}, u32[]{:S(2)}) collective-permute-start(bf16[320,128]{1,0:T(8,128)(2,1)} %shard_map.169.own_new), channel_id=1, source_target_pairs={{0,4},{4,0},{8,12},{12,8},{16,20},{20,16},{24,28},{28,24},{32,36},... | collective-permute-start | bytes 245768 | tf_op jit(solution)/shard_map/ppermute | solution.py:294
  122.8 8.9 %collective-permute-done.3.other_new = bf16[320,128]{1,0:T(8,128)(2,1)S(1)} collective-permute-done((bf16[320,128]{1,0:T(8,128)(2,1)}, bf16[320,128]{1,0:T(8,128)(2,1)S(1)}, u32[]{:S(2)}, u32[]{:S(2)}) %collective-permute-start.3) | collective-permute-done | bytes 81952 | tf_op jit(solution)/shard_map/ppermute | solution.py:294
  132.5 8.7 %shard_map.170 = bf16[16,80,128]{2,1,0:T(8,128)(2,1)} custom-call(bf16[1024,128]{1,0:T(8,128)(2,1)} %bitcast.72, bf16[2,2,1040,128]{3,2,1,0:T(8,128)(2,1)} %bitcast.67, bf16[2,2,144,512]{3,2,1,0:T(8,128)(2,1)} %shard_map.166.vt_ref, bf16[320,128]{1,0:T(8,128)(2,1)} %shard_map.169.own_new, bf16[320,128]{1,0:T(8,128)(2,1)} %copy-done.14), custom_call_target="tpu_custom_call" | custom-call | flops 1241513984 | bytes 3145728 | tf_op jit(solution)/shard_map/pallas_call | solution.py:194
  141.2 30.2 %all_to_all.48.in_ref = bf16[16,80,128]{2,1,0:T(8,128)(2,1)} all-to-all(bf16[16,80,128]{2,1,0:T(8,128)(2,1)} %shard_map.170), channel_id=1, replica_groups=mesh['y'=4,'xl'=2,'z'=16,'xh'=2,'core'=2] {'z'}, dimensions={0} | all-to-all | bytes 655360 | tf_op jit(solution)/shard_map/all_to_all | solution.py:38
  173.4 5.0 %all-gather.5.cloned.1.call-done.w_ref = bf16[16,320,128]{2,1,0:T(8,128)(2,1)} async-done(((bf16[1,320,128]{2,1,0:T(8,128)(2,1)}), bf16[16,320,128]{2,1,0:T(8,128)(2,1)}) %all-gather.5.cloned.1.call-update) | async-done | bytes 1310736 | tf_op jit(solution)/shard_map/all_gather | solution.py:373
  181.3 12.9 %all-to-all-start.7 = ((bf16[32,160,128]{2,1,0:T(8,128)(2,1)}), bf16[32,160,128]{2,1,0:T(8,128)(2,1)S(1)}, u32[]{:S(2)}, u32[]{:S(2)}) async-start(bf16[32,160,128]{2,1,0:T(8,128)(2,1)} %shard_map.172), calls=%async_computation.7 | async-start | bytes 2621440 | tf_op jit(solution)/shard_map/all_to_all | solution.py:38
  194.9 3.3 %collective-permute-start.5 = (bf16[2,16,128]{2,1,0:T(8,128)(2,1)S(1)}, bf16[2,16,128]{2,1,0:T(8,128)(2,1)S(1)}, u32[]{:S(2)}, u32[]{:S(2)}) collective-permute-start(bf16[2,16,128]{2,1,0:T(8,128)(2,1)S(1)} %get-tuple-element.32), channel_id=1, source_target_pairs={{0,64},{64,0},{1,65},{65,1},{2,66},{66,2},{3,67},{67,3},{4,68},{68... | collective-permute-start | bytes 24584 | tf_op jit(solution)/shard_map/ppermute | solution.py:387
  198.2 12.4 %collective-permute-done.5 = bf16[2,16,128]{2,1,0:T(8,128)(2,1)S(1)} collective-permute-done((bf16[2,16,128]{2,1,0:T(8,128)(2,1)S(1)}, bf16[2,16,128]{2,1,0:T(8,128)(2,1)S(1)}, u32[]{:S(2)}, u32[]{:S(2)}) %collective-permute-start.5) | collective-permute-done | bytes 8224 | tf_op jit(solution)/shard_map/ppermute | solution.py:387
  215.6 6.5 %all-to-all-start.8 = ((f32[16,1,64]{2,1,0:T(1,128)}), f32[16,1,64]{2,1,0:T(1,128)S(1)}, u32[]{:S(2)}, u32[]{:S(2)}) async-start(f32[16,1,64]{2,1,0:T(1,128)} %get-tuple-element.20), calls=%async_computation.8 | async-start | bytes 16384 | tf_op jit(solution)/shard_map/all_to_all | solution.py:38
  222.7 6.4 %all-to-all-done.8 = f32[16,1,64]{2,1,0:T(1,128)S(1)} async-done(((f32[16,1,64]{2,1,0:T(1,128)}), f32[16,1,64]{2,1,0:T(1,128)S(1)}, u32[]{:S(2)}, u32[]{:S(2)}) %all-to-all-start.8) | async-done | bytes 4128 | tf_op jit(solution)/shard_map/all_to_all | solution.py:38
  (91 shorter events, 32.3 us)
Async XLA Ops:
  7.2 29.8 %copy-start.3 = (bf16[512,256]{1,0:T(8,128)(2,1)S(1)}, bf16[512,256]{1,0:T(8,128)(2,1)}, u32[]{:S(2)}) copy-start(bf16[512,256]{1,0:T(8,128)(2,1)} %param.21) | copy-start | bytes 786436
  7.2 15.6 %copy-start.15 = (s32[2]{0:T(128)S(1)}, s32[2]{0:T(128)}, u32[]{:S(2)}) copy-start(s32[2]{0:T(128)} %param.28) | copy-start | bytes 28
  7.2 15.7 %copy-start.11 = (s32[4,64]{1,0:T(4,128)S(1)}, s32[4,64]{1,0:T(4,128)}, u32[]{:S(2)}) copy-start(s32[4,64]{1,0:T(4,128)} %param.29) | copy-start | bytes 3076
  7.2 19.5 %copy-start.7 = (bf16[16,320]{1,0:T(8,128)(2,1)S(1)}, bf16[16,320]{1,0:T(8,128)(2,1)}, u32[]{:S(2)}) copy-start(bf16[16,320]{1,0:T(8,128)(2,1)} %param.16) | copy-start | bytes 30724
  7.2 19.5 %copy-start.2 = (f32[4,16,320]{2,1,0:T(8,128)S(1)}, f32[4,16,320]{2,1,0:T(8,128)}, u32[]{:S(2)}) copy-start(f32[4,16,320]{2,1,0:T(8,128)} %param.15) | copy-start | bytes 245764
  7.2 91.2 %all-gather.3.cloned.1.call-start = ((), (), s32[]{:S(2)}) async-start(), calls=%async_computation.9 | async-start | bytes 4177920 | tf_op jit(solution)/shard_map/all_gather | solution.py:324
  7.3 15.5 %collective-permute-start = (bf16[512,256]{1,0:T(8,128)(2,1)}, bf16[512,256]{1,0:T(8,128)(2,1)S(1)}, u32[]{:S(2)}, u32[]{:S(2)}) collective-permute-start(bf16[512,256]{1,0:T(8,128)(2,1)} %param.21), channel_id=1, source_target_pairs={{0,4},{4,0},{8,12},{12,8},{16,20},{20,16},{24,28},{28,24},{32,36},... | collective-permute-start | bytes 786440 | tf_op jit(solution)/shard_map/ppermute | solution.py:294
  11.8 11.0 %collective-permute-start.1 = (bf16[512,256]{1,0:T(8,128)(2,1)}, bf16[512,256]{1,0:T(8,128)(2,1)S(1)}, u32[]{:S(2)}, u32[]{:S(2)}) collective-permute-start(bf16[512,256]{1,0:T(8,128)(2,1)} %param.22), channel_id=1, source_target_pairs={{0,4},{4,0},{8,12},{12,8},{16,20},{20,16},{24,28},{28,24},{32,36},... | collective-permute-start | bytes 786440 | tf_op jit(solution)/shard_map/ppermute | solution.py:294
  15.4 22.3 %copy-start.4 = (bf16[512,256]{1,0:T(8,128)(2,1)S(1)}, bf16[512,256]{1,0:T(8,128)(2,1)}, u32[]{:S(2)}) copy-start(bf16[512,256]{1,0:T(8,128)(2,1)} %param.22) | copy-start | bytes 786436
  23.3 26.9 %collective-permute-start.2 = (bf16[16,128]{1,0:T(8,128)(2,1)S(1)}, bf16[16,128]{1,0:T(8,128)(2,1)S(1)}, u32[]{:S(2)}, u32[]{:S(2)}) collective-permute-start(bf16[16,128]{1,0:T(8,128)(2,1)S(1)} %fusion.2), channel_id=1, source_target_pairs={{0,4},{4,0},{8,12},{12,8},{16,20},{20,16},{24,28},{28,24},{32,36},... | collective-permute-start | bytes 12296 | tf_op jit(solution)/shard_map/ppermute | solution.py:294
  26.8 11.7 %copy-start.13 = (s32[4]{0:T(128)S(1)}, s32[4]{0:T(128)}, u32[]{:S(2)}) copy-start(s32[4]{0:T(128)} %param.27) | copy-start | bytes 52
  27.4 11.7 %copy-start.12 = (f32[50]{0:T(128)S(1)}, f32[50]{0:T(128)}, u32[]{:S(2)}) copy-start(f32[50]{0:T(128)} %param.26) | copy-start | bytes 604
  27.4 16.5 %all-to-all-start.2 = ((f32[16,1,80]{2,1,0:T(1,128)}), f32[16,1,80]{2,1,0:T(1,128)S(1)}, u32[]{:S(2)}, u32[]{:S(2)}) async-start(f32[16,1,80]{2,1,0:T(1,128)} %broadcast_in_dim.17), calls=%async_computation.2 | async-start | bytes 16384 | tf_op jit(solution)/shard_map/all_to_all | solution.py:32
  37.0 6.9 %copy-start.8 = (f32[320]{0:T(512)S(1)}, f32[320]{0:T(512)}, u32[]{:S(2)}) copy-start(f32[320]{0:T(512)} %param.24) | copy-start | bytes 3844
  45.0 19.2 %all-to-all-start.3 = ((bf16[16,80,320]{2,1,0:T(8,128)(2,1)}), bf16[16,80,320]{2,1,0:T(8,128)(2,1)S(1)}, u32[]{:S(2)}, u32[]{:S(2)}) async-start(bf16[16,80,320]{2,1,0:T(8,128)(2,1)} %broadcast_in_dim.19), calls=%async_computation.3 | async-start | bytes 1966080 | tf_op jit(solution)/shard_map/all_to_all | solution.py:32
  72.3 22.1 %all-to-all-start.1 = ((bf16[2,2080,128]{2,1,0:T(8,128)(2,1)}), bf16[2,2080,128]{2,1,0:T(8,128)(2,1)S(1)}, u32[]{:S(2)}, u32[]{:S(2)}) async-start(bf16[2,2080,128]{2,1,0:T(8,128)(2,1)} %constant_dynamic-update-slice_fusion), calls=%async_computation.1 | async-start | bytes 2129920 | tf_op jit(solution)/shard_map/all_to_all | solution.py:38
  76.0 102.4 %all-gather.5.cloned.1.call-start = ((), (), s32[]{:S(2)}) async-start(), calls=%async_computation.10 | async-start | bytes 1392640 | tf_op jit(solution)/shard_map/all_gather | solution.py:373
  76.1 14.4 %collective-permute-start.4 = (bf16[160,128]{1,0:T(8,128)(2,1)S(1)}, bf16[160,128]{1,0:T(8,128)(2,1)S(1)}, u32[]{:S(2)}, u32[]{:S(2)}) collective-permute-start(bf16[160,128]{1,0:T(8,128)(2,1)S(1)} %get-tuple-element.34), channel_id=1, source_target_pairs={{0,64},{64,0},{1,65},{65,1},{2,66},{66,2},{3,67},{67,3},{4,68},{68... | collective-permute-start | bytes 122888 | tf_op jit(solution)/shard_map/ppermute | solution.py:367
  102.2 29.5 %all-to-all-start.5 = ((bf16[16,64,128]{2,1,0:T(8,128)(2,1)}), bf16[16,64,128]{2,1,0:T(8,128)(2,1)S(1)}, u32[]{:S(2)}, u32[]{:S(2)}) async-start(bf16[16,64,128]{2,1,0:T(8,128)(2,1)} %shard_map.168), calls=%async_computation.5 | async-start | bytes 524288 | tf_op jit(solution)/shard_map/all_to_all | solution.py:38
  119.6 12.2 %collective-permute-start.3 = (bf16[320,128]{1,0:T(8,128)(2,1)}, bf16[320,128]{1,0:T(8,128)(2,1)S(1)}, u32[]{:S(2)}, u32[]{:S(2)}) collective-permute-start(bf16[320,128]{1,0:T(8,128)(2,1)} %shard_map.169.own_new), channel_id=1, source_target_pairs={{0,4},{4,0},{8,12},{12,8},{16,20},{20,16},{24,28},{28,24},{32,36},... | collective-permute-start | bytes 245768 | tf_op jit(solution)/shard_map/ppermute | solution.py:294
  181.3 31.0 %all-to-all-start.7 = ((bf16[32,160,128]{2,1,0:T(8,128)(2,1)}), bf16[32,160,128]{2,1,0:T(8,128)(2,1)S(1)}, u32[]{:S(2)}, u32[]{:S(2)}) async-start(bf16[32,160,128]{2,1,0:T(8,128)(2,1)} %shard_map.172), calls=%async_computation.7 | async-start | bytes 2621440 | tf_op jit(solution)/shard_map/all_to_all | solution.py:38
  194.2 35.0 %copy-start.10 = (f32[320]{0:T(512)S(1)}, f32[320]{0:T(512)}, u32[]{:S(2)}) copy-start(f32[320]{0:T(512)} %param.25) | copy-start | bytes 3844
  194.9 15.7 %collective-permute-start.5 = (bf16[2,16,128]{2,1,0:T(8,128)(2,1)S(1)}, bf16[2,16,128]{2,1,0:T(8,128)(2,1)S(1)}, u32[]{:S(2)}, u32[]{:S(2)}) collective-permute-start(bf16[2,16,128]{2,1,0:T(8,128)(2,1)S(1)} %get-tuple-element.32), channel_id=1, source_target_pairs={{0,64},{64,0},{1,65},{65,1},{2,66},{66,2},{3,67},{67,3},{4,68},{68... | collective-permute-start | bytes 24584 | tf_op jit(solution)/shard_map/ppermute | solution.py:387
  215.6 13.5 %all-to-all-start.8 = ((f32[16,1,64]{2,1,0:T(1,128)}), f32[16,1,64]{2,1,0:T(1,128)S(1)}, u32[]{:S(2)}, u32[]{:S(2)}) async-start(f32[16,1,64]{2,1,0:T(1,128)} %get-tuple-element.20), calls=%async_computation.8 | async-start | bytes 16384 | tf_op jit(solution)/shard_map/all_to_all | solution.py:38
  (6 other events, 14.2 us)
Sparse Core Ops, SparseCore 0:
  22.9 75.4 all-gather.2
  100.5 77.8 all-gather.4

commit v8 on v7

--- a/solution.py
+++ b/solution.py
@@ -210,8 +210,7 @@
     )(queries, *arrays)
 
 
-def combine_kernel(in_ref, out_ref):
-    count = in_ref.shape[0]
+def combine(in_ref):
     totals = in_ref[:, 64:80, :].astype(F32)
     peak = totals[:, 0, :] + totals[:, 1, :] + totals[:, 2, :]
     denom = totals[:, 3, :] + totals[:, 4, :] + totals[:, 5, :]
@@ -224,21 +223,18 @@
     share = (share / jnp.where(even, low, high)).T
     for xl in range(2):
         mixed = jnp.zeros((64, HD), F32)
-        for i in range(xl, count, 2):
+        for i in range(xl, in_ref.shape[0], 2):
             mixed = mixed + in_ref[i, 0:64, :].astype(F32) * share[0:64, i : i + 1]
-        out_ref[64 * xl : 64 * (xl + 1)] = mixed.astype(BF16)
-
-
-def combine(parts):
-    return pl.pallas_call(
-        combine_kernel,
-        out_shape=jax.ShapeDtypeStruct((HD, HD), BF16),
-        compiler_params=pltpu.CompilerParams(vmem_limit_bytes=VMEM_LIMIT),
-    )(parts)
-
-
-def output_kernel(att_ref, w_ref, out_ref):
-    attention = att_ref[...]
+        yield mixed.astype(BF16)
+
+
+def output_kernel(in_ref, w_ref, out_ref, att):
+    @pl.when(pl.program_id(0) == 0)
+    def _():
+        for xl, rows in enumerate(combine(in_ref)):
+            att[64 * xl : 64 * (xl + 1)] = rows
+
+    attention = att[...]
     for m in range(8):
         weights = w_ref[2 * m : 2 * m + 2].reshape(320, HD)
         part = lax.dot_general(
@@ -253,18 +249,19 @@
             )
 
 
-def output_projection(attention, weights):
+def output_projection(shares, weights):
     return pl.pallas_call(
         output_kernel,
         grid=(2,),
         in_specs=[
-            pl.BlockSpec((HD, HD), lambda s: (0, 0)),
-            pl.BlockSpec((16, 160, HD), lambda s: (0, s, 0)),
+            pl.BlockSpec(shares.shape, lambda s: (0, 0, 0)),
+            pl.BlockSpec((16, 160, HD), lambda s: (0, s, 3)),
         ],
         out_specs=pl.BlockSpec((16, 160, HD), lambda s: (s, 0, 0)),
         out_shape=jax.ShapeDtypeStruct((32, 160, HD), BF16),
-        compiler_params=pltpu.CompilerParams(vmem_limit_bytes=VMEM_LIMIT),
-    )(attention, weights)
+        scratch_shapes=[pltpu.VMEM((HD, HD), BF16)],
+        compiler_params=pltpu.CompilerParams(vmem_limit_bytes=VMEM_LIMIT),
+    )(shares, weights)
 
 
 def over_heads_kernel(in_ref, y_ref, square_ref):
@@ -314,14 +311,15 @@
     flight, ch_dev, width = state.shape
     rows_count = flight * ch_dev
 
-    near_keys, near_values = from_neighbour(cache_keys), from_neighbour(cache_values)
+    tokens = jnp.concatenate([cache_keys, cache_values], axis=0)
+    near = from_neighbour(tokens)
 
     side = lax.axis_index("xl")
-    w_heads = jnp.concatenate([by_head(w) for w in (w_key, w_value, w_query)], axis=2)
-    w_heads, w_out, near_keys, near_values = lax.optimization_barrier(
-        (swapped(w_heads, "xl"), w_out, near_keys, near_values)
-    )
-    w_full = lax.all_gather(w_heads.reshape(320, 3 * HD), "z", axis=0, tiled=False)
+    parts = [by_head(w) for w in (w_key, w_value, w_query)]
+    parts.append(jnp.transpose(w_out.reshape(2, HD, 160), (0, 2, 1)))
+    shard = swapped(jnp.concatenate(parts, axis=2), "xl")
+    shard, near = lax.optimization_barrier((shard, near))
+    w_full = lax.all_gather(shard.reshape(320, 4 * HD), "z", axis=0, tiled=False)
 
     current = level_lookup(levels, noise_index)
     following = level_lookup(levels, noise_index + 1)
@@ -350,27 +348,15 @@
     seen = jnp.pad(jnp.concatenate([seen, seen], axis=1), ((0, 14), (0, 0)))
     kv = jnp.concatenate(
         [
-            by_head(cache_keys),
-            by_head(cache_values),
+            by_head(tokens),
             jnp.broadcast_to(seen[None], (2, *seen.shape)),
-            by_head(near_keys),
-            by_head(near_values),
+            by_head(near),
             jnp.broadcast_to(from_neighbour(seen)[None], (2, *seen.shape)),
         ],
         axis=1,
     )
     kv = swapped(kv, "xl").reshape(2, 2, 1040, HD)
     values_t = turn(kv)
-
-    low, high = jnp.transpose(w_out[:HD]), jnp.transpose(w_out[HD:])
-    mine = jnp.where(side == 0, low, high)
-    other = lax.ppermute(jnp.where(side == 0, high, low), "xl", [(0, 1), (1, 0)])
-    w_columns = jnp.where(
-        side == 0,
-        jnp.concatenate([mine, other], axis=0),
-        jnp.concatenate([other, mine], axis=0),
-    )
-    w_out_full = lax.all_gather(w_columns, "z", axis=0, tiled=False)
 
     w_full, values_t, features = lax.optimization_barrier((w_full, values_t, features))
     queries = project(features, w_full, 2, HD, (16, 64, HD))
@@ -379,7 +365,7 @@
     fresh = (new, from_neighbour(new))
     parts = attend(queries, kv, values_t, fresh)
     parts = swapped(parts, "z")
-    parts = swapped(output_projection(combine(parts), w_out_full), (*WIDE, "xl"))
+    parts = swapped(output_projection(parts, w_full), (*WIDE, "xl"))
 
     finished = new.reshape(2, 2, 80, HD)[:, :, 64:]
     mine = jnp.where(side == 0, finished[:, 0], finished[:, 1])

time: 239 us -> 227 us (0.950)
  starting transfers between devices: 69.2 us -> 61.5 us
  blocking collectives: 45.4 us -> 41 us
  waiting for transfers between devices: 64.3 us -> 67.8 us
  other arithmetic: 6.8 us -> 4.3 us
    all_to_all x4, waiting for transfers between devices: 8.06 us -> 20.9 us  [swapped(): return lax.all_to_all(blocks, axis, 0, 0, tiled=True)]
    ppermute x1 -> x0, waiting for transfers between devices: 11.1 us -> none  [local(): lax.ppermute(jnp.where(side == 0, high, low), 'xl', [(0, 1), (1, 0)])]
    ppermute x4 -> x3, waiting for transfers between devices: 8.94 us -> 3 us  [from_neighbour(): return lax.ppermute(array, 'z', [(z, z ^ 1) for z in range(16)])]
    all_gather x2 -> x1, waiting for transfers between devices: 5.8 us -> 10.6 us  [local(): lax.all_gather(shard.reshape(320, 4 * HD), 'z', axis=0, tiled=False)]
    all_to_all x2, blocking collectives: 37.6 us -> 33.1 us  [swapped(): return lax.all_to_all(blocks, axis, 0, 0, tiled=True)]
    ppermute x4 -> x3, starting transfers between devices: 13 us -> 9.55 us  [from_neighbour(): return lax.ppermute(array, 'z', [(z, z ^ 1) for z in range(16)])]
    all_to_all x4, starting transfers between devices: 36.3 us -> 32.9 us  [swapped(): return lax.all_to_all(blocks, axis, 0, 0, tiled=True)]
    ppermute x1 -> x0, starting transfers between devices: 3.29 us -> none  [local(): lax.ppermute(jnp.where(side == 0, high, low), 'xl', [(0, 1), (1, 0)])]
  transfers between devices with their start and end apart: 14 -> 11, of which waited for: 9 -> 9; matrix products, arithmetic and copies ran while one was open for 5% -> 3% of each run, Pallas kernels for 10% -> 4%
where the time goes in v8:
time: 227 us; the launch traced here: 226 us
  waiting for transfers between devices  67.8 us (30%)
  starting transfers between devices  61.5 us (27%)
  blocking collectives  41 us (18%)
  Pallas kernels  27.8 us (12%)
  between operations  14.4 us (6%)
  local copies, waits for them, and re-layouts  9.3 us (4%)
  other arithmetic  4.3 us (2%)
    all_to_all x2, blocking collectives, swapped(): return lax.all_to_all(blocks, axis, 0, 0, tiled=True)  33.1 us
    all_to_all x4, starting transfers between devices, swapped(): return lax.all_to_all(blocks, axis, 0, 0, tiled=True)  32.9 us
    all_to_all x2, waiting for transfers between devices, sent_to_all(): lax.all_to_all(jnp.broadcast_to(array[None], (devices, *array.shape)), ax...  20.9 us
    all_to_all x4, waiting for transfers between devices, swapped(): return lax.all_to_all(blocks, axis, 0, 0, tiled=True)  20.9 us
    all_to_all x2, starting transfers between devices, sent_to_all(): lax.all_to_all(jnp.broadcast_to(array[None], (devices, *array.shape)), ax...  15.8 us
    ppermute x1, waiting for transfers between devices, local(): other = lax.ppermute(other, 'xl', [(0, 1), (1, 0)])  12.4 us
    all_gather x1, waiting for transfers between devices, local(): lax.all_gather(shard.reshape(320, 4 * HD), 'z', axis=0, tiled=False)  10.6 us
    ppermute x3, starting transfers between devices, from_neighbour(): return lax.ppermute(array, 'z', [(z, z ^ 1) for z in range(16)])  9.55 us
  transfers between devices with their start and end apart: 11, of which 9 were waited for; matrix products, arithmetic and copies ran while one was open for 3% of the time, Pallas kernels for 4%

profile of v8, /device:TPU:1, one launch (start us, length us, event | category | flops | bytes accessed | tf_op | source)
XLA Modules:
  0.0 226.1 jit_solution(6394842009787288933)
XLA Ops:
  9.3 4.4 %collective-permute-start = (bf16[1024,256]{1,0:T(8,128)(2,1)S(1)}, bf16[1024,256]{1,0:T(8,128)(2,1)S(1)}, u32[]{:S(2)}, u32[]{:S(2)}) collective-permute-start(bf16[1024,256]{1,0:T(8,128)(2,1)S(1)} %constant_dynamic-update-slice_fusion), channel_id=1, source_target_pairs={{0,4},{4,0},{8,12},{12,8},{16,20},{20,16},{24,28},{28,24},{32,36},... | collective-permute-start | bytes 1572872 | tf_op jit(solution)/shard_map/ppermute | solution.py:291
  15.4 7.7 %all_to_all.46 = bf16[2,160,512]{2,1,0:T(8,128)(2,1)} all-to-all(bf16[2,160,512]{2,1,0:T(8,128)(2,1)S(1)} %pad_maximum_fusion.1), channel_id=1, replica_groups=mesh['y'=4,'xl'=2,'z'=16,'xh'=2,'core'=2] {'xl'}, dimensions={0} | all-to-all | bytes 655360 | tf_op jit(solution)/shard_map/all_to_all | solution.py:38
  26.3 12.1 %all-to-all-start.2 = ((f32[16,1,80]{2,1,0:T(1,128)}), f32[16,1,80]{2,1,0:T(1,128)S(1)}, u32[]{:S(2)}, u32[]{:S(2)}) async-start(f32[16,1,80]{2,1,0:T(1,128)} %broadcast_in_dim.17), calls=%async_computation.2 | async-start | bytes 16384 | tf_op jit(solution)/shard_map/all_to_all | solution.py:32
  38.8 6.5 %all-to-all-done.2 = f32[16,1,80]{2,1,0:T(1,128)S(1)} async-done(((f32[16,1,80]{2,1,0:T(1,128)}), f32[16,1,80]{2,1,0:T(1,128)S(1)}, u32[]{:S(2)}, u32[]{:S(2)}) %all-to-all-start.2) | async-done | bytes 5152 | tf_op jit(solution)/shard_map/all_to_all | solution.py:32
  46.5 3.6 %all-to-all-start.3 = ((bf16[16,80,320]{2,1,0:T(8,128)(2,1)}), bf16[16,80,320]{2,1,0:T(8,128)(2,1)S(1)}, u32[]{:S(2)}, u32[]{:S(2)}) async-start(bf16[16,80,320]{2,1,0:T(8,128)(2,1)} %broadcast_in_dim.19), calls=%async_computation.3 | async-start | bytes 1966080 | tf_op jit(solution)/shard_map/all_to_all | solution.py:32
  51.3 14.4 %all-to-all-done.3 = bf16[16,80,320]{2,1,0:T(8,128)(2,1)S(1)} async-done(((bf16[16,80,320]{2,1,0:T(8,128)(2,1)}), bf16[16,80,320]{2,1,0:T(8,128)(2,1)S(1)}, u32[]{:S(2)}, u32[]{:S(2)}) %all-to-all-start.3) | async-done | bytes 819232 | tf_op jit(solution)/shard_map/all_to_all | solution.py:32
  65.9 7.9 %all_to_all.47 = bf16[2,16,80,320]{3,2,1,0:T(8,128)(2,1)} all-to-all(bf16[2,16,80,320]{3,2,1,0:T(8,128)(2,1)S(1)} %broadcast_in_dim.20), channel_id=1, replica_groups=mesh['y'=4,'xl'=2,'z'=16,'xh'=2,'core'=2] {'core'}, dimensions={0} | all-to-all | bytes 3276800 | tf_op jit(solution)/shard_map/all_to_all | solution.py:32
  73.8 3.6 %all-to-all-start.1 = ((bf16[2,2080,128]{2,1,0:T(8,128)(2,1)}), bf16[2,2080,128]{2,1,0:T(8,128)(2,1)S(1)}, u32[]{:S(2)}, u32[]{:S(2)}) async-start(bf16[2,2080,128]{2,1,0:T(8,128)(2,1)} %pad_maximum_fusion), calls=%async_computation.1 | async-start | bytes 2129920 | tf_op jit(solution)/shard_map/all_to_all | solution.py:38
  77.4 3.2 %shard_map.167.h_ref = bf16[160,5120]{1,0:T(8,128)(2,1)} custom-call(bf16[2,4,2,2,80,320]{5,4,3,2,1,0:T(8,128)(2,1)} %bitcast.57), custom_call_target="tpu_custom_call" | custom-call | bytes 4194304 | tf_op jit(solution)/shard_map/pallas_call | solution.py:53
  80.6 10.4 %all-to-all-done.1 = bf16[2,2080,128]{2,1,0:T(8,128)(2,1)S(1)} async-done(((bf16[2,2080,128]{2,1,0:T(8,128)(2,1)}), bf16[2,2080,128]{2,1,0:T(8,128)(2,1)S(1)}, u32[]{:S(2)}, u32[]{:S(2)}) %all-to-all-start.1) | async-done | bytes 1064992 | tf_op jit(solution)/shard_map/all_to_all | solution.py:38
  94.3 10.6 %all-gather.2.cloned.1.call-done.w_ref = bf16[16,320,512]{2,1,0:T(8,128)(2,1)} async-done(((bf16[1,320,512]{2,1,0:T(8,128)(2,1)}), bf16[16,320,512]{2,1,0:T(8,128)(2,1)}) %all-gather.2.cloned.1.call-update) | async-done | bytes 5242896 | tf_op jit(solution)/shard_map/all_gather | solution.py:322
  104.9 3.9 %shard_map.168 = bf16[16,64,128]{2,1,0:T(8,128)(2,1)} custom-call(bf16[160,5120]{1,0:T(8,128)(2,1)} %shard_map.167.h_ref, bf16[16,320,512]{2,1,0:T(8,128)(2,1)} %all-gather.2.cloned.1.call-done.w_ref), custom_call_target="tpu_custom_call" | custom-call | flops 209715200 | bytes 4194304 | tf_op jit(solution)/shard_map/pallas_call | solution.py:89
  108.8 7.0 %all-to-all-start.5 = ((bf16[16,64,128]{2,1,0:T(8,128)(2,1)}), bf16[16,64,128]{2,1,0:T(8,128)(2,1)S(1)}, u32[]{:S(2)}, u32[]{:S(2)}) async-start(bf16[16,64,128]{2,1,0:T(8,128)(2,1)} %shard_map.168), calls=%async_computation.5 | async-start | bytes 524288 | tf_op jit(solution)/shard_map/all_to_all | solution.py:38
  115.8 4.2 %shard_map.169.own_new = bf16[320,128]{1,0:T(8,128)(2,1)} custom-call(bf16[160,5120]{1,0:T(8,128)(2,1)} %shard_map.167.h_ref, bf16[16,320,512]{2,1,0:T(8,128)(2,1)} %all-gather.2.cloned.1.call-done.w_ref), custom_call_target="tpu_custom_call" | custom-call | flops 419430400 | bytes 4194304 | tf_op jit(solution)/shard_map/pallas_call | solution.py:89
  119.9 3.3 %collective-permute-start.2 = (bf16[320,128]{1,0:T(8,128)(2,1)}, bf16[320,128]{1,0:T(8,128)(2,1)S(1)}, u32[]{:S(2)}, u32[]{:S(2)}) collective-permute-start(bf16[320,128]{1,0:T(8,128)(2,1)} %shard_map.169.own_new), channel_id=1, source_target_pairs={{0,4},{4,0},{8,12},{12,8},{16,20},{20,16},{24,28},{28,24},{32,36},... | collective-permute-start | bytes 245768 | tf_op jit(solution)/shard_map/ppermute | solution.py:291
  123.2 3.0 %collective-permute-done.2.other_new = bf16[320,128]{1,0:T(8,128)(2,1)S(1)} collective-permute-done((bf16[320,128]{1,0:T(8,128)(2,1)}, bf16[320,128]{1,0:T(8,128)(2,1)S(1)}, u32[]{:S(2)}, u32[]{:S(2)}) %collective-permute-start.2) | collective-permute-done | bytes 81952 | tf_op jit(solution)/shard_map/ppermute | solution.py:291
  129.3 8.6 %shard_map.170 = bf16[16,80,128]{2,1,0:T(8,128)(2,1)} custom-call(bf16[1024,128]{1,0:T(8,128)(2,1)} %bitcast.64, bf16[2,2,1040,128]{3,2,1,0:T(8,128)(2,1)} %bitcast.59, bf16[2,2,144,512]{3,2,1,0:T(8,128)(2,1)} %shard_map.166.vt_ref, bf16[320,128]{1,0:T(8,128)(2,1)} %shard_map.169.own_new, bf16[320,128]{1,0:T(8,128)(2,1)} %copy-done.12), custom_call_target="tpu_custom_call" | custom-call | flops 1241513984 | bytes 3145728 | tf_op jit(solution)/shard_map/pallas_call | solution.py:194
  138.0 25.5 %all_to_all.48.in_ref = bf16[16,80,128]{2,1,0:T(8,128)(2,1)} all-to-all(bf16[16,80,128]{2,1,0:T(8,128)(2,1)} %shard_map.170), channel_id=1, replica_groups=mesh['y'=4,'xl'=2,'z'=16,'xh'=2,'core'=2] {'z'}, dimensions={0} | all-to-all | bytes 655360 | tf_op jit(solution)/shard_map/all_to_all | solution.py:38
  163.4 3.3 %shard_map.171 = bf16[32,160,128]{2,1,0:T(8,128)(2,1)} custom-call(bf16[16,80,128]{2,1,0:T(8,128)(2,1)} %all_to_all.48.in_ref, bf16[16,320,512]{2,1,0:T(8,128)(2,1)} %all-gather.2.cloned.1.call-done.w_ref), custom_call_target="tpu_custom_call" | custom-call | tf_op jit(solution)/shard_map/pallas_call | solution.py:253
  166.8 15.8 %all-to-all-start.7 = ((bf16[32,160,128]{2,1,0:T(8,128)(2,1)}), bf16[32,160,128]{2,1,0:T(8,128)(2,1)S(1)}, u32[]{:S(2)}, u32[]{:S(2)}) async-start(bf16[32,160,128]{2,1,0:T(8,128)(2,1)} %shard_map.171), calls=%async_computation.7 | async-start | bytes 2621440 | tf_op jit(solution)/shard_map/all_to_all | solution.py:38
  183.3 3.3 %collective-permute-start.3 = (bf16[2,16,128]{2,1,0:T(8,128)(2,1)S(1)}, bf16[2,16,128]{2,1,0:T(8,128)(2,1)S(1)}, u32[]{:S(2)}, u32[]{:S(2)}) collective-permute-start(bf16[2,16,128]{2,1,0:T(8,128)(2,1)S(1)} %get-tuple-element.24), channel_id=1, source_target_pairs={{0,64},{64,0},{1,65},{65,1},{2,66},{66,2},{3,67},{67,3},{4,68},{68... | collective-permute-start | bytes 24584 | tf_op jit(solution)/shard_map/ppermute | solution.py:373
  186.6 12.4 %collective-permute-done.3 = bf16[2,16,128]{2,1,0:T(8,128)(2,1)S(1)} collective-permute-done((bf16[2,16,128]{2,1,0:T(8,128)(2,1)S(1)}, bf16[2,16,128]{2,1,0:T(8,128)(2,1)S(1)}, u32[]{:S(2)}, u32[]{:S(2)}) %collective-permute-start.3) | collective-permute-done | bytes 8224 | tf_op jit(solution)/shard_map/ppermute | solution.py:373
  204.0 6.5 %all-to-all-start.8 = ((f32[16,1,64]{2,1,0:T(1,128)}), f32[16,1,64]{2,1,0:T(1,128)S(1)}, u32[]{:S(2)}, u32[]{:S(2)}) async-start(f32[16,1,64]{2,1,0:T(1,128)} %get-tuple-element.16), calls=%async_computation.8 | async-start | bytes 16384 | tf_op jit(solution)/shard_map/all_to_all | solution.py:38
  211.1 6.4 %all-to-all-done.8 = f32[16,1,64]{2,1,0:T(1,128)S(1)} async-done(((f32[16,1,64]{2,1,0:T(1,128)}), f32[16,1,64]{2,1,0:T(1,128)S(1)}, u32[]{:S(2)}, u32[]{:S(2)}) %all-to-all-start.8) | async-done | bytes 4128 | tf_op jit(solution)/shard_map/all_to_all | solution.py:38
  (75 shorter events, 24.2 us)
Async XLA Ops:
  7.2 6.5 %copy-start = (bf16[256,160]{0,1:T(8,128)(2,1)S(1)}, bf16[256,160]{0,1:T(8,128)(2,1)}, u32[]{:S(2)}) copy-start(bf16[256,160]{0,1:T(8,128)(2,1)} %param.20) | copy-start | bytes 245764
  7.2 15.9 %copy-start.13 = (s32[2]{0:T(128)S(1)}, s32[2]{0:T(128)}, u32[]{:S(2)}) copy-start(s32[2]{0:T(128)} %param.28) | copy-start | bytes 28
  7.2 16.0 %copy-start.9 = (s32[4,64]{1,0:T(4,128)S(1)}, s32[4,64]{1,0:T(4,128)}, u32[]{:S(2)}) copy-start(s32[4,64]{1,0:T(4,128)} %param.29) | copy-start | bytes 3076
  7.2 18.3 %copy-start.5 = (bf16[16,320]{1,0:T(8,128)(2,1)S(1)}, bf16[16,320]{1,0:T(8,128)(2,1)}, u32[]{:S(2)}) copy-start(bf16[16,320]{1,0:T(8,128)(2,1)} %param.16) | copy-start | bytes 30724
  7.2 18.3 %copy-start.3 = (f32[4,16,320]{2,1,0:T(8,128)S(1)}, f32[4,16,320]{2,1,0:T(8,128)}, u32[]{:S(2)}) copy-start(f32[4,16,320]{2,1,0:T(8,128)} %param.15) | copy-start | bytes 245764
  7.2 31.2 %copy-start.11 = (s32[4]{0:T(128)S(1)}, s32[4]{0:T(128)}, u32[]{:S(2)}) copy-start(s32[4]{0:T(128)} %param.27) | copy-start | bytes 52
  7.2 31.2 %copy-start.10 = (f32[50]{0:T(128)S(1)}, f32[50]{0:T(128)}, u32[]{:S(2)}) copy-start(f32[50]{0:T(128)} %param.26) | copy-start | bytes 604
  7.2 38.1 %copy-start.6 = (f32[320]{0:T(512)S(1)}, f32[320]{0:T(512)}, u32[]{:S(2)}) copy-start(f32[320]{0:T(512)} %param.24) | copy-start | bytes 3844
  7.3 38.1 %copy-start.7 = (f32[320]{0:T(512)S(1)}, f32[320]{0:T(512)}, u32[]{:S(2)}) copy-start(f32[320]{0:T(512)} %param.23) | copy-start | bytes 3844
  7.3 97.6 %all-gather.2.cloned.1.call-start = ((), (), s32[]{:S(2)}) async-start(), calls=%async_computation.9 | async-start | bytes 5570560 | tf_op jit(solution)/shard_map/all_gather | solution.py:322
  9.3 13.8 %collective-permute-start = (bf16[1024,256]{1,0:T(8,128)(2,1)S(1)}, bf16[1024,256]{1,0:T(8,128)(2,1)S(1)}, u32[]{:S(2)}, u32[]{:S(2)}) collective-permute-start(bf16[1024,256]{1,0:T(8,128)(2,1)S(1)} %constant_dynamic-update-slice_fusion), channel_id=1, source_target_pairs={{0,4},{4,0},{8,12},{12,8},{16,20},{20,16},{24,28},{28,24},{32,36},... | collective-permute-start | bytes 1572872 | tf_op jit(solution)/shard_map/ppermute | solution.py:291
  23.6 26.7 %collective-permute-start.1 = (bf16[16,128]{1,0:T(8,128)(2,1)S(1)}, bf16[16,128]{1,0:T(8,128)(2,1)S(1)}, u32[]{:S(2)}, u32[]{:S(2)}) collective-permute-start(bf16[16,128]{1,0:T(8,128)(2,1)S(1)} %fusion.2), channel_id=1, source_target_pairs={{0,4},{4,0},{8,12},{12,8},{16,20},{20,16},{24,28},{28,24},{32,36},... | collective-permute-start | bytes 12296 | tf_op jit(solution)/shard_map/ppermute | solution.py:291
  26.3 19.0 %all-to-all-start.2 = ((f32[16,1,80]{2,1,0:T(1,128)}), f32[16,1,80]{2,1,0:T(1,128)S(1)}, u32[]{:S(2)}, u32[]{:S(2)}) async-start(f32[16,1,80]{2,1,0:T(1,128)} %broadcast_in_dim.17), calls=%async_computation.2 | async-start | bytes 16384 | tf_op jit(solution)/shard_map/all_to_all | solution.py:32
  46.5 19.2 %all-to-all-start.3 = ((bf16[16,80,320]{2,1,0:T(8,128)(2,1)}), bf16[16,80,320]{2,1,0:T(8,128)(2,1)S(1)}, u32[]{:S(2)}, u32[]{:S(2)}) async-start(bf16[16,80,320]{2,1,0:T(8,128)(2,1)} %broadcast_in_dim.19), calls=%async_computation.3 | async-start | bytes 1966080 | tf_op jit(solution)/shard_map/all_to_all | solution.py:32
  73.8 17.2 %all-to-all-start.1 = ((bf16[2,2080,128]{2,1,0:T(8,128)(2,1)}), bf16[2,2080,128]{2,1,0:T(8,128)(2,1)S(1)}, u32[]{:S(2)}, u32[]{:S(2)}) async-start(bf16[2,2080,128]{2,1,0:T(8,128)(2,1)} %pad_maximum_fusion), calls=%async_computation.1 | async-start | bytes 2129920 | tf_op jit(solution)/shard_map/all_to_all | solution.py:38
  91.0 1.0 copy-start.2
  108.8 19.9 %all-to-all-start.5 = ((bf16[16,64,128]{2,1,0:T(8,128)(2,1)}), bf16[16,64,128]{2,1,0:T(8,128)(2,1)S(1)}, u32[]{:S(2)}, u32[]{:S(2)}) async-start(bf16[16,64,128]{2,1,0:T(8,128)(2,1)} %shard_map.168), calls=%async_computation.5 | async-start | bytes 524288 | tf_op jit(solution)/shard_map/all_to_all | solution.py:38
  119.9 6.3 %collective-permute-start.2 = (bf16[320,128]{1,0:T(8,128)(2,1)}, bf16[320,128]{1,0:T(8,128)(2,1)S(1)}, u32[]{:S(2)}, u32[]{:S(2)}) collective-permute-start(bf16[320,128]{1,0:T(8,128)(2,1)} %shard_map.169.own_new), channel_id=1, source_target_pairs={{0,4},{4,0},{8,12},{12,8},{16,20},{20,16},{24,28},{28,24},{32,36},... | collective-permute-start | bytes 245768 | tf_op jit(solution)/shard_map/ppermute | solution.py:291
  126.2 2.4 %copy-start.12 = (bf16[320,128]{1,0:T(8,128)(2,1)}, bf16[320,128]{1,0:T(8,128)(2,1)S(1)}, u32[]{:S(2)}) copy-start(bf16[320,128]{1,0:T(8,128)(2,1)S(1)} %collective-permute-done.2.other_new) | copy-start | bytes 245764
  166.8 50.8 %copy-start.8 = (f32[320]{0:T(512)S(1)}, f32[320]{0:T(512)}, u32[]{:S(2)}) copy-start(f32[320]{0:T(512)} %param.25) | copy-start | bytes 3844
  166.8 34.0 %all-to-all-start.7 = ((bf16[32,160,128]{2,1,0:T(8,128)(2,1)}), bf16[32,160,128]{2,1,0:T(8,128)(2,1)S(1)}, u32[]{:S(2)}, u32[]{:S(2)}) async-start(bf16[32,160,128]{2,1,0:T(8,128)(2,1)} %shard_map.171), calls=%async_computation.7 | async-start | bytes 2621440 | tf_op jit(solution)/shard_map/all_to_all | solution.py:38
  183.3 15.7 %collective-permute-start.3 = (bf16[2,16,128]{2,1,0:T(8,128)(2,1)S(1)}, bf16[2,16,128]{2,1,0:T(8,128)(2,1)S(1)}, u32[]{:S(2)}, u32[]{:S(2)}) collective-permute-start(bf16[2,16,128]{2,1,0:T(8,128)(2,1)S(1)} %get-tuple-element.24), channel_id=1, source_target_pairs={{0,64},{64,0},{1,65},{65,1},{2,66},{66,2},{3,67},{67,3},{4,68},{68... | collective-permute-start | bytes 24584 | tf_op jit(solution)/shard_map/ppermute | solution.py:373
  200.7 1.1 copy-start.1
  204.0 13.5 %all-to-all-start.8 = ((f32[16,1,64]{2,1,0:T(1,128)}), f32[16,1,64]{2,1,0:T(1,128)S(1)}, u32[]{:S(2)}, u32[]{:S(2)}) async-start(f32[16,1,64]{2,1,0:T(1,128)} %get-tuple-element.16), calls=%async_computation.8 | async-start | bytes 16384 | tf_op jit(solution)/shard_map/all_to_all | solution.py:38
  (1 other events, 0.7 us)
Sparse Core Ops, SparseCore 0:
  23.3 81.5 all-gather.1

commit v9 on v8

--- a/solution.py
+++ b/solution.py
@@ -241,10 +241,10 @@
             attention, weights, (((1,), (1,)), ((), ())), preferred_element_type=F32
         ).astype(BF16)
         for xl in range(2):
-            block, at = part[64 * xl : 64 * (xl + 1)], 2 * m + xl
-            out_ref[at, 0:64] = block[:, 0:HD]
-            out_ref[at, 64:128] = block[:, HD : 2 * HD]
-            out_ref[at, 128:160] = jnp.concatenate(
+            block, at = part[64 * xl : 64 * (xl + 1)], 2 * (m // 2) + xl
+            out_ref[m % 2, at, 0:64] = block[:, 0:HD]
+            out_ref[m % 2, at, 64:128] = block[:, HD : 2 * HD]
+            out_ref[m % 2, at, 128:160] = jnp.concatenate(
                 [block[0:32, 2 * HD :], block[32:64, 2 * HD :]], axis=1
             )
 
@@ -257,8 +257,8 @@
             pl.BlockSpec(shares.shape, lambda s: (0, 0, 0)),
             pl.BlockSpec((16, 160, HD), lambda s: (0, s, 3)),
         ],
-        out_specs=pl.BlockSpec((16, 160, HD), lambda s: (s, 0, 0)),
-        out_shape=jax.ShapeDtypeStruct((32, 160, HD), BF16),
+        out_specs=pl.BlockSpec((2, 8, 160, HD), lambda s: (0, s, 0, 0)),
+        out_shape=jax.ShapeDtypeStruct((2, 16, 160, HD), BF16),
         scratch_shapes=[pltpu.VMEM((HD, HD), BF16)],
         compiler_params=pltpu.CompilerParams(vmem_limit_bytes=VMEM_LIMIT),
     )(shares, weights)
@@ -365,7 +365,8 @@
     fresh = (new, from_neighbour(new))
     parts = attend(queries, kv, values_t, fresh)
     parts = swapped(parts, "z")
-    parts = swapped(output_projection(parts, w_full), (*WIDE, "xl"))
+    parts = swapped(output_projection(parts, w_full), "core")
+    parts = swapped(parts[0] + parts[1], ("y", "xh", "xl"))
 
     finished = new.reshape(2, 2, 80, HD)[:, :, 64:]
     mine = jnp.where(side == 0, finished[:, 0], finished[:, 1])
@@ -381,9 +382,9 @@
     y, y_squares = over_heads(parts)
     y_squares = swapped(y_squares, WIDE).sum(axis=(0, 1))
     velocity = y * lax.rsqrt(y_squares / D + EPSILON)[:, None] * out_gain[None, :]
-    new_state = state + (following - current)[:, None, None] * velocity.reshape(
-        flight, ch_dev, width
-    )
+    step = jnp.repeat(following - current, ch_dev)[:, None]
+    new_state = state.reshape(rows_count, width) + step * velocity
+    new_state = new_state.reshape(flight, ch_dev, width)
     return new_state, new_keys, new_values
 
 

time: 227 us -> 226 us (level)
  blocking collectives: 41 us -> 55.3 us
  starting transfers between devices: 61.5 us -> 50.9 us
  waiting for transfers between devices: 67.8 us -> 61.7 us
    all_to_all x2 -> x3, blocking collectives: 33.1 us -> 47.5 us  [swapped(): return lax.all_to_all(blocks, axis, 0, 0, tiled=True)]
    all_to_all x4, starting transfers between devices: 32.9 us -> 22.3 us  [swapped(): return lax.all_to_all(blocks, axis, 0, 0, tiled=True)]
    ppermute x1, waiting for transfers between devices: 12.4 us -> 4.82 us  [local(): other = lax.ppermute(other, 'xl', [(0, 1), (1, 0)])]
where the time goes in v9:
time: 226 us; the launch traced here: 224 us
  waiting for transfers between devices  61.7 us (27%)
  blocking collectives  55.3 us (24%)
  starting transfers between devices  50.9 us (23%)
  Pallas kernels  27.5 us (12%)
  between operations  14.4 us (6%)
  local copies, waits for them, and re-layouts  9.25 us (4%)
  other arithmetic  5.17 us (2%)
    all_to_all x3, blocking collectives, swapped(): return lax.all_to_all(blocks, axis, 0, 0, tiled=True)  47.5 us
    all_to_all x4, waiting for transfers between devices, swapped(): return lax.all_to_all(blocks, axis, 0, 0, tiled=True)  22.4 us
    all_to_all x4, starting transfers between devices, swapped(): return lax.all_to_all(blocks, axis, 0, 0, tiled=True)  22.3 us
    all_to_all x2, waiting for transfers between devices, sent_to_all(): lax.all_to_all(jnp.broadcast_to(array[None], (devices, *array.shape)), ax...  20.9 us
    all_to_all x2, starting transfers between devices, sent_to_all(): lax.all_to_all(jnp.broadcast_to(array[None], (devices, *array.shape)), ax...  15.8 us
    all_gather x1, waiting for transfers between devices, local(): lax.all_gather(shard.reshape(320, 4 * HD), 'z', axis=0, tiled=False)  10.6 us
    ppermute x3, starting transfers between devices, from_neighbour(): return lax.ppermute(array, 'z', [(z, z ^ 1) for z in range(16)])  9.55 us
    pallas_call x1, Pallas kernels, attend(): pl.pallas_call(attend_kernel, grid=(rows // step,), in_specs=[pl.BlockSpe...  8.65 us
  transfers between devices with their start and end apart: 11, of which 9 were waited for; matrix products, arithmetic and copies ran while one was open for 3% of the time, Pallas kernels for 4%

profile of v9, /device:TPU:1, one launch (start us, length us, event | category | flops | bytes accessed | tf_op | source)
XLA Modules:
  0.0 224.2 jit_solution(2308266026870431529)
XLA Ops:
  9.3 4.4 %collective-permute-start = (bf16[1024,256]{1,0:T(8,128)(2,1)S(1)}, bf16[1024,256]{1,0:T(8,128)(2,1)S(1)}, u32[]{:S(2)}, u32[]{:S(2)}) collective-permute-start(bf16[1024,256]{1,0:T(8,128)(2,1)S(1)} %constant_dynamic-update-slice_fusion), channel_id=1, source_target_pairs={{0,4},{4,0},{8,12},{12,8},{16,20},{20,16},{24,28},{28,24},{32,36},... | collective-permute-start | bytes 1572872 | tf_op jit(solution)/shard_map/ppermute | solution.py:291
  15.4 7.7 %all_to_all.51 = bf16[2,160,512]{2,1,0:T(8,128)(2,1)} all-to-all(bf16[2,160,512]{2,1,0:T(8,128)(2,1)S(1)} %pad_maximum_fusion.1), channel_id=1, replica_groups=mesh['y'=4,'xl'=2,'z'=16,'xh'=2,'core'=2] {'xl'}, dimensions={0} | all-to-all | bytes 655360 | tf_op jit(solution)/shard_map/all_to_all | solution.py:38
  26.3 12.1 %all-to-all-start.2 = ((f32[16,1,80]{2,1,0:T(1,128)}), f32[16,1,80]{2,1,0:T(1,128)S(1)}, u32[]{:S(2)}, u32[]{:S(2)}) async-start(f32[16,1,80]{2,1,0:T(1,128)} %broadcast_in_dim.20), calls=%async_computation.2 | async-start | bytes 16384 | tf_op jit(solution)/shard_map/all_to_all | solution.py:32
  38.8 6.5 %all-to-all-done.2 = f32[16,1,80]{2,1,0:T(1,128)S(1)} async-done(((f32[16,1,80]{2,1,0:T(1,128)}), f32[16,1,80]{2,1,0:T(1,128)S(1)}, u32[]{:S(2)}, u32[]{:S(2)}) %all-to-all-start.2) | async-done | bytes 5152 | tf_op jit(solution)/shard_map/all_to_all | solution.py:32
  46.5 3.6 %all-to-all-start.3 = ((bf16[16,80,320]{2,1,0:T(8,128)(2,1)}), bf16[16,80,320]{2,1,0:T(8,128)(2,1)S(1)}, u32[]{:S(2)}, u32[]{:S(2)}) async-start(bf16[16,80,320]{2,1,0:T(8,128)(2,1)} %broadcast_in_dim.22), calls=%async_computation.3 | async-start | bytes 1966080 | tf_op jit(solution)/shard_map/all_to_all | solution.py:32
  51.3 14.4 %all-to-all-done.3 = bf16[16,80,320]{2,1,0:T(8,128)(2,1)S(1)} async-done(((bf16[16,80,320]{2,1,0:T(8,128)(2,1)}), bf16[16,80,320]{2,1,0:T(8,128)(2,1)S(1)}, u32[]{:S(2)}, u32[]{:S(2)}) %all-to-all-start.3) | async-done | bytes 819232 | tf_op jit(solution)/shard_map/all_to_all | solution.py:32
  65.9 7.9 %all_to_all.52 = bf16[2,16,80,320]{3,2,1,0:T(8,128)(2,1)} all-to-all(bf16[2,16,80,320]{3,2,1,0:T(8,128)(2,1)S(1)} %broadcast_in_dim.23), channel_id=1, replica_groups=mesh['y'=4,'xl'=2,'z'=16,'xh'=2,'core'=2] {'core'}, dimensions={0} | all-to-all | bytes 3276800 | tf_op jit(solution)/shard_map/all_to_all | solution.py:32
  73.8 3.6 %all-to-all-start.1 = ((bf16[2,2080,128]{2,1,0:T(8,128)(2,1)}), bf16[2,2080,128]{2,1,0:T(8,128)(2,1)S(1)}, u32[]{:S(2)}, u32[]{:S(2)}) async-start(bf16[2,2080,128]{2,1,0:T(8,128)(2,1)} %pad_maximum_fusion), calls=%async_computation.1 | async-start | bytes 2129920 | tf_op jit(solution)/shard_map/all_to_all | solution.py:38
  77.4 3.2 %shard_map.167.h_ref = bf16[160,5120]{1,0:T(8,128)(2,1)} custom-call(bf16[2,4,2,2,80,320]{5,4,3,2,1,0:T(8,128)(2,1)} %bitcast.60), custom_call_target="tpu_custom_call" | custom-call | bytes 4194304 | tf_op jit(solution)/shard_map/pallas_call | solution.py:53
  80.6 10.4 %all-to-all-done.1 = bf16[2,2080,128]{2,1,0:T(8,128)(2,1)S(1)} async-done(((bf16[2,2080,128]{2,1,0:T(8,128)(2,1)}), bf16[2,2080,128]{2,1,0:T(8,128)(2,1)S(1)}, u32[]{:S(2)}, u32[]{:S(2)}) %all-to-all-start.1) | async-done | bytes 1064992 | tf_op jit(solution)/shard_map/all_to_all | solution.py:38
  94.3 10.6 %all-gather.2.cloned.1.call-done.w_ref = bf16[16,320,512]{2,1,0:T(8,128)(2,1)} async-done(((bf16[1,320,512]{2,1,0:T(8,128)(2,1)}), bf16[16,320,512]{2,1,0:T(8,128)(2,1)}) %all-gather.2.cloned.1.call-update) | async-done | bytes 5242896 | tf_op jit(solution)/shard_map/all_gather | solution.py:322
  104.9 3.9 %shard_map.168 = bf16[16,64,128]{2,1,0:T(8,128)(2,1)} custom-call(bf16[160,5120]{1,0:T(8,128)(2,1)} %shard_map.167.h_ref, bf16[16,320,512]{2,1,0:T(8,128)(2,1)} %all-gather.2.cloned.1.call-done.w_ref), custom_call_target="tpu_custom_call" | custom-call | flops 209715200 | bytes 4194304 | tf_op jit(solution)/shard_map/pallas_call | solution.py:89
  108.8 7.0 %all-to-all-start.5 = ((bf16[16,64,128]{2,1,0:T(8,128)(2,1)}), bf16[16,64,128]{2,1,0:T(8,128)(2,1)S(1)}, u32[]{:S(2)}, u32[]{:S(2)}) async-start(bf16[16,64,128]{2,1,0:T(8,128)(2,1)} %shard_map.168), calls=%async_computation.5 | async-start | bytes 524288 | tf_op jit(solution)/shard_map/all_to_all | solution.py:38
  115.8 4.2 %shard_map.169.own_new = bf16[320,128]{1,0:T(8,128)(2,1)} custom-call(bf16[160,5120]{1,0:T(8,128)(2,1)} %shard_map.167.h_ref, bf16[16,320,512]{2,1,0:T(8,128)(2,1)} %all-gather.2.cloned.1.call-done.w_ref), custom_call_target="tpu_custom_call" | custom-call | flops 419430400 | bytes 4194304 | tf_op jit(solution)/shard_map/pallas_call | solution.py:89
  119.9 3.3 %collective-permute-start.2 = (bf16[320,128]{1,0:T(8,128)(2,1)}, bf16[320,128]{1,0:T(8,128)(2,1)S(1)}, u32[]{:S(2)}, u32[]{:S(2)}) collective-permute-start(bf16[320,128]{1,0:T(8,128)(2,1)} %shard_map.169.own_new), channel_id=1, source_target_pairs={{0,4},{4,0},{8,12},{12,8},{16,20},{20,16},{24,28},{28,24},{32,36},... | collective-permute-start | bytes 245768 | tf_op jit(solution)/shard_map/ppermute | solution.py:291
  129.3 8.6 %shard_map.170 = bf16[16,80,128]{2,1,0:T(8,128)(2,1)} custom-call(bf16[1024,128]{1,0:T(8,128)(2,1)} %bitcast.66, bf16[2,2,1040,128]{3,2,1,0:T(8,128)(2,1)} %bitcast.62, bf16[2,2,144,512]{3,2,1,0:T(8,128)(2,1)} %shard_map.166.vt_ref, bf16[320,128]{1,0:T(8,128)(2,1)} %shard_map.169.own_new, bf16[320,128]{1,0:T(8,128)(2,1)} %copy-done.12), custom_call_target="tpu_custom_call" | custom-call | flops 1241513984 | bytes 3145728 | tf_op jit(solution)/shard_map/pallas_call | solution.py:194
  138.0 25.5 %all_to_all.53.in_ref = bf16[16,80,128]{2,1,0:T(8,128)(2,1)} all-to-all(bf16[16,80,128]{2,1,0:T(8,128)(2,1)} %shard_map.170), channel_id=1, replica_groups=mesh['y'=4,'xl'=2,'z'=16,'xh'=2,'core'=2] {'z'}, dimensions={0} | all-to-all | bytes 655360 | tf_op jit(solution)/shard_map/all_to_all | solution.py:38
  163.4 3.4 %shard_map.171 = bf16[2,16,160,128]{3,2,1,0:T(8,128)(2,1)} custom-call(bf16[16,80,128]{2,1,0:T(8,128)(2,1)} %all_to_all.53.in_ref, bf16[16,320,512]{2,1,0:T(8,128)(2,1)} %all-gather.2.cloned.1.call-done.w_ref), custom_call_target="tpu_custom_call" | custom-call | tf_op jit(solution)/shard_map/pallas_call | solution.py:253
  166.8 14.3 %all_to_all.54 = bf16[2,16,160,128]{3,2,1,0:T(8,128)(2,1)S(1)} all-to-all(bf16[2,16,160,128]{3,2,1,0:T(8,128)(2,1)} %shard_map.171), channel_id=1, replica_groups=mesh['y'=4,'xl'=2,'z'=16,'xh'=2,'core'=2] {'core'}, dimensions={0} | all-to-all | bytes 2621440 | tf_op jit(solution)/shard_map/all_to_all | solution.py:38
  182.0 6.6 %all-to-all-start.8 = ((bf16[16,160,128]{2,1,0:T(8,128)(2,1)}), bf16[16,160,128]{2,1,0:T(8,128)(2,1)S(1)}, u32[]{:S(2)}, u32[]{:S(2)}) async-start(bf16[16,160,128]{2,1,0:T(8,128)(2,1)} %fusion), calls=%async_computation.8 | async-start | bytes 1310720 | tf_op jit(solution)/shard_map/all_to_all | solution.py:38
  189.4 3.2 %collective-permute-start.3 = (bf16[2,16,128]{2,1,0:T(8,128)(2,1)S(1)}, bf16[2,16,128]{2,1,0:T(8,128)(2,1)S(1)}, u32[]{:S(2)}, u32[]{:S(2)}) collective-permute-start(bf16[2,16,128]{2,1,0:T(8,128)(2,1)S(1)} %get-tuple-element.24), channel_id=1, source_target_pairs={{0,64},{64,0},{1,65},{65,1},{2,66},{66,2},{3,67},{67,3},{4,68},{68... | collective-permute-start | bytes 24584 | tf_op jit(solution)/shard_map/ppermute | solution.py:374
  192.8 4.8 %collective-permute-done.3 = bf16[2,16,128]{2,1,0:T(8,128)(2,1)S(1)} collective-permute-done((bf16[2,16,128]{2,1,0:T(8,128)(2,1)S(1)}, bf16[2,16,128]{2,1,0:T(8,128)(2,1)S(1)}, u32[]{:S(2)}, u32[]{:S(2)}) %collective-permute-start.3) | collective-permute-done | bytes 8224 | tf_op jit(solution)/shard_map/ppermute | solution.py:374
  203.5 5.1 %all-to-all-start.9 = ((f32[16,1,64]{2,1,0:T(1,128)}), f32[16,1,64]{2,1,0:T(1,128)S(1)}, u32[]{:S(2)}, u32[]{:S(2)}) async-start(f32[16,1,64]{2,1,0:T(1,128)} %get-tuple-element.16), calls=%async_computation.9 | async-start | bytes 16384 | tf_op jit(solution)/shard_map/all_to_all | solution.py:38
  209.2 6.4 %all-to-all-done.9 = f32[16,1,64]{2,1,0:T(1,128)S(1)} async-done(((f32[16,1,64]{2,1,0:T(1,128)}), f32[16,1,64]{2,1,0:T(1,128)S(1)}, u32[]{:S(2)}, u32[]{:S(2)}) %all-to-all-start.9) | async-done | bytes 4128 | tf_op jit(solution)/shard_map/all_to_all | solution.py:38
  (78 shorter events, 29.1 us)
Async XLA Ops:
  7.2 6.5 %copy-start = (bf16[256,160]{0,1:T(8,128)(2,1)S(1)}, bf16[256,160]{0,1:T(8,128)(2,1)}, u32[]{:S(2)}) copy-start(bf16[256,160]{0,1:T(8,128)(2,1)} %param.20) | copy-start | bytes 245764
  7.2 15.9 %copy-start.13 = (s32[2]{0:T(128)S(1)}, s32[2]{0:T(128)}, u32[]{:S(2)}) copy-start(s32[2]{0:T(128)} %param.28) | copy-start | bytes 28
  7.2 16.0 %copy-start.9 = (s32[4,64]{1,0:T(4,128)S(1)}, s32[4,64]{1,0:T(4,128)}, u32[]{:S(2)}) copy-start(s32[4,64]{1,0:T(4,128)} %param.29) | copy-start | bytes 3076
  7.2 18.3 %copy-start.5 = (bf16[16,320]{1,0:T(8,128)(2,1)S(1)}, bf16[16,320]{1,0:T(8,128)(2,1)}, u32[]{:S(2)}) copy-start(bf16[16,320]{1,0:T(8,128)(2,1)} %param.16) | copy-start | bytes 30724
  7.2 18.3 %copy-start.3 = (f32[4,16,320]{2,1,0:T(8,128)S(1)}, f32[4,16,320]{2,1,0:T(8,128)}, u32[]{:S(2)}) copy-start(f32[4,16,320]{2,1,0:T(8,128)} %param.15) | copy-start | bytes 245764
  7.2 31.2 %copy-start.11 = (s32[4]{0:T(128)S(1)}, s32[4]{0:T(128)}, u32[]{:S(2)}) copy-start(s32[4]{0:T(128)} %param.27) | copy-start | bytes 52
  7.2 31.2 %copy-start.10 = (f32[50]{0:T(128)S(1)}, f32[50]{0:T(128)}, u32[]{:S(2)}) copy-start(f32[50]{0:T(128)} %param.26) | copy-start | bytes 604
  7.2 38.1 %copy-start.6 = (f32[320]{0:T(512)S(1)}, f32[320]{0:T(512)}, u32[]{:S(2)}) copy-start(f32[320]{0:T(512)} %param.24) | copy-start | bytes 3844
  7.3 38.1 %copy-start.7 = (f32[320]{0:T(512)S(1)}, f32[320]{0:T(512)}, u32[]{:S(2)}) copy-start(f32[320]{0:T(512)} %param.23) | copy-start | bytes 3844
  7.3 97.6 %all-gather.2.cloned.1.call-start = ((), (), s32[]{:S(2)}) async-start(), calls=%async_computation.10 | async-start | bytes 5570560 | tf_op jit(solution)/shard_map/all_gather | solution.py:322
  9.3 13.8 %collective-permute-start = (bf16[1024,256]{1,0:T(8,128)(2,1)S(1)}, bf16[1024,256]{1,0:T(8,128)(2,1)S(1)}, u32[]{:S(2)}, u32[]{:S(2)}) collective-permute-start(bf16[1024,256]{1,0:T(8,128)(2,1)S(1)} %constant_dynamic-update-slice_fusion), channel_id=1, source_target_pairs={{0,4},{4,0},{8,12},{12,8},{16,20},{20,16},{24,28},{28,24},{32,36},... | collective-permute-start | bytes 1572872 | tf_op jit(solution)/shard_map/ppermute | solution.py:291
  23.6 26.7 %collective-permute-start.1 = (bf16[16,128]{1,0:T(8,128)(2,1)S(1)}, bf16[16,128]{1,0:T(8,128)(2,1)S(1)}, u32[]{:S(2)}, u32[]{:S(2)}) collective-permute-start(bf16[16,128]{1,0:T(8,128)(2,1)S(1)} %fusion.3), channel_id=1, source_target_pairs={{0,4},{4,0},{8,12},{12,8},{16,20},{20,16},{24,28},{28,24},{32,36},... | collective-permute-start | bytes 12296 | tf_op jit(solution)/shard_map/ppermute | solution.py:291
  26.3 19.0 %all-to-all-start.2 = ((f32[16,1,80]{2,1,0:T(1,128)}), f32[16,1,80]{2,1,0:T(1,128)S(1)}, u32[]{:S(2)}, u32[]{:S(2)}) async-start(f32[16,1,80]{2,1,0:T(1,128)} %broadcast_in_dim.20), calls=%async_computation.2 | async-start | bytes 16384 | tf_op jit(solution)/shard_map/all_to_all | solution.py:32
  46.5 19.2 %all-to-all-start.3 = ((bf16[16,80,320]{2,1,0:T(8,128)(2,1)}), bf16[16,80,320]{2,1,0:T(8,128)(2,1)S(1)}, u32[]{:S(2)}, u32[]{:S(2)}) async-start(bf16[16,80,320]{2,1,0:T(8,128)(2,1)} %broadcast_in_dim.22), calls=%async_computation.3 | async-start | bytes 1966080 | tf_op jit(solution)/shard_map/all_to_all | solution.py:32
  73.8 17.2 %all-to-all-start.1 = ((bf16[2,2080,128]{2,1,0:T(8,128)(2,1)}), bf16[2,2080,128]{2,1,0:T(8,128)(2,1)S(1)}, u32[]{:S(2)}, u32[]{:S(2)}) async-start(bf16[2,2080,128]{2,1,0:T(8,128)(2,1)} %pad_maximum_fusion), calls=%async_computation.1 | async-start | bytes 2129920 | tf_op jit(solution)/shard_map/all_to_all | solution.py:38
  91.0 1.0 copy-start.1
  108.8 19.9 %all-to-all-start.5 = ((bf16[16,64,128]{2,1,0:T(8,128)(2,1)}), bf16[16,64,128]{2,1,0:T(8,128)(2,1)S(1)}, u32[]{:S(2)}, u32[]{:S(2)}) async-start(bf16[16,64,128]{2,1,0:T(8,128)(2,1)} %shard_map.168), calls=%async_computation.5 | async-start | bytes 524288 | tf_op jit(solution)/shard_map/all_to_all | solution.py:38
  119.9 6.3 %collective-permute-start.2 = (bf16[320,128]{1,0:T(8,128)(2,1)}, bf16[320,128]{1,0:T(8,128)(2,1)S(1)}, u32[]{:S(2)}, u32[]{:S(2)}) collective-permute-start(bf16[320,128]{1,0:T(8,128)(2,1)} %shard_map.169.own_new), channel_id=1, source_target_pairs={{0,4},{4,0},{8,12},{12,8},{16,20},{20,16},{24,28},{28,24},{32,36},... | collective-permute-start | bytes 245768 | tf_op jit(solution)/shard_map/ppermute | solution.py:291
  126.2 2.4 %copy-start.12 = (bf16[320,128]{1,0:T(8,128)(2,1)}, bf16[320,128]{1,0:T(8,128)(2,1)S(1)}, u32[]{:S(2)}) copy-start(bf16[320,128]{1,0:T(8,128)(2,1)S(1)} %collective-permute-done.2.other_new) | copy-start | bytes 245764
  181.1 34.6 %copy-start.8 = (f32[320]{0:T(512)S(1)}, f32[320]{0:T(512)}, u32[]{:S(2)}) copy-start(f32[320]{0:T(512)} %param.25) | copy-start | bytes 3844
  182.0 18.7 %all-to-all-start.8 = ((bf16[16,160,128]{2,1,0:T(8,128)(2,1)}), bf16[16,160,128]{2,1,0:T(8,128)(2,1)S(1)}, u32[]{:S(2)}, u32[]{:S(2)}) async-start(bf16[16,160,128]{2,1,0:T(8,128)(2,1)} %fusion), calls=%async_computation.8 | async-start | bytes 1310720 | tf_op jit(solution)/shard_map/all_to_all | solution.py:38
  189.4 8.2 %collective-permute-start.3 = (bf16[2,16,128]{2,1,0:T(8,128)(2,1)S(1)}, bf16[2,16,128]{2,1,0:T(8,128)(2,1)S(1)}, u32[]{:S(2)}, u32[]{:S(2)}) collective-permute-start(bf16[2,16,128]{2,1,0:T(8,128)(2,1)S(1)} %get-tuple-element.24), channel_id=1, source_target_pairs={{0,64},{64,0},{1,65},{65,1},{2,66},{66,2},{3,67},{67,3},{4,68},{68... | collective-permute-start | bytes 24584 | tf_op jit(solution)/shard_map/ppermute | solution.py:374
  200.8 0.9 copy-start.2
  203.5 12.2 %all-to-all-start.9 = ((f32[16,1,64]{2,1,0:T(1,128)}), f32[16,1,64]{2,1,0:T(1,128)S(1)}, u32[]{:S(2)}, u32[]{:S(2)}) async-start(f32[16,1,64]{2,1,0:T(1,128)} %get-tuple-element.16), calls=%async_computation.9 | async-start | bytes 16384 | tf_op jit(solution)/shard_map/all_to_all | solution.py:38
  (1 other events, 0.7 us)
Sparse Core Ops, SparseCore 0:
  23.3 81.5 all-gather.1

commit v10 on v9

--- a/solution.py
+++ b/solution.py
@@ -42,6 +42,27 @@
     return jnp.stack([matrix[:, :HD], matrix[:, HD:]])
 
 
+def prepare_kernel(keys_ref, values_ref, k_ref, v_ref, q_ref, out_ref, tokens_ref, shard_ref):
+    tokens_ref[0:512, :] = keys_ref[...]
+    tokens_ref[512:1024, :] = values_ref[...]
+    for head in range(2):
+        at = slice(HD * head, HD * (head + 1))
+        for i, ref in enumerate((k_ref, v_ref, q_ref, out_ref)):
+            shard_ref[head, :, HD * i : HD * (i + 1)] = ref[:, at]
+
+
+def prepare(*arrays):
+    return pl.pallas_call(
+        prepare_kernel,
+        out_shape=(
+            jax.ShapeDtypeStruct((1024, 2 * HD), BF16),
+            jax.ShapeDtypeStruct((2, 160, 4 * HD), BF16),
+        ),
+        compiler_params=pltpu.CompilerParams(vmem_limit_bytes=VMEM_LIMIT),
+        cost_estimate=pl.CostEstimate(flops=0, bytes_accessed=2 * 2**20, transcendentals=0),
+    )(*arrays)
+
+
 def lay_out_kernel(h_ref, out_ref):
     for j in range(16):
         for xl in range(2):
@@ -61,7 +82,7 @@
 def project_kernel(h_ref, w_ref, out_ref, acc):
     step = pl.program_id(0)
     width = acc.shape[1]
-    weights = w_ref[...].reshape(D // 4, width)
+    weights = w_ref[...].reshape(D // 2, width)
     part = jnp.dot(h_ref[...], weights, preferred_element_type=F32)
 
     @pl.when(step == 0)
@@ -88,10 +109,10 @@
 def project(features, weights, block, width, shape):
     return pl.pallas_call(
         project_kernel,
-        grid=(4,),
+        grid=(2,),
         in_specs=[
-            pl.BlockSpec((160, D // 4), lambda s: (0, s)),
-            pl.BlockSpec((8, 160, width), lambda s: (s % 2, s // 2, block)),
+            pl.BlockSpec((160, D // 2), lambda s: (0, s)),
+            pl.BlockSpec((16, 160, width), lambda s: (0, s, block)),
         ],
         out_specs=pl.BlockSpec(shape, lambda s: (0,) * len(shape)),
         out_shape=jax.ShapeDtypeStruct(shape, BF16),
@@ -311,13 +332,10 @@
     flight, ch_dev, width = state.shape
     rows_count = flight * ch_dev
 
-    tokens = jnp.concatenate([cache_keys, cache_values], axis=0)
+    side = lax.axis_index("xl")
+    tokens, shard = prepare(cache_keys, cache_values, w_key, w_value, w_query, w_out.T)
     near = from_neighbour(tokens)
-
-    side = lax.axis_index("xl")
-    parts = [by_head(w) for w in (w_key, w_value, w_query)]
-    parts.append(jnp.transpose(w_out.reshape(2, HD, 160), (0, 2, 1)))
-    shard = swapped(jnp.concatenate(parts, axis=2), "xl")
+    shard = swapped(shard, "xl")
     shard, near = lax.optimization_barrier((shard, near))
     w_full = lax.all_gather(shard.reshape(320, 4 * HD), "z", axis=0, tiled=False)
 

time: 226 us -> 222 us (0.982)
  local copies, waits for them, and re-layouts: 9.25 us -> 5.58 us
    pallas_call x2 -> x3, Pallas kernels: 8.06 us -> 8.45 us  [the longest x2 6.27 us: project(): pl.pallas_call(project_kernel, grid=(2,), in_specs=[pl.BlockSpec((160, D...]
where the time goes in v10:
time: 222 us; the launch traced here: 220 us
  waiting for transfers between devices  60.3 us (27%)
  blocking collectives  53.8 us (24%)
  starting transfers between devices  51 us (23%)
  Pallas kernels  27.9 us (13%)
  between operations  14.3 us (6%)
  other arithmetic  7.22 us (3%)
  local copies, waits for them, and re-layouts  5.58 us (3%)
    all_to_all x3, blocking collectives, swapped(): return lax.all_to_all(blocks, axis, 0, 0, tiled=True)  45.9 us
    all_to_all x4, waiting for transfers between devices, swapped(): return lax.all_to_all(blocks, axis, 0, 0, tiled=True)  23.3 us
    all_to_all x4, starting transfers between devices, swapped(): return lax.all_to_all(blocks, axis, 0, 0, tiled=True)  21.7 us
    all_to_all x2, waiting for transfers between devices, sent_to_all(): lax.all_to_all(jnp.broadcast_to(array[None], (devices, *array.shape)), ax...  20.9 us
    all_to_all x2, starting transfers between devices, sent_to_all(): lax.all_to_all(jnp.broadcast_to(array[None], (devices, *array.shape)), ax...  15.9 us
    ppermute x3, starting transfers between devices, from_neighbour(): return lax.ppermute(array, 'z', [(z, z ^ 1) for z in range(16)])  10.1 us
    pallas_call x1, Pallas kernels, attend(): pl.pallas_call(attend_kernel, grid=(rows // step,), in_specs=[pl.BlockSpe...  8.65 us
    all_gather x1, waiting for transfers between devices, local(): lax.all_gather(shard.reshape(320, 4 * HD), 'z', axis=0, tiled=False)  8.49 us
  transfers between devices with their start and end apart: 11, of which 9 were waited for; matrix products, arithmetic and copies ran while one was open for 3% of the time, Pallas kernels for 4%

profile of v10, /device:TPU:1, one launch (start us, length us, event | category | flops | bytes accessed | tf_op | source)
XLA Modules:
  0.0 220.1 jit_solution(17153504262958402225)
XLA Ops:
  9.4 4.4 %collective-permute-start = (bf16[1024,256]{1,0:T(8,128)(2,1)}, bf16[1024,256]{1,0:T(8,128)(2,1)S(1)}, u32[]{:S(2)}, u32[]{:S(2)}) collective-permute-start(bf16[1024,256]{1,0:T(8,128)(2,1)} %get-tuple-element.13), channel_id=1, source_target_pairs={{0,4},{4,0},{8,12},{12,8},{16,20},{20,16},{24,28},{28,24},{32,36},... | collective-permute-start | bytes 1572872 | tf_op jit(solution)/shard_map/ppermute | solution.py:312
  13.8 8.8 %all_to_all.51 = bf16[2,160,512]{2,1,0:T(8,128)(2,1)} all-to-all(bf16[2,160,512]{2,1,0:T(8,128)(2,1)} %get-tuple-element.12), channel_id=1, replica_groups=mesh['y'=4,'xl'=2,'z'=16,'xh'=2,'core'=2] {'xl'}, dimensions={0} | all-to-all | bytes 655360 | tf_op jit(solution)/shard_map/all_to_all | solution.py:38
  28.5 12.3 %all-to-all-start.2 = ((f32[16,1,80]{2,1,0:T(1,128)}), f32[16,1,80]{2,1,0:T(1,128)S(1)}, u32[]{:S(2)}, u32[]{:S(2)}) async-start(f32[16,1,80]{2,1,0:T(1,128)} %broadcast_in_dim.20), calls=%async_computation.2 | async-start | bytes 16384 | tf_op jit(solution)/shard_map/all_to_all | solution.py:32
  41.2 6.5 %all-to-all-done.2 = f32[16,1,80]{2,1,0:T(1,128)S(1)} async-done(((f32[16,1,80]{2,1,0:T(1,128)}), f32[16,1,80]{2,1,0:T(1,128)S(1)}, u32[]{:S(2)}, u32[]{:S(2)}) %all-to-all-start.2) | async-done | bytes 5152 | tf_op jit(solution)/shard_map/all_to_all | solution.py:32
  48.9 3.6 %all-to-all-start.3 = ((bf16[16,80,320]{2,1,0:T(8,128)(2,1)}), bf16[16,80,320]{2,1,0:T(8,128)(2,1)S(1)}, u32[]{:S(2)}, u32[]{:S(2)}) async-start(bf16[16,80,320]{2,1,0:T(8,128)(2,1)} %broadcast_in_dim.22), calls=%async_computation.3 | async-start | bytes 1966080 | tf_op jit(solution)/shard_map/all_to_all | solution.py:32
  53.7 14.4 %all-to-all-done.3 = bf16[16,80,320]{2,1,0:T(8,128)(2,1)S(1)} async-done(((bf16[16,80,320]{2,1,0:T(8,128)(2,1)}), bf16[16,80,320]{2,1,0:T(8,128)(2,1)S(1)}, u32[]{:S(2)}, u32[]{:S(2)}) %all-to-all-start.3) | async-done | bytes 819232 | tf_op jit(solution)/shard_map/all_to_all | solution.py:32
  68.3 7.9 %all_to_all.52 = bf16[2,16,80,320]{3,2,1,0:T(8,128)(2,1)} all-to-all(bf16[2,16,80,320]{3,2,1,0:T(8,128)(2,1)S(1)} %broadcast_in_dim.23), channel_id=1, replica_groups=mesh['y'=4,'xl'=2,'z'=16,'xh'=2,'core'=2] {'core'}, dimensions={0} | all-to-all | bytes 3276800 | tf_op jit(solution)/shard_map/all_to_all | solution.py:32
  76.2 3.6 %all-to-all-start.1 = ((bf16[2,2080,128]{2,1,0:T(8,128)(2,1)}), bf16[2,2080,128]{2,1,0:T(8,128)(2,1)S(1)}, u32[]{:S(2)}, u32[]{:S(2)}) async-start(bf16[2,2080,128]{2,1,0:T(8,128)(2,1)} %pad_maximum_fusion), calls=%async_computation.1 | async-start | bytes 2129920 | tf_op jit(solution)/shard_map/all_to_all | solution.py:38
  79.8 3.3 %shard_map.168.h_ref = bf16[160,5120]{1,0:T(8,128)(2,1)} custom-call(bf16[2,4,2,2,80,320]{5,4,3,2,1,0:T(8,128)(2,1)} %bitcast.42), custom_call_target="tpu_custom_call" | custom-call | bytes 4194304 | tf_op jit(solution)/shard_map/pallas_call | solution.py:74
  83.0 10.3 %all-to-all-done.1 = bf16[2,2080,128]{2,1,0:T(8,128)(2,1)S(1)} async-done(((bf16[2,2080,128]{2,1,0:T(8,128)(2,1)}), bf16[2,2080,128]{2,1,0:T(8,128)(2,1)S(1)}, u32[]{:S(2)}, u32[]{:S(2)}) %all-to-all-start.1) | async-done | bytes 1064992 | tf_op jit(solution)/shard_map/all_to_all | solution.py:38
  96.6 8.5 %all-gather.2.cloned.1.call-done.w_ref = bf16[16,320,512]{2,1,0:T(8,128)(2,1)} async-done(((bf16[1,320,512]{2,1,0:T(8,128)(2,1)}), bf16[16,320,512]{2,1,0:T(8,128)(2,1)}) %all-gather.2.cloned.1.call-update) | async-done | bytes 5242896 | tf_op jit(solution)/shard_map/all_gather | solution.py:340
  108.1 6.9 %all-to-all-start.5 = ((bf16[16,64,128]{2,1,0:T(8,128)(2,1)}), bf16[16,64,128]{2,1,0:T(8,128)(2,1)S(1)}, u32[]{:S(2)}, u32[]{:S(2)}) async-start(bf16[16,64,128]{2,1,0:T(8,128)(2,1)} %shard_map.169), calls=%async_computation.5 | async-start | bytes 524288 | tf_op jit(solution)/shard_map/all_to_all | solution.py:38
  115.0 3.3 %shard_map.170.own_new = bf16[320,128]{1,0:T(8,128)(2,1)} custom-call(bf16[160,5120]{1,0:T(8,128)(2,1)} %shard_map.168.h_ref, bf16[16,320,512]{2,1,0:T(8,128)(2,1)} %all-gather.2.cloned.1.call-done.w_ref), custom_call_target="tpu_custom_call" | custom-call | flops 419430400 | bytes 4194304 | tf_op jit(solution)/shard_map/pallas_call | solution.py:110
  118.3 3.3 %collective-permute-start.2 = (bf16[320,128]{1,0:T(8,128)(2,1)}, bf16[320,128]{1,0:T(8,128)(2,1)S(1)}, u32[]{:S(2)}, u32[]{:S(2)}) collective-permute-start(bf16[320,128]{1,0:T(8,128)(2,1)} %shard_map.170.own_new), channel_id=1, source_target_pairs={{0,4},{4,0},{8,12},{12,8},{16,20},{20,16},{24,28},{28,24},{32,36},... | collective-permute-start | bytes 245768 | tf_op jit(solution)/shard_map/ppermute | solution.py:312
  124.4 3.4 %all-to-all-done.5 = bf16[16,64,128]{2,1,0:T(8,128)(2,1)S(1)} async-done(((bf16[16,64,128]{2,1,0:T(8,128)(2,1)}), bf16[16,64,128]{2,1,0:T(8,128)(2,1)S(1)}, u32[]{:S(2)}, u32[]{:S(2)}) %all-to-all-start.5) | async-done | bytes 262176 | tf_op jit(solution)/shard_map/all_to_all | solution.py:38
  128.5 8.7 %shard_map.171 = bf16[16,80,128]{2,1,0:T(8,128)(2,1)} custom-call(bf16[1024,128]{1,0:T(8,128)(2,1)} %bitcast.48, bf16[2,2,1040,128]{3,2,1,0:T(8,128)(2,1)} %bitcast.44, bf16[2,2,144,512]{3,2,1,0:T(8,128)(2,1)} %shard_map.167.vt_ref, bf16[320,128]{1,0:T(8,128)(2,1)} %shard_map.170.own_new, bf16[320,128]{1,0:T(8,128)(2,1)} %copy-done.10), custom_call_target="tpu_custom_call" | custom-call | flops 1241513984 | bytes 3145728 | tf_op jit(solution)/shard_map/pallas_call | solution.py:215
  137.1 21.3 %all_to_all.53.in_ref = bf16[16,80,128]{2,1,0:T(8,128)(2,1)} all-to-all(bf16[16,80,128]{2,1,0:T(8,128)(2,1)} %shard_map.171), channel_id=1, replica_groups=mesh['y'=4,'xl'=2,'z'=16,'xh'=2,'core'=2] {'z'}, dimensions={0} | all-to-all | bytes 655360 | tf_op jit(solution)/shard_map/all_to_all | solution.py:38
  158.4 3.3 %shard_map.172 = bf16[2,16,160,128]{3,2,1,0:T(8,128)(2,1)} custom-call(bf16[16,80,128]{2,1,0:T(8,128)(2,1)} %all_to_all.53.in_ref, bf16[16,320,512]{2,1,0:T(8,128)(2,1)} %all-gather.2.cloned.1.call-done.w_ref), custom_call_target="tpu_custom_call" | custom-call | tf_op jit(solution)/shard_map/pallas_call | solution.py:274
  161.7 15.9 %all_to_all.54 = bf16[2,16,160,128]{3,2,1,0:T(8,128)(2,1)S(1)} all-to-all(bf16[2,16,160,128]{3,2,1,0:T(8,128)(2,1)} %shard_map.172), channel_id=1, replica_groups=mesh['y'=4,'xl'=2,'z'=16,'xh'=2,'core'=2] {'core'}, dimensions={0} | all-to-all | bytes 2621440 | tf_op jit(solution)/shard_map/all_to_all | solution.py:38
  178.5 6.1 %all-to-all-start.8 = ((bf16[16,160,128]{2,1,0:T(8,128)(2,1)}), bf16[16,160,128]{2,1,0:T(8,128)(2,1)S(1)}, u32[]{:S(2)}, u32[]{:S(2)}) async-start(bf16[16,160,128]{2,1,0:T(8,128)(2,1)} %fusion), calls=%async_computation.8 | async-start | bytes 1310720 | tf_op jit(solution)/shard_map/all_to_all | solution.py:38
  185.3 3.2 %collective-permute-start.3 = (bf16[2,16,128]{2,1,0:T(8,128)(2,1)S(1)}, bf16[2,16,128]{2,1,0:T(8,128)(2,1)S(1)}, u32[]{:S(2)}, u32[]{:S(2)}) collective-permute-start(bf16[2,16,128]{2,1,0:T(8,128)(2,1)S(1)} %get-tuple-element.28), channel_id=1, source_target_pairs={{0,64},{64,0},{1,65},{65,1},{2,66},{66,2},{3,67},{67,3},{4,68},{68... | collective-permute-start | bytes 24584 | tf_op jit(solution)/shard_map/ppermute | solution.py:392
  188.7 4.8 %collective-permute-done.3 = bf16[2,16,128]{2,1,0:T(8,128)(2,1)S(1)} collective-permute-done((bf16[2,16,128]{2,1,0:T(8,128)(2,1)S(1)}, bf16[2,16,128]{2,1,0:T(8,128)(2,1)S(1)}, u32[]{:S(2)}, u32[]{:S(2)}) %collective-permute-start.3) | collective-permute-done | bytes 8224 | tf_op jit(solution)/shard_map/ppermute | solution.py:392
  199.4 5.1 %all-to-all-start.9 = ((f32[16,1,64]{2,1,0:T(1,128)}), f32[16,1,64]{2,1,0:T(1,128)S(1)}, u32[]{:S(2)}, u32[]{:S(2)}) async-start(f32[16,1,64]{2,1,0:T(1,128)} %get-tuple-element.20), calls=%async_computation.9 | async-start | bytes 16384 | tf_op jit(solution)/shard_map/all_to_all | solution.py:38
  205.1 6.4 %all-to-all-done.9 = f32[16,1,64]{2,1,0:T(1,128)S(1)} async-done(((f32[16,1,64]{2,1,0:T(1,128)}), f32[16,1,64]{2,1,0:T(1,128)S(1)}, u32[]{:S(2)}, u32[]{:S(2)}) %all-to-all-start.9) | async-done | bytes 4128 | tf_op jit(solution)/shard_map/all_to_all | solution.py:38
  (67 shorter events, 30.6 us)
Async XLA Ops:
  7.2 20.6 %copy-start.2 = (f32[4,16,320]{2,1,0:T(8,128)S(1)}, f32[4,16,320]{2,1,0:T(8,128)}, u32[]{:S(2)}) copy-start(f32[4,16,320]{2,1,0:T(8,128)} %param.15) | copy-start | bytes 245764
  7.2 33.6 %copy-start.9 = (s32[4]{0:T(128)S(1)}, s32[4]{0:T(128)}, u32[]{:S(2)}) copy-start(s32[4]{0:T(128)} %param.27) | copy-start | bytes 52
  7.2 33.6 %copy-start.8 = (f32[50]{0:T(128)S(1)}, f32[50]{0:T(128)}, u32[]{:S(2)}) copy-start(f32[50]{0:T(128)} %param.26) | copy-start | bytes 604
  7.2 40.5 %copy-start.6 = (f32[320]{0:T(512)S(1)}, f32[320]{0:T(512)}, u32[]{:S(2)}) copy-start(f32[320]{0:T(512)} %param.23) | copy-start | bytes 3844
  7.2 40.5 %copy-start.5 = (f32[320]{0:T(512)S(1)}, f32[320]{0:T(512)}, u32[]{:S(2)}) copy-start(f32[320]{0:T(512)} %param.24) | copy-start | bytes 3844
  7.2 97.9 %all-gather.2.cloned.1.call-start = ((), (), s32[]{:S(2)}) async-start(), calls=%async_computation.10 | async-start | bytes 5570560 | tf_op jit(solution)/shard_map/all_gather | solution.py:340
  9.4 13.2 %collective-permute-start = (bf16[1024,256]{1,0:T(8,128)(2,1)}, bf16[1024,256]{1,0:T(8,128)(2,1)S(1)}, u32[]{:S(2)}, u32[]{:S(2)}) collective-permute-start(bf16[1024,256]{1,0:T(8,128)(2,1)} %get-tuple-element.13), channel_id=1, source_target_pairs={{0,4},{4,0},{8,12},{12,8},{16,20},{20,16},{24,28},{28,24},{32,36},... | collective-permute-start | bytes 1572872 | tf_op jit(solution)/shard_map/ppermute | solution.py:312
  22.6 29.9 %copy-start.3 = (bf16[1024,256]{1,0:T(8,128)(2,1)S(1)}, bf16[1024,256]{1,0:T(8,128)(2,1)}, u32[]{:S(2)}) copy-start(bf16[1024,256]{1,0:T(8,128)(2,1)} %get-tuple-element.13) | copy-start | bytes 1572868
  24.5 28.1 %collective-permute-start.1 = (bf16[16,128]{1,0:T(8,128)(2,1)S(1)}, bf16[16,128]{1,0:T(8,128)(2,1)S(1)}, u32[]{:S(2)}, u32[]{:S(2)}) collective-permute-start(bf16[16,128]{1,0:T(8,128)(2,1)S(1)} %fusion.3), channel_id=1, source_target_pairs={{0,4},{4,0},{8,12},{12,8},{16,20},{20,16},{24,28},{28,24},{32,36},... | collective-permute-start | bytes 12296 | tf_op jit(solution)/shard_map/ppermute | solution.py:312
  28.5 19.2 %all-to-all-start.2 = ((f32[16,1,80]{2,1,0:T(1,128)}), f32[16,1,80]{2,1,0:T(1,128)S(1)}, u32[]{:S(2)}, u32[]{:S(2)}) async-start(f32[16,1,80]{2,1,0:T(1,128)} %broadcast_in_dim.20), calls=%async_computation.2 | async-start | bytes 16384 | tf_op jit(solution)/shard_map/all_to_all | solution.py:32
  48.9 19.2 %all-to-all-start.3 = ((bf16[16,80,320]{2,1,0:T(8,128)(2,1)}), bf16[16,80,320]{2,1,0:T(8,128)(2,1)S(1)}, u32[]{:S(2)}, u32[]{:S(2)}) async-start(bf16[16,80,320]{2,1,0:T(8,128)(2,1)} %broadcast_in_dim.22), calls=%async_computation.3 | async-start | bytes 1966080 | tf_op jit(solution)/shard_map/all_to_all | solution.py:32
  76.2 17.2 %all-to-all-start.1 = ((bf16[2,2080,128]{2,1,0:T(8,128)(2,1)}), bf16[2,2080,128]{2,1,0:T(8,128)(2,1)S(1)}, u32[]{:S(2)}, u32[]{:S(2)}) async-start(bf16[2,2080,128]{2,1,0:T(8,128)(2,1)} %pad_maximum_fusion), calls=%async_computation.1 | async-start | bytes 2129920 | tf_op jit(solution)/shard_map/all_to_all | solution.py:38
  93.4 1.0 copy-start
  108.1 19.7 %all-to-all-start.5 = ((bf16[16,64,128]{2,1,0:T(8,128)(2,1)}), bf16[16,64,128]{2,1,0:T(8,128)(2,1)S(1)}, u32[]{:S(2)}, u32[]{:S(2)}) async-start(bf16[16,64,128]{2,1,0:T(8,128)(2,1)} %shard_map.169), calls=%async_computation.5 | async-start | bytes 524288 | tf_op jit(solution)/shard_map/all_to_all | solution.py:38
  118.3 6.0 %collective-permute-start.2 = (bf16[320,128]{1,0:T(8,128)(2,1)}, bf16[320,128]{1,0:T(8,128)(2,1)S(1)}, u32[]{:S(2)}, u32[]{:S(2)}) collective-permute-start(bf16[320,128]{1,0:T(8,128)(2,1)} %shard_map.170.own_new), channel_id=1, source_target_pairs={{0,4},{4,0},{8,12},{12,8},{16,20},{20,16},{24,28},{28,24},{32,36},... | collective-permute-start | bytes 245768 | tf_op jit(solution)/shard_map/ppermute | solution.py:312
  124.4 3.4 %copy-start.10 = (bf16[320,128]{1,0:T(8,128)(2,1)}, bf16[320,128]{1,0:T(8,128)(2,1)S(1)}, u32[]{:S(2)}) copy-start(bf16[320,128]{1,0:T(8,128)(2,1)S(1)} %collective-permute-done.2.other_new) | copy-start | bytes 245764
  127.8 0.7 copy-start.4
  177.5 34.0 %copy-start.7 = (f32[320]{0:T(512)S(1)}, f32[320]{0:T(512)}, u32[]{:S(2)}) copy-start(f32[320]{0:T(512)} %param.25) | copy-start | bytes 3844
  178.5 18.2 %all-to-all-start.8 = ((bf16[16,160,128]{2,1,0:T(8,128)(2,1)}), bf16[16,160,128]{2,1,0:T(8,128)(2,1)S(1)}, u32[]{:S(2)}, u32[]{:S(2)}) async-start(bf16[16,160,128]{2,1,0:T(8,128)(2,1)} %fusion), calls=%async_computation.8 | async-start | bytes 1310720 | tf_op jit(solution)/shard_map/all_to_all | solution.py:38
  185.3 8.2 %collective-permute-start.3 = (bf16[2,16,128]{2,1,0:T(8,128)(2,1)S(1)}, bf16[2,16,128]{2,1,0:T(8,128)(2,1)S(1)}, u32[]{:S(2)}, u32[]{:S(2)}) collective-permute-start(bf16[2,16,128]{2,1,0:T(8,128)(2,1)S(1)} %get-tuple-element.28), channel_id=1, source_target_pairs={{0,64},{64,0},{1,65},{65,1},{2,66},{66,2},{3,67},{67,3},{4,68},{68... | collective-permute-start | bytes 24584 | tf_op jit(solution)/shard_map/ppermute | solution.py:392
  196.6 0.9 copy-start.1
  199.4 12.2 %all-to-all-start.9 = ((f32[16,1,64]{2,1,0:T(1,128)}), f32[16,1,64]{2,1,0:T(1,128)S(1)}, u32[]{:S(2)}, u32[]{:S(2)}) async-start(f32[16,1,64]{2,1,0:T(1,128)} %get-tuple-element.20), calls=%async_computation.9 | async-start | bytes 16384 | tf_op jit(solution)/shard_map/all_to_all | solution.py:38
Sparse Core Ops, SparseCore 0:
  22.8 82.3 all-gather.1

commit v11 on v10

--- a/solution.py
+++ b/solution.py
@@ -205,7 +205,7 @@
 
 
 def attend(queries, kv, values_t, fresh):
-    step = 256
+    step = 512
     rows = queries.shape[0]
     arrays = (kv, values_t, *fresh)
 

time: 222 us -> 219 us (0.986)
  Pallas kernels: 27.9 us -> 25.6 us
  transfers between devices with their start and end apart: 11 -> 11, of which waited for: 9 -> 9; matrix products, arithmetic and copies ran while one was open for 3% -> 4% of each run, Pallas kernels for 4% -> 4%
where the time goes in v11:
time: 219 us; the launch traced here: 218 us
  waiting for transfers between devices  60.3 us (28%)
  blocking collectives  53.8 us (25%)
  starting transfers between devices  51 us (23%)
  Pallas kernels  25.6 us (12%)
  between operations  14.3 us (7%)
  other arithmetic  7.22 us (3%)
  local copies, waits for them, and re-layouts  5.58 us (3%)
    all_to_all x3, blocking collectives, swapped(): return lax.all_to_all(blocks, axis, 0, 0, tiled=True)  45.9 us
    all_to_all x4, waiting for transfers between devices, swapped(): return lax.all_to_all(blocks, axis, 0, 0, tiled=True)  23.3 us
    all_to_all x4, starting transfers between devices, swapped(): return lax.all_to_all(blocks, axis, 0, 0, tiled=True)  21.7 us
    all_to_all x2, waiting for transfers between devices, sent_to_all(): lax.all_to_all(jnp.broadcast_to(array[None], (devices, *array.shape)), ax...  20.9 us
    all_to_all x2, starting transfers between devices, sent_to_all(): lax.all_to_all(jnp.broadcast_to(array[None], (devices, *array.shape)), ax...  15.9 us
    ppermute x3, starting transfers between devices, from_neighbour(): return lax.ppermute(array, 'z', [(z, z ^ 1) for z in range(16)])  10.1 us
    all_gather x1, waiting for transfers between devices, local(): lax.all_gather(shard.reshape(320, 4 * HD), 'z', axis=0, tiled=False)  8.49 us
    all_to_all x1, blocking collectives, sent_to_all(): lax.all_to_all(jnp.broadcast_to(array[None], (devices, *array.shape)), ax...  7.89 us
  transfers between devices with their start and end apart: 11, of which 9 were waited for; matrix products, arithmetic and copies ran while one was open for 4% of the time, Pallas kernels for 4%

profile of v11, /device:TPU:1, one launch (start us, length us, event | category | flops | bytes accessed | tf_op | source)
XLA Modules:
  0.0 217.8 jit_solution(2028853225093310156)
XLA Ops:
  9.4 4.4 %collective-permute-start = (bf16[1024,256]{1,0:T(8,128)(2,1)}, bf16[1024,256]{1,0:T(8,128)(2,1)S(1)}, u32[]{:S(2)}, u32[]{:S(2)}) collective-permute-start(bf16[1024,256]{1,0:T(8,128)(2,1)} %get-tuple-element.13), channel_id=1, source_target_pairs={{0,4},{4,0},{8,12},{12,8},{16,20},{20,16},{24,28},{28,24},{32,36},... | collective-permute-start | bytes 1572872 | tf_op jit(solution)/shard_map/ppermute | solution.py:312
  13.8 8.8 %all_to_all.51 = bf16[2,160,512]{2,1,0:T(8,128)(2,1)} all-to-all(bf16[2,160,512]{2,1,0:T(8,128)(2,1)} %get-tuple-element.12), channel_id=1, replica_groups=mesh['y'=4,'xl'=2,'z'=16,'xh'=2,'core'=2] {'xl'}, dimensions={0} | all-to-all | bytes 655360 | tf_op jit(solution)/shard_map/all_to_all | solution.py:38
  28.5 12.3 %all-to-all-start.2 = ((f32[16,1,80]{2,1,0:T(1,128)}), f32[16,1,80]{2,1,0:T(1,128)S(1)}, u32[]{:S(2)}, u32[]{:S(2)}) async-start(f32[16,1,80]{2,1,0:T(1,128)} %broadcast_in_dim.20), calls=%async_computation.2 | async-start | bytes 16384 | tf_op jit(solution)/shard_map/all_to_all | solution.py:32
  41.2 6.5 %all-to-all-done.2 = f32[16,1,80]{2,1,0:T(1,128)S(1)} async-done(((f32[16,1,80]{2,1,0:T(1,128)}), f32[16,1,80]{2,1,0:T(1,128)S(1)}, u32[]{:S(2)}, u32[]{:S(2)}) %all-to-all-start.2) | async-done | bytes 5152 | tf_op jit(solution)/shard_map/all_to_all | solution.py:32
  48.9 3.6 %all-to-all-start.3 = ((bf16[16,80,320]{2,1,0:T(8,128)(2,1)}), bf16[16,80,320]{2,1,0:T(8,128)(2,1)S(1)}, u32[]{:S(2)}, u32[]{:S(2)}) async-start(bf16[16,80,320]{2,1,0:T(8,128)(2,1)} %broadcast_in_dim.22), calls=%async_computation.3 | async-start | bytes 1966080 | tf_op jit(solution)/shard_map/all_to_all | solution.py:32
  53.7 14.4 %all-to-all-done.3 = bf16[16,80,320]{2,1,0:T(8,128)(2,1)S(1)} async-done(((bf16[16,80,320]{2,1,0:T(8,128)(2,1)}), bf16[16,80,320]{2,1,0:T(8,128)(2,1)S(1)}, u32[]{:S(2)}, u32[]{:S(2)}) %all-to-all-start.3) | async-done | bytes 819232 | tf_op jit(solution)/shard_map/all_to_all | solution.py:32
  68.3 7.9 %all_to_all.52 = bf16[2,16,80,320]{3,2,1,0:T(8,128)(2,1)} all-to-all(bf16[2,16,80,320]{3,2,1,0:T(8,128)(2,1)S(1)} %broadcast_in_dim.23), channel_id=1, replica_groups=mesh['y'=4,'xl'=2,'z'=16,'xh'=2,'core'=2] {'core'}, dimensions={0} | all-to-all | bytes 3276800 | tf_op jit(solution)/shard_map/all_to_all | solution.py:32
  76.2 3.6 %all-to-all-start.1 = ((bf16[2,2080,128]{2,1,0:T(8,128)(2,1)}), bf16[2,2080,128]{2,1,0:T(8,128)(2,1)S(1)}, u32[]{:S(2)}, u32[]{:S(2)}) async-start(bf16[2,2080,128]{2,1,0:T(8,128)(2,1)} %pad_maximum_fusion), calls=%async_computation.1 | async-start | bytes 2129920 | tf_op jit(solution)/shard_map/all_to_all | solution.py:38
  79.8 3.3 %shard_map.168.h_ref = bf16[160,5120]{1,0:T(8,128)(2,1)} custom-call(bf16[2,4,2,2,80,320]{5,4,3,2,1,0:T(8,128)(2,1)} %bitcast.42), custom_call_target="tpu_custom_call" | custom-call | bytes 4194304 | tf_op jit(solution)/shard_map/pallas_call | solution.py:74
  83.0 10.3 %all-to-all-done.1 = bf16[2,2080,128]{2,1,0:T(8,128)(2,1)S(1)} async-done(((bf16[2,2080,128]{2,1,0:T(8,128)(2,1)}), bf16[2,2080,128]{2,1,0:T(8,128)(2,1)S(1)}, u32[]{:S(2)}, u32[]{:S(2)}) %all-to-all-start.1) | async-done | bytes 1064992 | tf_op jit(solution)/shard_map/all_to_all | solution.py:38
  96.6 8.5 %all-gather.2.cloned.1.call-done.w_ref = bf16[16,320,512]{2,1,0:T(8,128)(2,1)} async-done(((bf16[1,320,512]{2,1,0:T(8,128)(2,1)}), bf16[16,320,512]{2,1,0:T(8,128)(2,1)}) %all-gather.2.cloned.1.call-update) | async-done | bytes 5242896 | tf_op jit(solution)/shard_map/all_gather | solution.py:340
  108.1 6.9 %all-to-all-start.5 = ((bf16[16,64,128]{2,1,0:T(8,128)(2,1)}), bf16[16,64,128]{2,1,0:T(8,128)(2,1)S(1)}, u32[]{:S(2)}, u32[]{:S(2)}) async-start(bf16[16,64,128]{2,1,0:T(8,128)(2,1)} %shard_map.169), calls=%async_computation.5 | async-start | bytes 524288 | tf_op jit(solution)/shard_map/all_to_all | solution.py:38
  115.0 3.3 %shard_map.170.own_new = bf16[320,128]{1,0:T(8,128)(2,1)} custom-call(bf16[160,5120]{1,0:T(8,128)(2,1)} %shard_map.168.h_ref, bf16[16,320,512]{2,1,0:T(8,128)(2,1)} %all-gather.2.cloned.1.call-done.w_ref), custom_call_target="tpu_custom_call" | custom-call | flops 419430400 | bytes 4194304 | tf_op jit(solution)/shard_map/pallas_call | solution.py:110
  118.3 3.3 %collective-permute-start.2 = (bf16[320,128]{1,0:T(8,128)(2,1)}, bf16[320,128]{1,0:T(8,128)(2,1)S(1)}, u32[]{:S(2)}, u32[]{:S(2)}) collective-permute-start(bf16[320,128]{1,0:T(8,128)(2,1)} %shard_map.170.own_new), channel_id=1, source_target_pairs={{0,4},{4,0},{8,12},{12,8},{16,20},{20,16},{24,28},{28,24},{32,36},... | collective-permute-start | bytes 245768 | tf_op jit(solution)/shard_map/ppermute | solution.py:312
  124.4 3.4 %all-to-all-done.5 = bf16[16,64,128]{2,1,0:T(8,128)(2,1)S(1)} async-done(((bf16[16,64,128]{2,1,0:T(8,128)(2,1)}), bf16[16,64,128]{2,1,0:T(8,128)(2,1)S(1)}, u32[]{:S(2)}, u32[]{:S(2)}) %all-to-all-start.5) | async-done | bytes 262176 | tf_op jit(solution)/shard_map/all_to_all | solution.py:38
  128.5 6.4 %shard_map.171 = bf16[16,80,128]{2,1,0:T(8,128)(2,1)} custom-call(bf16[1024,128]{1,0:T(8,128)(2,1)} %bitcast.48, bf16[2,2,1040,128]{3,2,1,0:T(8,128)(2,1)} %bitcast.44, bf16[2,2,144,512]{3,2,1,0:T(8,128)(2,1)} %shard_map.167.vt_ref, bf16[320,128]{1,0:T(8,128)(2,1)} %shard_map.170.own_new, bf16[320,128]{1,0:T(8,128)(2,1)} %copy-done.10), custom_call_target="tpu_custom_call" | custom-call | flops 1241513984 | bytes 3145728 | tf_op jit(solution)/shard_map/pallas_call | solution.py:215
  134.9 21.2 %all_to_all.53.in_ref = bf16[16,80,128]{2,1,0:T(8,128)(2,1)} all-to-all(bf16[16,80,128]{2,1,0:T(8,128)(2,1)} %shard_map.171), channel_id=1, replica_groups=mesh['y'=4,'xl'=2,'z'=16,'xh'=2,'core'=2] {'z'}, dimensions={0} | all-to-all | bytes 655360 | tf_op jit(solution)/shard_map/all_to_all | solution.py:38
  156.1 3.3 %shard_map.172 = bf16[2,16,160,128]{3,2,1,0:T(8,128)(2,1)} custom-call(bf16[16,80,128]{2,1,0:T(8,128)(2,1)} %all_to_all.53.in_ref, bf16[16,320,512]{2,1,0:T(8,128)(2,1)} %all-gather.2.cloned.1.call-done.w_ref), custom_call_target="tpu_custom_call" | custom-call | tf_op jit(solution)/shard_map/pallas_call | solution.py:274
  159.5 15.8 %all_to_all.54 = bf16[2,16,160,128]{3,2,1,0:T(8,128)(2,1)S(1)} all-to-all(bf16[2,16,160,128]{3,2,1,0:T(8,128)(2,1)} %shard_map.172), channel_id=1, replica_groups=mesh['y'=4,'xl'=2,'z'=16,'xh'=2,'core'=2] {'core'}, dimensions={0} | all-to-all | bytes 2621440 | tf_op jit(solution)/shard_map/all_to_all | solution.py:38
  176.2 6.1 %all-to-all-start.8 = ((bf16[16,160,128]{2,1,0:T(8,128)(2,1)}), bf16[16,160,128]{2,1,0:T(8,128)(2,1)S(1)}, u32[]{:S(2)}, u32[]{:S(2)}) async-start(bf16[16,160,128]{2,1,0:T(8,128)(2,1)} %fusion), calls=%async_computation.8 | async-start | bytes 1310720 | tf_op jit(solution)/shard_map/all_to_all | solution.py:38
  183.0 3.2 %collective-permute-start.3 = (bf16[2,16,128]{2,1,0:T(8,128)(2,1)S(1)}, bf16[2,16,128]{2,1,0:T(8,128)(2,1)S(1)}, u32[]{:S(2)}, u32[]{:S(2)}) collective-permute-start(bf16[2,16,128]{2,1,0:T(8,128)(2,1)S(1)} %get-tuple-element.28), channel_id=1, source_target_pairs={{0,64},{64,0},{1,65},{65,1},{2,66},{66,2},{3,67},{67,3},{4,68},{68... | collective-permute-start | bytes 24584 | tf_op jit(solution)/shard_map/ppermute | solution.py:392
  186.5 4.8 %collective-permute-done.3 = bf16[2,16,128]{2,1,0:T(8,128)(2,1)S(1)} collective-permute-done((bf16[2,16,128]{2,1,0:T(8,128)(2,1)S(1)}, bf16[2,16,128]{2,1,0:T(8,128)(2,1)S(1)}, u32[]{:S(2)}, u32[]{:S(2)}) %collective-permute-start.3) | collective-permute-done | bytes 8224 | tf_op jit(solution)/shard_map/ppermute | solution.py:392
  197.2 5.1 %all-to-all-start.9 = ((f32[16,1,64]{2,1,0:T(1,128)}), f32[16,1,64]{2,1,0:T(1,128)S(1)}, u32[]{:S(2)}, u32[]{:S(2)}) async-start(f32[16,1,64]{2,1,0:T(1,128)} %get-tuple-element.20), calls=%async_computation.9 | async-start | bytes 16384 | tf_op jit(solution)/shard_map/all_to_all | solution.py:38
  202.9 6.4 %all-to-all-done.9 = f32[16,1,64]{2,1,0:T(1,128)S(1)} async-done(((f32[16,1,64]{2,1,0:T(1,128)}), f32[16,1,64]{2,1,0:T(1,128)S(1)}, u32[]{:S(2)}, u32[]{:S(2)}) %all-to-all-start.9) | async-done | bytes 4128 | tf_op jit(solution)/shard_map/all_to_all | solution.py:38
  (67 shorter events, 30.6 us)
Async XLA Ops:
  7.2 20.6 %copy-start.2 = (f32[4,16,320]{2,1,0:T(8,128)S(1)}, f32[4,16,320]{2,1,0:T(8,128)}, u32[]{:S(2)}) copy-start(f32[4,16,320]{2,1,0:T(8,128)} %param.15) | copy-start | bytes 245764
  7.2 33.6 %copy-start.9 = (s32[4]{0:T(128)S(1)}, s32[4]{0:T(128)}, u32[]{:S(2)}) copy-start(s32[4]{0:T(128)} %param.27) | copy-start | bytes 52
  7.2 33.6 %copy-start.8 = (f32[50]{0:T(128)S(1)}, f32[50]{0:T(128)}, u32[]{:S(2)}) copy-start(f32[50]{0:T(128)} %param.26) | copy-start | bytes 604
  7.2 40.5 %copy-start.6 = (f32[320]{0:T(512)S(1)}, f32[320]{0:T(512)}, u32[]{:S(2)}) copy-start(f32[320]{0:T(512)} %param.23) | copy-start | bytes 3844
  7.2 40.5 %copy-start.5 = (f32[320]{0:T(512)S(1)}, f32[320]{0:T(512)}, u32[]{:S(2)}) copy-start(f32[320]{0:T(512)} %param.24) | copy-start | bytes 3844
  7.2 97.9 %all-gather.2.cloned.1.call-start = ((), (), s32[]{:S(2)}) async-start(), calls=%async_computation.10 | async-start | bytes 5570560 | tf_op jit(solution)/shard_map/all_gather | solution.py:340
  9.4 13.2 %collective-permute-start = (bf16[1024,256]{1,0:T(8,128)(2,1)}, bf16[1024,256]{1,0:T(8,128)(2,1)S(1)}, u32[]{:S(2)}, u32[]{:S(2)}) collective-permute-start(bf16[1024,256]{1,0:T(8,128)(2,1)} %get-tuple-element.13), channel_id=1, source_target_pairs={{0,4},{4,0},{8,12},{12,8},{16,20},{20,16},{24,28},{28,24},{32,36},... | collective-permute-start | bytes 1572872 | tf_op jit(solution)/shard_map/ppermute | solution.py:312
  22.6 29.9 %copy-start.3 = (bf16[1024,256]{1,0:T(8,128)(2,1)S(1)}, bf16[1024,256]{1,0:T(8,128)(2,1)}, u32[]{:S(2)}) copy-start(bf16[1024,256]{1,0:T(8,128)(2,1)} %get-tuple-element.13) | copy-start | bytes 1572868
  24.5 28.1 %collective-permute-start.1 = (bf16[16,128]{1,0:T(8,128)(2,1)S(1)}, bf16[16,128]{1,0:T(8,128)(2,1)S(1)}, u32[]{:S(2)}, u32[]{:S(2)}) collective-permute-start(bf16[16,128]{1,0:T(8,128)(2,1)S(1)} %fusion.3), channel_id=1, source_target_pairs={{0,4},{4,0},{8,12},{12,8},{16,20},{20,16},{24,28},{28,24},{32,36},... | collective-permute-start | bytes 12296 | tf_op jit(solution)/shard_map/ppermute | solution.py:312
  28.5 19.2 %all-to-all-start.2 = ((f32[16,1,80]{2,1,0:T(1,128)}), f32[16,1,80]{2,1,0:T(1,128)S(1)}, u32[]{:S(2)}, u32[]{:S(2)}) async-start(f32[16,1,80]{2,1,0:T(1,128)} %broadcast_in_dim.20), calls=%async_computation.2 | async-start | bytes 16384 | tf_op jit(solution)/shard_map/all_to_all | solution.py:32
  48.9 19.2 %all-to-all-start.3 = ((bf16[16,80,320]{2,1,0:T(8,128)(2,1)}), bf16[16,80,320]{2,1,0:T(8,128)(2,1)S(1)}, u32[]{:S(2)}, u32[]{:S(2)}) async-start(bf16[16,80,320]{2,1,0:T(8,128)(2,1)} %broadcast_in_dim.22), calls=%async_computation.3 | async-start | bytes 1966080 | tf_op jit(solution)/shard_map/all_to_all | solution.py:32
  76.2 17.2 %all-to-all-start.1 = ((bf16[2,2080,128]{2,1,0:T(8,128)(2,1)}), bf16[2,2080,128]{2,1,0:T(8,128)(2,1)S(1)}, u32[]{:S(2)}, u32[]{:S(2)}) async-start(bf16[2,2080,128]{2,1,0:T(8,128)(2,1)} %pad_maximum_fusion), calls=%async_computation.1 | async-start | bytes 2129920 | tf_op jit(solution)/shard_map/all_to_all | solution.py:38
  93.4 1.0 copy-start
  108.1 19.7 %all-to-all-start.5 = ((bf16[16,64,128]{2,1,0:T(8,128)(2,1)}), bf16[16,64,128]{2,1,0:T(8,128)(2,1)S(1)}, u32[]{:S(2)}, u32[]{:S(2)}) async-start(bf16[16,64,128]{2,1,0:T(8,128)(2,1)} %shard_map.169), calls=%async_computation.5 | async-start | bytes 524288 | tf_op jit(solution)/shard_map/all_to_all | solution.py:38
  118.3 6.0 %collective-permute-start.2 = (bf16[320,128]{1,0:T(8,128)(2,1)}, bf16[320,128]{1,0:T(8,128)(2,1)S(1)}, u32[]{:S(2)}, u32[]{:S(2)}) collective-permute-start(bf16[320,128]{1,0:T(8,128)(2,1)} %shard_map.170.own_new), channel_id=1, source_target_pairs={{0,4},{4,0},{8,12},{12,8},{16,20},{20,16},{24,28},{28,24},{32,36},... | collective-permute-start | bytes 245768 | tf_op jit(solution)/shard_map/ppermute | solution.py:312
  124.4 3.4 %copy-start.10 = (bf16[320,128]{1,0:T(8,128)(2,1)}, bf16[320,128]{1,0:T(8,128)(2,1)S(1)}, u32[]{:S(2)}) copy-start(bf16[320,128]{1,0:T(8,128)(2,1)S(1)} %collective-permute-done.2.other_new) | copy-start | bytes 245764
  127.8 0.7 copy-start.4
  175.3 34.0 %copy-start.7 = (f32[320]{0:T(512)S(1)}, f32[320]{0:T(512)}, u32[]{:S(2)}) copy-start(f32[320]{0:T(512)} %param.25) | copy-start | bytes 3844
  176.2 18.2 %all-to-all-start.8 = ((bf16[16,160,128]{2,1,0:T(8,128)(2,1)}), bf16[16,160,128]{2,1,0:T(8,128)(2,1)S(1)}, u32[]{:S(2)}, u32[]{:S(2)}) async-start(bf16[16,160,128]{2,1,0:T(8,128)(2,1)} %fusion), calls=%async_computation.8 | async-start | bytes 1310720 | tf_op jit(solution)/shard_map/all_to_all | solution.py:38
  183.0 8.2 %collective-permute-start.3 = (bf16[2,16,128]{2,1,0:T(8,128)(2,1)S(1)}, bf16[2,16,128]{2,1,0:T(8,128)(2,1)S(1)}, u32[]{:S(2)}, u32[]{:S(2)}) collective-permute-start(bf16[2,16,128]{2,1,0:T(8,128)(2,1)S(1)} %get-tuple-element.28), channel_id=1, source_target_pairs={{0,64},{64,0},{1,65},{65,1},{2,66},{66,2},{3,67},{67,3},{4,68},{68... | collective-permute-start | bytes 24584 | tf_op jit(solution)/shard_map/ppermute | solution.py:392
  194.4 0.9 copy-start.1
  197.2 12.2 %all-to-all-start.9 = ((f32[16,1,64]{2,1,0:T(1,128)}), f32[16,1,64]{2,1,0:T(1,128)S(1)}, u32[]{:S(2)}, u32[]{:S(2)}) async-start(f32[16,1,64]{2,1,0:T(1,128)} %get-tuple-element.20), calls=%async_computation.9 | async-start | bytes 16384 | tf_op jit(solution)/shard_map/all_to_all | solution.py:38
Sparse Core Ops, SparseCore 0:
  22.8 82.3 all-gather.1
